TPU v7x, 128 devices: a whole 4x4x4 slice. The times are simulated.
128 devices in a mesh: dp: 8 (over z_hi, x), vocab: 16 (over y, z_lo, core).
Axes of the slice: x: 4, y: 4, z: 4 (z_hi: 2, z_lo: 2; z = z_hi * 2 + z_lo), core: 2. Of those that a mesh axis runs over, the one named last changes fastest.
Arguments:
- hidden: bfloat16 [1024, 3584], P('dp'), may hold values from -60 to 60
- head_weight: bfloat16 [3584, 131072], P(None, ('dp', 'vocab')), may hold values from -1 to 1
- teacher_logits: bfloat16 [1024, 131072], P('vocab', 'dp'), may hold values from -30 to 30
Outputs:
- grad_hidden: bfloat16 [1024, 3584], P(('dp', 'vocab'))
- grad_head: bfloat16 [3584, 131072], P(None, ('dp', 'vocab'))
All inputs are finite; a program needn't handle non-finite values.
Results may differ from a plain program's by a relative error of at most 0.015.
Values may be sent and summed in bfloat16 or wider, within the bound.
No kernel may reach another device: no remote copies, remote signals or barrier semaphores. Data moves between devices by JAX's collectives and lax.ppermute only.
A program may use at most 128 MiB of HBM per device.

v0:
```python
import jax
import jax.numpy as jnp
from jax import lax
from jax.sharding import PartitionSpec as P


def per_device(hidden, head_weight, teacher_logits):
    teacher = lax.all_to_all(teacher_logits, "vocab", split_axis=1, concat_axis=0, tiled=True)
    gathered = lax.all_gather(hidden, "dp", axis=0, tiled=True)
    raw = jnp.dot(gathered, head_weight, preferred_element_type=jnp.float32)
    capped = jnp.tanh(raw / 30.0)
    student_exp = jnp.exp(15.0 * capped)
    teacher_exp = jnp.exp(teacher.astype(jnp.float32) / 2.0)
    student_total, teacher_total = lax.psum(
        (jnp.sum(student_exp, axis=1), jnp.sum(teacher_exp, axis=1)), ("dp", "vocab")
    )
    student_prob = student_exp / student_total[:, None]
    teacher_prob = teacher_exp / teacher_total[:, None]
    delta = (4096.0 * 2.0 * (student_prob - teacher_prob) * (1.0 - capped * capped)).astype(
        jnp.bfloat16
    )
    grad_head = lax.dot_general(
        gathered, delta, (((0,), (0,)), ((), ())), preferred_element_type=jnp.float32
    )
    share = lax.psum_scatter(
        lax.dot_general(
            delta, head_weight, (((1,), (1,)), ((), ())), preferred_element_type=jnp.float32
        ),
        ("dp", "vocab"),
        scatter_dimension=0,
        tiled=True,
    )
    return (share.astype(jnp.bfloat16), grad_head.astype(jnp.bfloat16))


def solution(mesh):
    placed = (P("dp", None), P(None, ("dp", "vocab")), P("vocab", "dp"))
    return jax.shard_map(
        per_device,
        mesh=mesh,
        in_specs=placed,
        out_specs=(P(("dp", "vocab"), None), P(None, ("dp", "vocab"))),
        check_vma=False,
    )
```

profile of v0, /device:TPU:1, one launch (start us, length us, event | category | flops | bytes accessed | tf_op | source)
XLA Modules:
  0.0 884.6 jit_solution(12272259481311134418)
XLA Ops:
  7.2 0.0 all-gather.2.cloned.1.call-start
  7.2 0.7 all-gather.2.cloned.1.call-update
  7.9 0.0 reduce-scatter.2.cloned.1.call-start
  7.9 1.8 copy.21
  9.7 34.9 %all_to_all.13 = bf16[64,16,1024]{2,0,1:T(8,128)(2,1)S(1)} all-to-all(bf16[64,16,1024]{2,0,1:T(8,128)(2,1)S(1)} %bitcast.16), channel_id=1, replica_groups=mesh['dp'=8,'vocab'=16] {'vocab'}, dimensions={1} | all-to-all | bytes 4194304 | tf_op jit(solution)/shard_map/all_to_all | solution.py:8
  44.6 2.7 fusion.2
  47.3 0.1 reduce_sum.25
  47.4 5.4 copy.15
  52.8 75.0 %all-gather.2.cloned.1.call-done = bf16[1024,3584]{1,0:T(8,128)(2,1)} async-done(((bf16[128,3584]{1,0:T(8,128)(2,1)}), bf16[1024,3584]{1,0:T(8,128)(2,1)}) %all-gather.2.cloned.1.call-update) | async-done | bytes 7340048 | tf_op jit(solution)/shard_map/all_gather | solution.py:9
  127.8 14.0 %fusion.1 = (f32[1024]{0:T(1024)S(1)}, f32[1024,1024]{0,1:T(8,128)}) fusion(bf16[1024,3584]{1,0:T(8,128)(2,1)} %all-gather.2.cloned.1.call-done, bf16[3584,1024]{1,0:T(8,128)(2,1)} %param.4), kind=kOutput, calls=%fused_computation.5 | convolution fusion | flops 7519337472 | bytes 18878464 | tf_op jit(solution)/shard_map/dot_general | solution.py:10
  141.9 64.8 %all-reduce = (f32[1024]{0:T(1024)S(1)}, f32[1024]{0:T(1024)S(1)}) all-reduce(f32[1024]{0:T(1024)S(1)} %reduce_sum.25, f32[1024]{0:T(1024)S(1)} %get-tuple-element.14), channel_id=1, replica_groups=mesh['dp'=8,'vocab'=16] {'dp','vocab'}, use_global_device_ids=true, to_apply=%region_3.0 | all-reduce | flops 2048 | bytes 16384 | tf_op jit(solution)/shard_map/psum | solution.py:14
  206.6 18.5 %fusion.3 = f32[1024,3584]{1,0:T(8,128)} fusion(bf16[3584,1024]{1,0:T(8,128)(2,1)} %param.4, f32[1024,1024]{0,1:T(8,128)} %copy.15, f32[1024,1024]{0,1:T(8,128)} %get-tuple-element.15, f32[1024]{0:T(1024)S(1)} %get-tuple-element.10, f32[1024]{0:T(1024)S(1)} %get-tuple-element.11), kind=kOutput, calls=%fused_computation.9 | convolution fusion | flops 7526678528 | bytes 30416896 | tf_op jit(solution)/shard_map/dot_general | solution.py:26
  225.2 0.0 reduce-scatter.2.cloned.1.call-update
  225.2 16.7 %fusion = bf16[3584,1024]{0,1:T(8,128)(2,1)} fusion(bf16[1024,3584]{1,0:T(8,128)(2,1)} %all-gather.2.cloned.1.call-done, f32[1024,1024]{0,1:T(8,128)} %copy.15, f32[1024,1024]{0,1:T(8,128)} %get-tuple-element.15, f32[1024]{0:T(1024)S(1)} %get-tuple-element.10, f32[1024]{0:T(1024)S(1)} %get-tuple-element.11), kind=kOutput, calls=%fused_computation.1 | convolution fusion | flops 7530348544 | bytes 23076864 | tf_op jit(solution)/shard_map/dot_general | solution.py:22
  241.9 10.4 %copy.16 = bf16[3584,1024]{1,0:T(8,128)(2,1)} copy(bf16[3584,1024]{0,1:T(8,128)(2,1)} %fusion) | data formatting | bytes 14680064
  252.3 623.9 %reduce-scatter.2.cloned.1.call-done = f32[8,3584]{1,0:T(8,128)} async-done(((f32[1024,3584]{1,0:T(8,128)}), f32[8,3584]{1,0:T(8,128)}) %reduce-scatter.2.cloned.1.call-update) | async-done | bytes 114704 | tf_op jit(solution)/shard_map/reduce_scatter | solution.py:25
  876.2 1.5 convert_element_type.21
Async XLA Ops:
  7.2 120.7 %all-gather.2.cloned.1.call-start = ((), (), s32[]{:S(2)}) async-start(), calls=%async_computation.2 | async-start | bytes 8257536 | tf_op jit(solution)/shard_map/all_gather | solution.py:9
  7.9 868.3 %reduce-scatter.2.cloned.1.call-start = ((), (), s32[]{:S(2)}) async-start(), calls=%async_computation.3 | async-start | bytes 14794752 | tf_op jit(solution)/shard_map/reduce_scatter | solution.py:25
Sparse Core Ops, SparseCore 0:
  10.3 117.4 all-gather.1
  225.3 650.8 reduce-scatter.1
where the time goes:
time: 892 us; the launch traced here: 885 us
  waiting for transfers between devices  700 us (78%)
  blocking collectives  99.7 us (11%)
  matrix products  49.3 us (6%)
  local copies, waits for them, and re-layouts  17.6 us (2%)
  between operations  14 us (2%)
    reduce_scatter x1, waiting for transfers between devices, per_device(): lax.psum_scatter(lax.dot_general(delta, head_weight, (((1,), (1,)), ((),...  624 us
    all_gather x1, waiting for transfers between devices, per_device(): gathered = lax.all_gather(hidden, 'dp', axis=0, tiled=True)  75 us
    psum x1, blocking collectives, per_device(): lax.psum((jnp.sum(student_exp, axis=1), jnp.sum(teacher_exp, axis=1)), ('...  64.8 us
    all_to_all x1, blocking collectives, per_device(): lax.all_to_all(teacher_logits, 'vocab', split_axis=1, concat_axis=0, tile...  34.9 us
    dot_general x1, matrix products, per_device(): lax.dot_general(delta, head_weight, (((1,), (1,)), ((), ())), preferred_e...  18.5 us
  transfers between devices with their start and end apart: 2, of which 2 were waited for; matrix products, arithmetic and copies ran while one was open for 4% of the time, Pallas kernels for 0%

commit v1 on v0

v1 whole, which is shorter than its diff:
```python
import jax
import jax.numpy as jnp
from jax import lax
from jax.sharding import Mesh, PartitionSpec as P

BF = jnp.bfloat16
F32 = jnp.float32
CHIPS = ("zh", "x", "y", "zl")
Z = ("zh", "zl")


def shift(v, axis, size, step):
    return lax.ppermute(v, axis, [(i, (i + step) % size) for i in range(size)])


def swap(v):
    return shift(v, "core", 2, 1)


def total(v):
    v = v + swap(v)
    for axis in ("x", "y", Z):
        v = v + shift(v, axis, 4, 1) + shift(v, axis, 4, 3) + shift(v, axis, 4, 2)
    return v


def gather_rows(own):
    far = shift(own, "zh", 2, 1)
    zh, x = lax.axis_index("zh"), lax.axis_index("x")
    rows, cols = own.shape
    out = jnp.zeros((8, rows, cols), own.dtype)
    for block, hi in ((own, zh), (far, 1 - zh)):
        for step in (0, 1, 3, 2):
            moved = block if step == 0 else shift(block, "x", 4, step)
            out = lax.dynamic_update_index_in_dim(out, moved, hi * 4 + (x - step) % 4, 0)
    return out.reshape(8 * rows, cols)


def per_device(hidden, head_weight, teacher_logits):
    core = lax.axis_index("core")
    half = hidden.shape[1] // 2
    own = gather_rows(lax.dynamic_slice_in_dim(hidden, core * half, half, 1))
    teacher = lax.all_to_all(
        teacher_logits, ("y", "zl", "core"), split_axis=1, concat_axis=0, tiled=True
    )
    other = swap(own)
    gathered = jnp.where(
        core == 0, jnp.concatenate([own, other], 1), jnp.concatenate([other, own], 1)
    )
    raw = jnp.dot(gathered, head_weight, preferred_element_type=F32)
    capped = jnp.tanh(raw / 30.0)
    student_exp = jnp.exp(15.0 * capped)
    teacher_exp = jnp.exp(teacher.astype(F32) / 2.0)
    totals = total(jnp.stack([jnp.sum(student_exp, axis=1), jnp.sum(teacher_exp, axis=1)]))
    student_prob = student_exp / totals[0][:, None]
    teacher_prob = teacher_exp / totals[1][:, None]
    delta = (4096.0 * 2.0 * (student_prob - teacher_prob) * (1.0 - capped * capped)).astype(BF)
    share = lax.dot_general(
        delta, head_weight, (((1,), (1,)), ((), ())), preferred_element_type=F32
    ).astype(BF)
    keep = lax.dynamic_slice_in_dim(share, core * half, half, 1)
    give = lax.dynamic_slice_in_dim(share, (1 - core) * half, half, 1)
    chip = (keep.astype(F32) + swap(give).astype(F32)).astype(BF)
    chip = lax.all_to_all(chip, CHIPS, split_axis=0, concat_axis=0, tiled=True)
    chip = jnp.sum(chip.reshape(64, 16, half).astype(F32), axis=0).astype(BF)
    mine = lax.dynamic_slice_in_dim(chip, core * 8, 8, 0)
    rest = swap(lax.dynamic_slice_in_dim(chip, (1 - core) * 8, 8, 0))
    grad_hidden = jnp.where(
        core == 0, jnp.concatenate([mine, rest], 1), jnp.concatenate([rest, mine], 1)
    )
    grad_head = lax.dot_general(
        gathered, delta, (((0,), (0,)), ((), ())), preferred_element_type=F32
    )
    return grad_hidden, grad_head.astype(BF)


def solution(mesh):
    fine = Mesh(mesh.devices.reshape(2, 4, 4, 2, 2), ("zh", "x", "y", "zl", "core"))
    dp, vocab = ("zh", "x"), ("y", "zl", "core")
    return jax.shard_map(
        per_device,
        mesh=fine,
        in_specs=(P(dp, None), P(None, dp + vocab), P(vocab, dp)),
        out_specs=(P(dp + vocab, None), P(None, dp + vocab)),
        check_vma=False,
    )
```

time: 892 us -> 242 us (0.27)
  waiting for transfers between devices: 700 us -> 115 us
  blocking collectives: 99.7 us -> 0 us
  starting transfers between devices: 0.08 us -> 45.3 us
  between operations: 14 us -> 0.75 us
    reduce_scatter x1 -> x0, waiting for transfers between devices: 624 us -> none  [per_device(): lax.psum_scatter(lax.dot_general(delta, head_weight, (((1,), (1,)), ((),...]
    all_gather x1 -> x0, waiting for transfers between devices: 75 us -> none  [per_device(): gathered = lax.all_gather(hidden, 'dp', axis=0, tiled=True)]
    all_to_all x0 -> x2, waiting for transfers between devices: none -> 71.7 us  [the longest x1 44.8 us: per_device(): chip = lax.all_to_all(chip, CHIPS, split_axis=0, concat_axis=0, tiled=True)]
    psum x1 -> x0, blocking collectives: 64.8 us -> none  [per_device(): lax.psum((jnp.sum(student_exp, axis=1), jnp.sum(teacher_exp, axis=1)), ('...]
    ppermute x0 -> x20, waiting for transfers between devices: none -> 42.9 us  [shift(): return lax.ppermute(v, axis, [(i, (i + step) % size) for i in range(size)])]
    all_to_all x1 -> x0, blocking collectives: 34.9 us -> none  [per_device(): lax.all_to_all(teacher_logits, 'vocab', split_axis=1, concat_axis=0, tile...]
    ppermute x0 -> x20, starting transfers between devices: none -> 34.2 us  [shift(): return lax.ppermute(v, axis, [(i, (i + step) % size) for i in range(size)])]
    all_to_all x0 -> x2, starting transfers between devices: none -> 11.1 us  [the longest x1 6.06 us: per_device(): chip = lax.all_to_all(chip, CHIPS, split_axis=0, concat_axis=0, tiled=True)]
  transfers between devices with their start and end apart: 2 -> 22, of which waited for: 2 -> 12; matrix products, arithmetic and copies ran while one was open for 4% -> 16% of each run, Pallas kernels for 0% -> 0%
where the time goes in v1:
time: 242 us; the launch traced here: 240 us
  waiting for transfers between devices  115 us (48%)
  matrix products  52.9 us (22%)
  starting transfers between devices  45.3 us (19%)
  local copies, waits for them, and re-layouts  18.1 us (7%)
  other arithmetic  8.68 us (4%)
    all_to_all x1, waiting for transfers between devices, per_device(): chip = lax.all_to_all(chip, CHIPS, split_axis=0, concat_axis=0, tiled=True)  44.8 us
    ppermute x20, waiting for transfers between devices, shift(): return lax.ppermute(v, axis, [(i, (i + step) % size) for i in range(size)])  42.9 us
    ppermute x20, starting transfers between devices, shift(): return lax.ppermute(v, axis, [(i, (i + step) % size) for i in range(size)])  34.2 us
    all_to_all x1, waiting for transfers between devices, per_device(): lax.all_to_all(teacher_logits, ('y', 'zl', 'core'), split_axis=1, concat_...  26.9 us
    dot_general x1, matrix products, per_device(): lax.dot_general(gathered, delta, (((0,), (0,)), ((), ())), preferred_elem...  22.2 us
    dot_general x1, matrix products, per_device(): lax.dot_general(delta, head_weight, (((1,), (1,)), ((), ())), preferred_e...  15.5 us
    dot_general x1, matrix products, per_device(): raw = jnp.dot(gathered, head_weight, preferred_element_type=F32)  15.2 us
    dynamic_update_slice x8, local copies, waits for them, and re-layouts, gather_rows(): lax.dynamic_update_index_in_dim(out, moved, hi * 4 + (x - step) % 4, 0)  8.82 us
  transfers between devices with their start and end apart: 22, of which 12 were waited for; matrix products, arithmetic and copies ran while one was open for 16% of the time, Pallas kernels for 0%

profile of v1, /device:TPU:1, one launch (start us, length us, event | category | flops | bytes accessed | tf_op | source)
XLA Modules:
  0.0 240.5 jit_solution(14905286624336850596)
XLA Ops:
  0.7 2.1 broadcast_in_dim.28
  2.7 2.2 bitcast_dynamic-update-slice_fusion.7
  4.9 4.4 %collective-permute-start.3 = (bf16[128,1792]{1,0:T(8,128)(2,1)}, bf16[128,1792]{1,0:T(8,128)(2,1)S(1)}, u32[]{:S(2)}, u32[]{:S(2)}) collective-permute-start(bf16[128,1792]{1,0:T(8,128)(2,1)} %get-tuple-element.3), channel_id=1, source_target_pairs={{0,64},{64,0},{1,65},{65,1},{2,66},{66,2},{3,67},{67,3},{4,68},{68... | collective-permute-start | bytes 1376264 | tf_op jit(solution)/shard_map/ppermute | solution.py:13
  12.0 1.5 collective-permute-start.2
  13.5 6.2 %collective-permute-done.3 = bf16[128,1792]{1,0:T(8,128)(2,1)S(1)} collective-permute-done((bf16[128,1792]{1,0:T(8,128)(2,1)}, bf16[128,1792]{1,0:T(8,128)(2,1)S(1)}, u32[]{:S(2)}, u32[]{:S(2)}) %collective-permute-start.3) | collective-permute-done | bytes 458784 | tf_op jit(solution)/shard_map/ppermute | solution.py:13
  22.4 1.5 collective-permute-start.6
  24.0 1.8 bitcast_dynamic-update-slice_fusion.6
  26.6 6.1 %collective-permute-done.2 = bf16[128,1792]{1,0:T(8,128)(2,1)S(1)} collective-permute-done((bf16[128,1792]{1,0:T(8,128)(2,1)}, bf16[128,1792]{1,0:T(8,128)(2,1)S(1)}, u32[]{:S(2)}, u32[]{:S(2)}) %collective-permute-start.2) | collective-permute-done | bytes 458784 | tf_op jit(solution)/shard_map/ppermute | solution.py:13
  34.3 7.8 %collective-permute-done.4 = bf16[128,1792]{1,0:T(8,128)(2,1)S(1)} collective-permute-done((bf16[128,1792]{1,0:T(8,128)(2,1)S(1)}, bf16[128,1792]{1,0:T(8,128)(2,1)S(1)}, u32[]{:S(2)}, u32[]{:S(2)}) %collective-permute-start.4) | collective-permute-done | bytes 458784 | tf_op jit(solution)/shard_map/ppermute | solution.py:13
  43.7 8.7 %collective-permute-done.6 = bf16[128,1792]{1,0:T(8,128)(2,1)S(1)} collective-permute-done((bf16[128,1792]{1,0:T(8,128)(2,1)S(1)}, bf16[128,1792]{1,0:T(8,128)(2,1)S(1)}, u32[]{:S(2)}, u32[]{:S(2)}) %collective-permute-start.6) | collective-permute-done | bytes 458784 | tf_op jit(solution)/shard_map/ppermute | solution.py:13
  53.1 1.9 collective-permute-start.7
  55.0 1.6 copy.20
  56.5 5.0 %all-to-all-start = ((bf16[64,16,1024]{2,0,1:T(8,128)(2,1)}), bf16[64,16,1024]{2,0,1:T(8,128)(2,1)S(1)}, u32[]{:S(2)}, u32[]{:S(2)}) async-start(bf16[64,16,1024]{2,0,1:T(8,128)(2,1)} %bitcast.34), calls=%async_computation | async-start | bytes 4194304 | tf_op jit(solution)/shard_map/all_to_all | solution.py:43
  61.6 26.9 %all-to-all-done = bf16[64,16,1024]{2,0,1:T(8,128)(2,1)S(1)} async-done(((bf16[64,16,1024]{2,0,1:T(8,128)(2,1)}), bf16[64,16,1024]{2,0,1:T(8,128)(2,1)S(1)}, u32[]{:S(2)}, u32[]{:S(2)}) %all-to-all-start) | async-done | bytes 2097184 | tf_op jit(solution)/shard_map/all_to_all | solution.py:43
  88.5 2.7 %fusion.2 = (f32[64,16]{0,1:T(8,128)S(1)}, f32[64,16,1024]{2,0,1:T(8,128)}) fusion(bf16[64,16,1024]{2,0,1:T(8,128)(2,1)S(1)} %all-to-all-done), kind=kLoop, calls=%fused_computation.11 | loop fusion | flops 3144704 | bytes 6295552 | tf_op jit(solution)/shard_map/reduce_sum | solution.py:54
  91.3 15.2 %fusion = (f32[1024]{0:T(1024)S(1)}, f32[1024,1024]{0,1:T(8,128)}) fusion(bf16[3584,1024]{1,0:T(8,128)(2,1)} %param.4, bf16[1024,1792]{1,0:T(8,128)(2,1)} %collective-permute-done.7, bf16[1024,1792]{1,0:T(8,128)(2,1)} %bitcast.8, pred[]{:T(512)S(6)} %eq.13), kind=kOutput, calls=%fused_computation.7 | convolution fusion | flops 7552367616 | bytes 18878464 | tf_op jit(solution)/shard_map/dot_general | solution.py:50
  108.4 2.5 %collective-permute-start.10 = (f32[2,1024]{1,0:T(2,128)S(1)}, f32[2,1024]{1,0:T(2,128)S(1)}, u32[]{:S(2)}, u32[]{:S(2)}) collective-permute-start(f32[2,1024]{1,0:T(2,128)S(1)} %fusion.5), channel_id=1, source_target_pairs={{0,48},{16,0},{32,16},{48,32},{1,49},{17,1},{33,17},{49,33},{2,50}... | collective-permute-start | bytes 24584 | tf_op jit(solution)/shard_map/ppermute | solution.py:13
  111.7 3.2 %collective-permute-done.11 = f32[2,1024]{1,0:T(2,128)S(1)} collective-permute-done((f32[2,1024]{1,0:T(2,128)S(1)}, f32[2,1024]{1,0:T(2,128)S(1)}, u32[]{:S(2)}, u32[]{:S(2)}) %collective-permute-start.11) | collective-permute-done | bytes 8224 | tf_op jit(solution)/shard_map/ppermute | solution.py:13
  115.0 2.7 %collective-permute-start.13 = (f32[2,1024]{1,0:T(2,128)S(1)}, f32[2,1024]{1,0:T(2,128)S(1)}, u32[]{:S(2)}, u32[]{:S(2)}) collective-permute-start(f32[2,1024]{1,0:T(2,128)S(1)} %add_add_fusion.2), channel_id=1, source_target_pairs={{0,12},{4,0},{8,4},{12,8},{1,13},{5,1},{9,5},{13,9},{2,14},{6,2},{... | collective-permute-start | bytes 24584 | tf_op jit(solution)/shard_map/ppermute | solution.py:13
  118.7 3.0 %collective-permute-done.14 = f32[2,1024]{1,0:T(2,128)S(1)} collective-permute-done((f32[2,1024]{1,0:T(2,128)S(1)}, f32[2,1024]{1,0:T(2,128)S(1)}, u32[]{:S(2)}, u32[]{:S(2)}) %collective-permute-start.14) | collective-permute-done | bytes 8224 | tf_op jit(solution)/shard_map/ppermute | solution.py:13
  121.7 2.7 %collective-permute-start.15 = (f32[2,1024]{1,0:T(2,128)S(1)}, f32[2,1024]{1,0:T(2,128)S(1)}, u32[]{:S(2)}, u32[]{:S(2)}) collective-permute-start(f32[2,1024]{1,0:T(2,128)S(1)} %add_add_fusion.1), channel_id=1, source_target_pairs={{0,2},{2,64},{64,66},{66,0},{1,3},{3,65},{65,67},{67,1},{4,6},{6,6... | collective-permute-start | bytes 24584 | tf_op jit(solution)/shard_map/ppermute | solution.py:13
  124.6 1.7 collective-permute-start.17
  126.3 5.3 %copy.15 = f32[1024,1024]{0,1:T(8,128)} copy(f32[1024,1024]{1,0:T(8,128)} %bitcast.32) | data formatting | bytes 8388608 | tf_op jit(solution)/shard_map/exp | solution.py:53
  131.7 15.5 %convolution_convert_fusion.1 = bf16[1024,3584]{1,0:T(8,128)(2,1)S(1)} fusion(bf16[3584,1024]{1,0:T(8,128)(2,1)} %param.4, f32[1024,1024]{0,1:T(8,128)} %copy.15, f32[1024,1024]{0,1:T(8,128)} %get-tuple-element.11, f32[1024]{0:T(1024)S(1)} %bitcast.42, f32[1024]{0:T(1024)S(1)} %bitcast.40), kind=kOutput, calls=%fused_computation.1 | convolution fusion | flops 7530348544 | bytes 23076864 | tf_op jit(solution)/shard_map/dot_general | solution.py:58
  147.5 4.2 %collective-permute-start.18 = (bf16[1024,1792]{1,0:T(8,128)(2,1)S(1)}, bf16[1024,1792]{1,0:T(8,128)(2,1)S(1)}, u32[]{:S(2)}, u32[]{:S(2)}) collective-permute-start(bf16[1024,1792]{1,0:T(8,128)(2,1)S(1)} %constant_dynamic-slice_fusion.2), channel_id=1, source_target_pairs={{0,1},{1,0},{2,3},{3,2},{4,5},{5,4},{6,7},{7,6},{8,9},{9,8},{10,11... | collective-permute-start | bytes 11010056 | tf_op jit(solution)/shard_map/ppermute | solution.py:13
  151.6 6.0 %collective-permute-done.18 = bf16[1024,1792]{1,0:T(8,128)(2,1)S(1)} collective-permute-done((bf16[1024,1792]{1,0:T(8,128)(2,1)S(1)}, bf16[1024,1792]{1,0:T(8,128)(2,1)S(1)}, u32[]{:S(2)}, u32[]{:S(2)}) %collective-permute-start.18) | collective-permute-done | bytes 3670048 | tf_op jit(solution)/shard_map/ppermute | solution.py:13
  157.7 2.7 %add_convert_fusion = bf16[1024,1792]{1,0:T(8,128)(2,1)} fusion(bf16[1024,1792]{1,0:T(8,128)(2,1)S(1)} %collective-permute-done.18, bf16[1024,3584]{1,0:T(8,128)(2,1)S(1)} %convolution_convert_fusion.1, s32[]{:T(128)S(6)} %select_n.83), kind=kLoop, calls=%fused_computation.3 | loop fusion | flops 7340032 | bytes 11010052 | tf_op jit(solution)/shard_map/convert_element_type | solution.py:63
  160.4 6.1 %all-to-all-start.1 = ((bf16[64,16,1792]{2,1,0:T(8,128)(2,1)}), bf16[64,16,1792]{2,1,0:T(8,128)(2,1)}, u32[]{:S(2)}, u32[]{:S(2)}) async-start(bf16[64,16,1792]{2,1,0:T(8,128)(2,1)} %bitcast.33), calls=%async_computation.1 | async-start | bytes 7340032 | tf_op jit(solution)/shard_map/all_to_all | solution.py:64
  166.5 44.8 %all-to-all-done.1 = bf16[64,16,1792]{2,1,0:T(8,128)(2,1)} async-done(((bf16[64,16,1792]{2,1,0:T(8,128)(2,1)}), bf16[64,16,1792]{2,1,0:T(8,128)(2,1)}, u32[]{:S(2)}, u32[]{:S(2)}) %all-to-all-start.1) | async-done | bytes 3670048 | tf_op jit(solution)/shard_map/all_to_all | solution.py:64
  211.3 2.6 %reduce_sum.35 = bf16[16,1792]{1,0:T(8,128)(2,1)S(1)} reduce(bf16[64,16,1792]{2,1,0:T(8,128)(2,1)} %all-to-all-done.1, bf16[]{:T(256)} %constant.81.clone.1), dimensions={0}, to_apply=%region_2.3 | reduce | flops 1806336 | bytes 3727362 | tf_op jit(solution)/shard_map/reduce_sum | solution.py:65
  213.9 3.8 %collective-permute-start.19 = (bf16[8,1792]{1,0:T(8,128)(2,1)S(1)}, bf16[8,1792]{1,0:T(8,128)(2,1)S(1)}, u32[]{:S(2)}, u32[]{:S(2)}) collective-permute-start(bf16[8,1792]{1,0:T(8,128)(2,1)S(1)} %get-tuple-element.7), channel_id=1, source_target_pairs={{0,1},{1,0},{2,3},{3,2},{4,5},{5,4},{6,7},{7,6},{8,9},{9,8},{10,11... | collective-permute-start | bytes 86024 | tf_op jit(solution)/shard_map/ppermute | solution.py:13
  217.6 22.2 %convolution_convert_fusion = bf16[3584,1024]{1,0:T(8,128)(2,1)} fusion(bf16[1024,1792]{1,0:T(8,128)(2,1)} %collective-permute-done.7, bf16[1024,1792]{1,0:T(8,128)(2,1)} %bitcast.8, pred[]{:T(512)S(6)} %eq.13, f32[1024,1024]{0,1:T(8,128)} %copy.15, f32[1024,1024]{0,1:T(8,128)} %get-tuple-element.11, f32[1024]{0:T(1024)S(1)} %bitcast.43, f32[1024]{0:T(1024)S(1)} %bitcast.41), kind=kOutput, calls=%fused_computation | convolution fusion | flops 7563378688 | bytes 23076864 | tf_op jit(solution)/shard_map/dot_general | solution.py:71
  (41 shorter events, 15.2 us)
Async XLA Ops:
  2.7 52.3 %copy-start = (bf16[64,16384]{1,0:T(8,128)(2,1)S(1)}, bf16[64,16384]{1,0:T(8,128)(2,1)}, u32[]{:S(2)}) copy-start(bf16[64,16384]{1,0:T(8,128)(2,1)} %param.5) | copy-start | bytes 6291460
  4.9 14.9 %collective-permute-start.3 = (bf16[128,1792]{1,0:T(8,128)(2,1)}, bf16[128,1792]{1,0:T(8,128)(2,1)S(1)}, u32[]{:S(2)}, u32[]{:S(2)}) collective-permute-start(bf16[128,1792]{1,0:T(8,128)(2,1)} %get-tuple-element.3), channel_id=1, source_target_pairs={{0,64},{64,0},{1,65},{65,1},{2,66},{66,2},{3,67},{67,3},{4,68},{68... | collective-permute-start | bytes 1376264 | tf_op jit(solution)/shard_map/ppermute | solution.py:13
  9.3 13.1 %collective-permute-start = (bf16[128,1792]{1,0:T(8,128)(2,1)}, bf16[128,1792]{1,0:T(8,128)(2,1)}, u32[]{:S(2)}, u32[]{:S(2)}) collective-permute-start(bf16[128,1792]{1,0:T(8,128)(2,1)} %get-tuple-element.3), channel_id=1, source_target_pairs={{0,16},{16,32},{32,48},{48,0},{1,17},{17,33},{33,49},{49,1},{2,18}... | collective-permute-start | bytes 1376264 | tf_op jit(solution)/shard_map/ppermute | solution.py:13
  10.5 15.2 %collective-permute-start.1 = (bf16[128,1792]{1,0:T(8,128)(2,1)}, bf16[128,1792]{1,0:T(8,128)(2,1)S(1)}, u32[]{:S(2)}, u32[]{:S(2)}) collective-permute-start(bf16[128,1792]{1,0:T(8,128)(2,1)} %get-tuple-element.3), channel_id=1, source_target_pairs={{0,48},{16,0},{32,16},{48,32},{1,49},{17,1},{33,17},{49,33},{2,50}... | collective-permute-start | bytes 1376264 | tf_op jit(solution)/shard_map/ppermute | solution.py:13
  12.0 20.7 %collective-permute-start.2 = (bf16[128,1792]{1,0:T(8,128)(2,1)}, bf16[128,1792]{1,0:T(8,128)(2,1)S(1)}, u32[]{:S(2)}, u32[]{:S(2)}) collective-permute-start(bf16[128,1792]{1,0:T(8,128)(2,1)} %get-tuple-element.3), channel_id=1, source_target_pairs={{0,32},{16,48},{32,0},{48,16},{1,33},{17,49},{33,1},{49,17},{2,34}... | collective-permute-start | bytes 1376264 | tf_op jit(solution)/shard_map/ppermute | solution.py:13
  19.7 22.3 %collective-permute-start.4 = (bf16[128,1792]{1,0:T(8,128)(2,1)S(1)}, bf16[128,1792]{1,0:T(8,128)(2,1)S(1)}, u32[]{:S(2)}, u32[]{:S(2)}) collective-permute-start(bf16[128,1792]{1,0:T(8,128)(2,1)S(1)} %collective-permute-done.3), channel_id=1, source_target_pairs={{0,16},{16,32},{32,48},{48,0},{1,17},{17,33},{33,49},{49,1},{2,18}... | collective-permute-start | bytes 1376264 | tf_op jit(solution)/shard_map/ppermute | solution.py:13
  21.0 21.9 %collective-permute-start.5 = (bf16[128,1792]{1,0:T(8,128)(2,1)S(1)}, bf16[128,1792]{1,0:T(8,128)(2,1)S(1)}, u32[]{:S(2)}, u32[]{:S(2)}) collective-permute-start(bf16[128,1792]{1,0:T(8,128)(2,1)S(1)} %collective-permute-done.3), channel_id=1, source_target_pairs={{0,48},{16,0},{32,16},{48,32},{1,49},{17,1},{33,17},{49,33},{2,50}... | collective-permute-start | bytes 1376264 | tf_op jit(solution)/shard_map/ppermute | solution.py:13
  22.4 29.9 %collective-permute-start.6 = (bf16[128,1792]{1,0:T(8,128)(2,1)S(1)}, bf16[128,1792]{1,0:T(8,128)(2,1)S(1)}, u32[]{:S(2)}, u32[]{:S(2)}) collective-permute-start(bf16[128,1792]{1,0:T(8,128)(2,1)S(1)} %collective-permute-done.3), channel_id=1, source_target_pairs={{0,32},{16,48},{32,0},{48,16},{1,33},{17,49},{33,1},{49,17},{2,34}... | collective-permute-start | bytes 1376264 | tf_op jit(solution)/shard_map/ppermute | solution.py:13
  53.1 38.2 %collective-permute-start.7 = (bf16[1024,1792]{1,0:T(8,128)(2,1)}, bf16[1024,1792]{1,0:T(8,128)(2,1)}, u32[]{:S(2)}, u32[]{:S(2)}) collective-permute-start(bf16[1024,1792]{1,0:T(8,128)(2,1)} %bitcast.8), channel_id=1, source_target_pairs={{0,1},{1,0},{2,3},{3,2},{4,5},{5,4},{6,7},{7,6},{8,9},{9,8},{10,11... | collective-permute-start | bytes 11010056 | tf_op jit(solution)/shard_map/ppermute | solution.py:13
  56.5 32.0 %all-to-all-start = ((bf16[64,16,1024]{2,0,1:T(8,128)(2,1)}), bf16[64,16,1024]{2,0,1:T(8,128)(2,1)S(1)}, u32[]{:S(2)}, u32[]{:S(2)}) async-start(bf16[64,16,1024]{2,0,1:T(8,128)(2,1)} %bitcast.34), calls=%async_computation | async-start | bytes 4194304 | tf_op jit(solution)/shard_map/all_to_all | solution.py:43
  106.5 1.8 collective-permute-start.8
  108.4 3.3 %collective-permute-start.10 = (f32[2,1024]{1,0:T(2,128)S(1)}, f32[2,1024]{1,0:T(2,128)S(1)}, u32[]{:S(2)}, u32[]{:S(2)}) collective-permute-start(f32[2,1024]{1,0:T(2,128)S(1)} %fusion.5), channel_id=1, source_target_pairs={{0,48},{16,0},{32,16},{48,32},{1,49},{17,1},{33,17},{49,33},{2,50}... | collective-permute-start | bytes 24584 | tf_op jit(solution)/shard_map/ppermute | solution.py:13
  110.9 4.0 %collective-permute-start.11 = (f32[2,1024]{1,0:T(2,128)S(1)}, f32[2,1024]{1,0:T(2,128)S(1)}, u32[]{:S(2)}, u32[]{:S(2)}) collective-permute-start(f32[2,1024]{1,0:T(2,128)S(1)} %fusion.5), channel_id=1, source_target_pairs={{0,32},{16,48},{32,0},{48,16},{1,33},{17,49},{33,1},{49,17},{2,34}... | collective-permute-start | bytes 24584 | tf_op jit(solution)/shard_map/ppermute | solution.py:13
  111.1 3.8 %collective-permute-start.9 = (f32[2,1024]{1,0:T(2,128)S(1)}, f32[2,1024]{1,0:T(2,128)S(1)}, u32[]{:S(2)}, u32[]{:S(2)}) collective-permute-start(f32[2,1024]{1,0:T(2,128)S(1)} %fusion.5), channel_id=1, source_target_pairs={{0,16},{16,32},{32,48},{48,0},{1,17},{17,33},{33,49},{49,1},{2,18}... | collective-permute-start | bytes 24584 | tf_op jit(solution)/shard_map/ppermute | solution.py:13
  114.9 3.8 %collective-permute-start.12 = (f32[2,1024]{1,0:T(2,128)S(1)}, f32[2,1024]{1,0:T(2,128)S(1)}, u32[]{:S(2)}, u32[]{:S(2)}) collective-permute-start(f32[2,1024]{1,0:T(2,128)S(1)} %add_add_fusion.2), channel_id=1, source_target_pairs={{0,4},{4,8},{8,12},{12,0},{1,5},{5,9},{9,13},{13,1},{2,6},{6,10},{... | collective-permute-start | bytes 24584 | tf_op jit(solution)/shard_map/ppermute | solution.py:13
  115.0 3.7 %collective-permute-start.13 = (f32[2,1024]{1,0:T(2,128)S(1)}, f32[2,1024]{1,0:T(2,128)S(1)}, u32[]{:S(2)}, u32[]{:S(2)}) collective-permute-start(f32[2,1024]{1,0:T(2,128)S(1)} %add_add_fusion.2), channel_id=1, source_target_pairs={{0,12},{4,0},{8,4},{12,8},{1,13},{5,1},{9,5},{13,9},{2,14},{6,2},{... | collective-permute-start | bytes 24584 | tf_op jit(solution)/shard_map/ppermute | solution.py:13
  117.7 4.0 %collective-permute-start.14 = (f32[2,1024]{1,0:T(2,128)S(1)}, f32[2,1024]{1,0:T(2,128)S(1)}, u32[]{:S(2)}, u32[]{:S(2)}) collective-permute-start(f32[2,1024]{1,0:T(2,128)S(1)} %add_add_fusion.2), channel_id=1, source_target_pairs={{0,8},{4,12},{8,0},{12,4},{1,9},{5,13},{9,1},{13,5},{2,10},{6,14},... | collective-permute-start | bytes 24584 | tf_op jit(solution)/shard_map/ppermute | solution.py:13
  121.7 10.0 %collective-permute-start.15 = (f32[2,1024]{1,0:T(2,128)S(1)}, f32[2,1024]{1,0:T(2,128)S(1)}, u32[]{:S(2)}, u32[]{:S(2)}) collective-permute-start(f32[2,1024]{1,0:T(2,128)S(1)} %add_add_fusion.1), channel_id=1, source_target_pairs={{0,2},{2,64},{64,66},{66,0},{1,3},{3,65},{65,67},{67,1},{4,6},{6,6... | collective-permute-start | bytes 24584 | tf_op jit(solution)/shard_map/ppermute | solution.py:13
  124.5 7.2 %collective-permute-start.16 = (f32[2,1024]{1,0:T(2,128)S(1)}, f32[2,1024]{1,0:T(2,128)S(1)}, u32[]{:S(2)}, u32[]{:S(2)}) collective-permute-start(f32[2,1024]{1,0:T(2,128)S(1)} %add_add_fusion.1), channel_id=1, source_target_pairs={{0,66},{2,0},{64,2},{66,64},{1,67},{3,1},{65,3},{67,65},{4,70},{6,... | collective-permute-start | bytes 24584 | tf_op jit(solution)/shard_map/ppermute | solution.py:13
  124.6 7.0 %collective-permute-start.17 = (f32[2,1024]{1,0:T(2,128)S(1)}, f32[2,1024]{1,0:T(2,128)S(1)}, u32[]{:S(2)}, u32[]{:S(2)}) collective-permute-start(f32[2,1024]{1,0:T(2,128)S(1)} %add_add_fusion.1), channel_id=1, source_target_pairs={{0,64},{2,66},{64,0},{66,2},{1,65},{3,67},{65,1},{67,3},{4,68},{6,... | collective-permute-start | bytes 24584 | tf_op jit(solution)/shard_map/ppermute | solution.py:13
  147.5 10.2 %collective-permute-start.18 = (bf16[1024,1792]{1,0:T(8,128)(2,1)S(1)}, bf16[1024,1792]{1,0:T(8,128)(2,1)S(1)}, u32[]{:S(2)}, u32[]{:S(2)}) collective-permute-start(bf16[1024,1792]{1,0:T(8,128)(2,1)S(1)} %constant_dynamic-slice_fusion.2), channel_id=1, source_target_pairs={{0,1},{1,0},{2,3},{3,2},{4,5},{5,4},{6,7},{7,6},{8,9},{9,8},{10,11... | collective-permute-start | bytes 11010056 | tf_op jit(solution)/shard_map/ppermute | solution.py:13
  160.4 50.9 %all-to-all-start.1 = ((bf16[64,16,1792]{2,1,0:T(8,128)(2,1)}), bf16[64,16,1792]{2,1,0:T(8,128)(2,1)}, u32[]{:S(2)}, u32[]{:S(2)}) async-start(bf16[64,16,1792]{2,1,0:T(8,128)(2,1)} %bitcast.33), calls=%async_computation.1 | async-start | bytes 7340032 | tf_op jit(solution)/shard_map/all_to_all | solution.py:64
  213.9 25.9 %collective-permute-start.19 = (bf16[8,1792]{1,0:T(8,128)(2,1)S(1)}, bf16[8,1792]{1,0:T(8,128)(2,1)S(1)}, u32[]{:S(2)}, u32[]{:S(2)}) collective-permute-start(bf16[8,1792]{1,0:T(8,128)(2,1)S(1)} %get-tuple-element.7), channel_id=1, source_target_pairs={{0,1},{1,0},{2,3},{3,2},{4,5},{5,4},{6,7},{7,6},{8,9},{9,8},{10,11... | collective-permute-start | bytes 86024 | tf_op jit(solution)/shard_map/ppermute | solution.py:13

commit v2 on v1

v2 whole, which is shorter than its diff:
```python
import functools

import jax
import jax.numpy as jnp
from jax import lax
from jax.experimental import pallas as pl
from jax.experimental.pallas import tpu as pltpu
from jax.sharding import Mesh, PartitionSpec as P

BF = jnp.bfloat16
F32 = jnp.float32
CHIPS = ("zh", "x", "y", "zl")
Z = ("zh", "zl")
SMEM = pl.BlockSpec(memory_space=pltpu.SMEM)
VMEM = pl.BlockSpec(memory_space=pltpu.VMEM)
ANY = pl.BlockSpec(memory_space=pl.ANY)


def shift(v, axis, size, step):
    return lax.ppermute(v, axis, [(i, (i + step) % size) for i in range(size)])


def swap(v):
    return shift(v, "core", 2, 1)


def total(v):
    v = v + swap(v)
    for axis in ("x", "y", Z):
        v = v + shift(v, axis, 4, 1) + shift(v, axis, 4, 3) + shift(v, axis, 4, 2)
    return v


def scores_kernel(tile, place, hidden, *refs):
    blocks, (weight, teacher_sum, gathered, capped, sums) = refs[:14], refs[14:19]
    rows_v, weight_v, capped_v, part, row_sem, weight_sem, out_sem, capped_sem = refs[19:]
    rows, half = blocks[0].shape
    own = pl.multiple_of(place[8] * half, half)
    other = pl.multiple_of((1 - place[8]) * half, half)
    loads = []
    for i in range(8):
        at = pl.ds(pl.multiple_of(place[i] * rows, rows), rows)
        if i == 0:
            loads.append((hidden, rows_v.at[at, :]))
        else:
            loads.append((blocks[i - 1], rows_v.at[at, pl.ds(own, half)]))
            loads.append((blocks[i + 6], rows_v.at[at, pl.ds(other, half)]))
    loads = [pltpu.make_async_copy(a, b, row_sem.at[i]) for i, (a, b) in enumerate(loads)]
    count = weight.shape[1] // tile
    cols = [slice(n * tile, (n + 1) * tile) for n in range(count)]
    weights = [
        pltpu.make_async_copy(weight.at[:, c], weight_v.at[:, c], weight_sem.at[n])
        for n, c in enumerate(cols)
    ]
    weights[0].start()
    for c in loads:
        c.start()
    for c in weights[1:]:
        c.start()
    for c in loads:
        c.wait()
    keep = pltpu.make_async_copy(rows_v, gathered, out_sem)
    keep.start()
    part[...] = jnp.zeros_like(part)
    stores = []
    for n, c in enumerate(cols):
        weights[n].wait()

        @pl.loop(0, rows_v.shape[0] // 512)
        def _(m):
            at = pl.ds(pl.multiple_of(m * 512, 512), 512)
            raw = jnp.dot(rows_v[at, :], weight_v[:, c], preferred_element_type=F32)
            cap = jnp.tanh(raw / 30.0)
            capped_v[at, c] = cap
            e = jnp.exp(15.0 * cap)
            s = part[at, :]
            for k in range(tile // 128):
                s = s + e[:, k * 128 : (k + 1) * 128]
            part[at, :] = s

        stores.append(
            pltpu.make_async_copy(capped_v.at[:, c], capped.at[:, c], capped_sem.at[n])
        )
        stores[-1].start()
    sums[0:1, :] = jnp.sum(part[...].T, axis=0, keepdims=True)
    sums[1:2, :] = teacher_sum[...]
    for c in stores + [keep]:
        c.wait()


def scores(place, hidden, own, other, weight, teacher_sum):
    rows, depth, cols, tile = 8 * hidden.shape[0], *weight.shape, 256
    return pl.pallas_call(
        functools.partial(scores_kernel, tile),
        name="scores",
        out_shape=(
            jax.ShapeDtypeStruct((rows, depth), BF),
            jax.ShapeDtypeStruct((rows, cols), F32),
            jax.ShapeDtypeStruct((2, rows), F32),
        ),
        in_specs=[SMEM, ANY] + [ANY] * 14 + [ANY, VMEM],
        out_specs=(ANY, ANY, VMEM),
        scratch_shapes=[
            pltpu.VMEM((rows, depth), BF),
            pltpu.VMEM((depth, cols), BF),
            pltpu.VMEM((rows, cols), F32),
            pltpu.VMEM((rows, 128), F32),
            pltpu.SemaphoreType.DMA((15,)),
            pltpu.SemaphoreType.DMA((cols // tile,)),
            pltpu.SemaphoreType.DMA,
            pltpu.SemaphoreType.DMA((cols // tile,)),
        ],
        compiler_params=pltpu.CompilerParams(vmem_limit_bytes=40 << 20),
        cost_estimate=pl.CostEstimate(
            flops=2 * rows * depth * cols, bytes_accessed=20 << 20, transcendentals=2 * rows * cols
        ),
    )(place, hidden, *own, *other, weight, teacher_sum)


def delta_kernel(core, capped, teacher, totals, weight, delta, share):
    scale = (8192.0 / totals[...]).T
    cap = capped[...]
    student = jnp.exp(15.0 * cap) * scale[:, 0:1]
    target = jnp.exp(teacher[...].astype(F32) * 0.5) * scale[:, 1:2]
    d = ((student - target) * (1.0 - cap * cap)).astype(BF)
    delta[...] = d
    share[...] = lax.dot_general(
        d, weight[...], (((1,), (1,)), ((), ())), preferred_element_type=F32
    ).astype(BF)


def delta_and_share(core, capped, teacher, totals, weight):
    (rows, cols), half, tile = capped.shape, weight.shape[0] // 2, 256
    block = lambda shape, f: pl.BlockSpec(shape, f)
    return pl.pallas_call(
        delta_kernel,
        name="delta_and_share",
        grid_spec=pltpu.PrefetchScalarGridSpec(
            num_scalar_prefetch=1,
            grid=(rows // tile,),
            in_specs=[
                block((tile, cols), lambda i, core: (i, 0)),
                block((tile, cols), lambda i, core: (i, 0)),
                block((8, tile), lambda i, core: (0, i)),
                block((half, cols), lambda i, core: (1 - core[0], 0)),
            ],
            out_specs=[
                block((tile, cols), lambda i, core: (i, 0)),
                block((tile, half), lambda i, core: (i, 0)),
            ],
        ),
        out_shape=(
            jax.ShapeDtypeStruct((rows, cols), BF),
            jax.ShapeDtypeStruct((rows, half), BF),
        ),
        compiler_params=pltpu.CompilerParams(vmem_limit_bytes=40 << 20),
        cost_estimate=pl.CostEstimate(
            flops=2 * rows * half * cols, bytes_accessed=16 << 20, transcendentals=2 * rows * cols
        ),
    )(core, capped, teacher, totals, weight)


def share_kernel(core, delta, weight, share):
    share[...] = lax.dot_general(
        delta[...], weight[...], (((1,), (1,)), ((), ())), preferred_element_type=F32
    ).astype(BF)


def own_share(core, delta, weight):
    (rows, cols), half, tile = delta.shape, weight.shape[0] // 2, 256
    return pl.pallas_call(
        share_kernel,
        name="own_share",
        grid_spec=pltpu.PrefetchScalarGridSpec(
            num_scalar_prefetch=1,
            grid=(rows // tile,),
            in_specs=[
                pl.BlockSpec((tile, cols), lambda i, core: (i, 0)),
                pl.BlockSpec((half, cols), lambda i, core: (core[0], 0)),
            ],
            out_specs=pl.BlockSpec((tile, half), lambda i, core: (i, 0)),
        ),
        out_shape=jax.ShapeDtypeStruct((rows, half), BF),
        compiler_params=pltpu.CompilerParams(vmem_limit_bytes=40 << 20),
        cost_estimate=pl.CostEstimate(
            flops=2 * rows * half * cols, bytes_accessed=10 << 20, transcendentals=0
        ),
    )(core, delta, weight)


def chip_sum_kernel(parts, after, out):
    out[...] = jnp.sum(parts[...].astype(F32), axis=0).astype(BF)


def chip_sum(parts, after):
    _, rows, cols = parts.shape
    tile = 256
    return pl.pallas_call(
        chip_sum_kernel,
        name="chip_sum",
        grid=(cols // tile,),
        in_specs=[pl.BlockSpec((parts.shape[0], rows, tile), lambda i: (0, 0, i)), ANY],
        out_specs=pl.BlockSpec((rows, tile), lambda i: (0, i)),
        out_shape=jax.ShapeDtypeStruct((rows, cols), BF),
        cost_estimate=pl.CostEstimate(flops=parts.size, bytes_accessed=4 << 20, transcendentals=0),
    )(parts, after)


def per_device(hidden, head_weight, teacher_logits):
    core = lax.axis_index("core")
    zh, x = lax.axis_index("zh"), lax.axis_index("x")
    vocab = lax.axis_index(("y", "zl", "core"))
    half = hidden.shape[1] // 2
    rows = 8 * hidden.shape[0]
    steps = (1, 3, 2)

    near = lax.dynamic_slice_in_dim(hidden, core * half, half, 1)
    far = shift(near, "zh", 2, 1)
    own = [shift(near, "x", 4, s) for s in steps]
    own += [far] + [shift(far, "x", 4, s) for s in steps]
    other = [swap(b) for b in own]
    place = [zh * 4 + (x - s) % 4 for s in (0,) + steps]
    place += [(1 - zh) * 4 + (x - s) % 4 for s in (0,) + steps]
    place = jnp.stack(place + [core]).astype(jnp.int32)

    teacher = lax.all_to_all(
        teacher_logits, ("y", "zl", "core"), split_axis=1, concat_axis=0, tiled=True
    )
    mine = jnp.sum(jnp.exp(teacher_logits.astype(F32) / 2.0), axis=1)
    teacher_sum = lax.dynamic_update_slice_in_dim(
        jnp.zeros((rows,), F32), mine, vocab * mine.shape[0], 0
    )
    gathered, capped, sums = scores(place, hidden, own, other, head_weight, teacher_sum[None])
    totals = jnp.concatenate([total(sums), jnp.ones((6, rows), F32)])

    which = core[None].astype(jnp.int32)
    delta, give = delta_and_share(which, capped, teacher, totals, head_weight)
    keep = own_share(which, delta, head_weight)
    chip = (keep.astype(F32) + swap(give).astype(F32)).astype(BF)
    parts = lax.all_to_all(chip, CHIPS, split_axis=0, concat_axis=0, tiled=True)
    grad_head = lax.dot_general(
        gathered, delta, (((0,), (0,)), ((), ())), preferred_element_type=F32
    ).astype(BF)
    summed = chip_sum(parts.reshape(64, rows // 64, half), grad_head)
    mine = lax.dynamic_slice_in_dim(summed, core * 8, 8, 0)
    rest = swap(lax.dynamic_slice_in_dim(summed, (1 - core) * 8, 8, 0))
    grad_hidden = jnp.where(
        core == 0, jnp.concatenate([mine, rest], 1), jnp.concatenate([rest, mine], 1)
    )
    return grad_hidden, grad_head


def solution(mesh):
    fine = Mesh(mesh.devices.reshape(2, 4, 4, 2, 2), ("zh", "x", "y", "zl", "core"))
    dp, vocab = ("zh", "x"), ("y", "zl", "core")
    return jax.shard_map(
        per_device,
        mesh=fine,
        in_specs=(P(dp, None), P(None, dp + vocab), P(vocab, dp)),
        out_specs=(P(dp + vocab, None), P(None, dp + vocab)),
        check_vma=False,
    )
```

time: 242 us -> 185 us (0.76)
  waiting for transfers between devices: 115 us -> 57.3 us
  matrix products: 52.9 us -> 13 us
  Pallas kernels: 0 us -> 34.2 us
  starting transfers between devices: 45.3 us -> 60.2 us
  local copies, waits for them, and re-layouts: 18.1 us -> 12.7 us
  other arithmetic: 8.68 us -> 5.8 us
    pallas_call x0 -> x4, Pallas kernels: none -> 34.2 us  [the longest x1 15.7 us: scores(): pl.pallas_call(functools.partial(scores_kernel, tile), name='scores', out...]
    dot_general x2 -> x0, matrix products: 30.7 us -> none  [the longest x1 15.5 us: per_device(): lax.dot_general(delta, head_weight, (((1,), (1,)), ((), ())), preferred_e...]
    all_to_all x1, waiting for transfers between devices: 26.9 us -> 0.01 us  [per_device(): lax.all_to_all(teacher_logits, ('y', 'zl', 'core'), split_axis=1, concat_...]
    ppermute x20 -> x26, waiting for transfers between devices: 42.9 us -> 25.6 us  [shift(): return lax.ppermute(v, axis, [(i, (i + step) % size) for i in range(size)])]
    ppermute x20 -> x26, starting transfers between devices: 34.2 us -> 49.3 us  [shift(): return lax.ppermute(v, axis, [(i, (i + step) % size) for i in range(size)])]
    all_to_all x1, waiting for transfers between devices: 44.8 us -> 31.8 us  [per_device(): parts = lax.all_to_all(chip, CHIPS, split_axis=0, concat_axis=0, tiled=True)]
    dot_general x1, matrix products: 22.2 us -> 13 us  [per_device(): lax.dot_general(gathered, delta, (((0,), (0,)), ((), ())), preferred_elem...]
    dynamic_update_slice x8 -> x1, local copies, waits for them, and re-layouts: 8.82 us -> 0.26 us  [per_device(): lax.dynamic_update_slice_in_dim(jnp.zeros((rows,), F32), mine, vocab * mi...]
  transfers between devices with their start and end apart: 22 -> 28, of which waited for: 12 -> 12; matrix products, arithmetic and copies ran while one was open for 16% -> 10% of each run, Pallas kernels for 0% -> 11%
where the time goes in v2:
time: 185 us; the launch traced here: 184 us
  starting transfers between devices  60.2 us (33%)
  waiting for transfers between devices  57.3 us (31%)
  Pallas kernels  34.2 us (18%)
  matrix products  13 us (7%)
  local copies, waits for them, and re-layouts  12.7 us (7%)
  other arithmetic  5.8 us (3%)
    ppermute x26, starting transfers between devices, shift(): return lax.ppermute(v, axis, [(i, (i + step) % size) for i in range(size)])  49.3 us
    all_to_all x1, waiting for transfers between devices, per_device(): parts = lax.all_to_all(chip, CHIPS, split_axis=0, concat_axis=0, tiled=True)  31.8 us
    ppermute x26, waiting for transfers between devices, shift(): return lax.ppermute(v, axis, [(i, (i + step) % size) for i in range(size)])  25.6 us
    pallas_call x1, Pallas kernels, scores(): pl.pallas_call(functools.partial(scores_kernel, tile), name='scores', out...  15.7 us
    dot_general x1, matrix products, per_device(): lax.dot_general(gathered, delta, (((0,), (0,)), ((), ())), preferred_elem...  13 us
    pallas_call x1, Pallas kernels, delta_and_share(): pl.pallas_call(delta_kernel, name='delta_and_share', grid_spec=pltpu.Pref...  8.62 us
    unnamed x12, local copies, waits for them, and re-layouts  7.29 us
    all_to_all x1, starting transfers between devices, per_device(): parts = lax.all_to_all(chip, CHIPS, split_axis=0, concat_axis=0, tiled=True)  5.74 us
  transfers between devices with their start and end apart: 28, of which 12 were waited for; matrix products, arithmetic and copies ran while one was open for 10% of the time, Pallas kernels for 11%

profile of v2, /device:TPU:1, one launch (start us, length us, event | category | flops | bytes accessed | tf_op | source)
XLA Modules:
  0.0 184.1 jit_solution(2422773427251093603)
XLA Ops:
  1.7 4.5 %collective-permute-start.3 = (bf16[128,1792]{1,0:T(8,128)(2,1)S(1)}, bf16[128,1792]{1,0:T(8,128)(2,1)S(1)}, u32[]{:S(2)}, u32[]{:S(2)}) collective-permute-start(bf16[128,1792]{1,0:T(8,128)(2,1)S(1)} %constant_dynamic-slice_fusion.2), channel_id=1, source_target_pairs={{0,64},{64,0},{1,65},{65,1},{2,66},{66,2},{3,67},{67,3},{4,68},{68... | collective-permute-start | bytes 1376264 | tf_op jit(solution)/shard_map/ppermute | solution.py:20
  7.4 1.5 collective-permute-start.1
  8.9 1.5 collective-permute-start.2
  10.4 6.0 %collective-permute-done.3.refs_3_ = bf16[128,1792]{1,0:T(8,128)(2,1)S(1)} collective-permute-done((bf16[128,1792]{1,0:T(8,128)(2,1)S(1)}, bf16[128,1792]{1,0:T(8,128)(2,1)S(1)}, u32[]{:S(2)}, u32[]{:S(2)}) %collective-permute-start.3) | collective-permute-done | bytes 458784 | tf_op jit(solution)/shard_map/ppermute | solution.py:20
  17.7 1.5 collective-permute-start.5
  19.1 1.5 collective-permute-start.6
  20.7 10.9 %collective-permute-start.7 = (bf16[128,1792]{1,0:T(8,128)(2,1)}, bf16[128,1792]{1,0:T(8,128)(2,1)}, u32[]{:S(2)}, u32[]{:S(2)}) collective-permute-start(bf16[128,1792]{1,0:T(8,128)(2,1)} %collective-permute-done.refs_0_), channel_id=1, source_target_pairs={{0,1},{1,0},{2,3},{3,2},{4,5},{5,4},{6,7},{7,6},{8,9},{9,8},{10,11... | collective-permute-start | bytes 1376264 | tf_op jit(solution)/shard_map/ppermute | solution.py:20
  32.8 3.2 %copy.8 = bf16[8,16,8,1024]{3,2,0,1:T(8,128)(2,1)} copy(bf16[8,16,8,1024]{3,2,1,0:T(8,128)(2,1)} %bitcast.22) | data formatting | bytes 4194304 | tf_op jit(solution)/shard_map/all_to_all | solution.py:226
  36.0 5.2 %all-to-all-start = ((bf16[64,16,1024]{2,0,1:T(8,128)(2,1)}), bf16[64,16,1024]{2,0,1:T(8,128)(2,1)S(1)}, u32[]{:S(2)}, u32[]{:S(2)}) async-start(bf16[64,16,1024]{2,0,1:T(8,128)(2,1)} %bitcast.23), calls=%async_computation | async-start | bytes 4194304 | tf_op jit(solution)/shard_map/all_to_all | solution.py:226
  41.9 7.2 %collective-permute-done.6.refs_6_ = bf16[128,1792]{1,0:T(8,128)(2,1)} collective-permute-done((bf16[128,1792]{1,0:T(8,128)(2,1)S(1)}, bf16[128,1792]{1,0:T(8,128)(2,1)}, u32[]{:S(2)}, u32[]{:S(2)}) %collective-permute-start.6) | collective-permute-done | bytes 458784 | tf_op jit(solution)/shard_map/ppermute | solution.py:20
  49.1 1.9 %collective-permute-start.11 = (bf16[128,1792]{1,0:T(8,128)(2,1)}, bf16[128,1792]{1,0:T(8,128)(2,1)}, u32[]{:S(2)}, u32[]{:S(2)}) collective-permute-start(bf16[128,1792]{1,0:T(8,128)(2,1)} %collective-permute-done.4.refs_4_), channel_id=1, source_target_pairs={{0,1},{1,0},{2,3},{3,2},{4,5},{5,4},{6,7},{7,6},{8,9},{9,8},{10,11... | collective-permute-start | bytes 1376264 | tf_op jit(solution)/shard_map/ppermute | solution.py:20
  51.5 2.4 %exponential_reduce_fusion = f32[64]{0:T(128)S(1)} fusion(bf16[64,16384]{1,0:T(8,128)(2,1)} %param.5), kind=kLoop, calls=%fused_computation.2 | loop fusion | flops 3145664 | bytes 2097408 | tf_op jit(solution)/shard_map/reduce_sum | solution.py:229
  54.3 15.7 %scores.1 = (bf16[1024,3584]{1,0:T(8,128)(2,1)}, f32[1024,1024]{1,0:T(8,128)S(1)}, f32[2,1024]{1,0:T(2,128)S(1)}) custom-call(s32[9]{0:T(128)S(1)} %stack.36.place, bf16[128,3584]{1,0:T(8,128)(2,1)S(1)} %copy-done, bf16[128,1792]{1,0:T(8,128)(2,1)} %collective-permute-done.refs_0_, bf16[128,1792]{1,0:T(8,128)(2,1)} %collective-permute-done.1.refs_1_, ...), custom_call_target="tpu_custom_call" | custom-call | flops 7516192768 | bytes 20971520 | tf_op jit(solution)/shard_map/scores/pallas_call | solution.py:93
  70.0 2.0 %copy-done.2 = f32[1024,1024]{1,0:T(8,128)} copy-done((f32[1024,1024]{1,0:T(8,128)}, f32[1024,1024]{1,0:T(8,128)S(1)}, u32[]{:S(2)}) %copy-start.2) | copy-done | bytes 4194328
  73.7 2.7 %collective-permute-start.16 = (f32[2,1024]{1,0:T(2,128)S(1)}, f32[2,1024]{1,0:T(2,128)S(1)}, u32[]{:S(2)}, u32[]{:S(2)}) collective-permute-start(f32[2,1024]{1,0:T(2,128)S(1)} %add.113), channel_id=1, source_target_pairs={{0,48},{16,0},{32,16},{48,32},{1,49},{17,1},{33,17},{49,33},{2,50}... | collective-permute-start | bytes 24584 | tf_op jit(solution)/shard_map/ppermute | solution.py:20
  77.3 2.9 %collective-permute-done.15 = f32[2,1024]{1,0:T(2,128)S(1)} collective-permute-done((f32[2,1024]{1,0:T(2,128)S(1)}, f32[2,1024]{1,0:T(2,128)S(1)}, u32[]{:S(2)}, u32[]{:S(2)}) %collective-permute-start.15) | collective-permute-done | bytes 8224 | tf_op jit(solution)/shard_map/ppermute | solution.py:20
  80.1 3.0 %collective-permute-start.20 = (f32[2,1024]{1,0:T(2,128)S(1)}, f32[2,1024]{1,0:T(2,128)S(1)}, u32[]{:S(2)}, u32[]{:S(2)}) collective-permute-start(f32[2,1024]{1,0:T(2,128)S(1)} %add_add_fusion.2), channel_id=1, source_target_pairs={{0,8},{4,12},{8,0},{12,4},{1,9},{5,13},{9,1},{13,5},{2,10},{6,14},... | collective-permute-start | bytes 24584 | tf_op jit(solution)/shard_map/ppermute | solution.py:20
  84.6 1.3 collective-permute-done.19
  85.9 1.7 collective-permute-done.18
  87.8 3.0 %collective-permute-start.22 = (f32[2,1024]{1,0:T(2,128)S(1)}, f32[2,1024]{1,0:T(2,128)S(1)}, u32[]{:S(2)}, u32[]{:S(2)}) collective-permute-start(f32[2,1024]{1,0:T(2,128)S(1)} %add_add_fusion.1), channel_id=1, source_target_pairs={{0,66},{2,0},{64,2},{66,64},{1,67},{3,1},{65,3},{67,65},{4,70},{6,... | collective-permute-start | bytes 24584 | tf_op jit(solution)/shard_map/ppermute | solution.py:20
  91.7 2.8 %collective-permute-done.21 = f32[2,1024]{1,0:T(2,128)S(1)} collective-permute-done((f32[2,1024]{1,0:T(2,128)S(1)}, f32[2,1024]{1,0:T(2,128)S(1)}, u32[]{:S(2)}, u32[]{:S(2)}) %collective-permute-start.21) | collective-permute-done | bytes 8224 | tf_op jit(solution)/shard_map/ppermute | solution.py:20
  94.6 2.2 %copy-done.3 = f32[1024,1024]{1,0:T(8,128)S(1)} copy-done((f32[1024,1024]{1,0:T(8,128)S(1)}, f32[1024,1024]{1,0:T(8,128)}, u32[]{:S(2)}) %copy-start.3) | copy-done | bytes 4194328
  96.8 8.6 %delta_and_share.1 = (bf16[1024,1024]{1,0:T(8,128)(2,1)S(1)}, bf16[1024,1792]{1,0:T(8,128)(2,1)S(1)}) custom-call(s32[1]{0:T(128)} %bitcast.core, f32[1024,1024]{1,0:T(8,128)S(1)} %copy-done.3, bf16[1024,1024]{1,0:T(8,128)(2,1)S(1)} %bitcast.20, f32[8,1024]{1,0:T(8,128)S(1)} %concatenate.9.totals, bf16[3584,1024]{1,0:T(8,128)(2,1)} %weight.3), custom_call_target="tpu_custom_call" | custom-call | flops 3758096384 | bytes 16777216 | tf_op jit(solution)/shard_map/delta_and_share/pallas_call | solution.py:135
  105.4 5.4 %collective-permute-start.24 = (bf16[1024,1792]{1,0:T(8,128)(2,1)S(1)}, bf16[1024,1792]{1,0:T(8,128)(2,1)S(1)}, u32[]{:S(2)}, u32[]{:S(2)}) collective-permute-start(bf16[1024,1792]{1,0:T(8,128)(2,1)S(1)} %get-tuple-element.10), channel_id=1, source_target_pairs={{0,1},{1,0},{2,3},{3,2},{4,5},{5,4},{6,7},{7,6},{8,9},{9,8},{10,11... | collective-permute-start | bytes 11010056 | tf_op jit(solution)/shard_map/ppermute | solution.py:20
  110.8 3.1 %copy-done.1 = bf16[3584,1024]{1,0:T(8,128)(2,1)S(1)} copy-done((bf16[3584,1024]{1,0:T(8,128)(2,1)S(1)}, bf16[3584,1024]{1,0:T(8,128)(2,1)}, u32[]{:S(2)}) %copy-start.1) | copy-done | bytes 7340056
  113.9 4.7 %own_share.1 = bf16[1024,1792]{1,0:T(8,128)(2,1)S(1)} custom-call(s32[1]{0:T(128)} %bitcast.core, bf16[1024,1024]{1,0:T(8,128)(2,1)S(1)} %get-tuple-element.9.delta, bf16[3584,1024]{1,0:T(8,128)(2,1)S(1)} %copy-done.1), custom_call_target="tpu_custom_call" | custom-call | flops 3758096384 | bytes 10485760 | tf_op jit(solution)/shard_map/own_share/pallas_call | solution.py:171
  118.6 2.8 %add_convert_fusion = bf16[1024,1792]{1,0:T(8,128)(2,1)} fusion(bf16[1024,1792]{1,0:T(8,128)(2,1)S(1)} %collective-permute-done.24, bf16[1024,1792]{1,0:T(8,128)(2,1)S(1)} %own_share.1), kind=kLoop, calls=%fused_computation.1 | loop fusion | flops 7340032 | bytes 11010048 | tf_op jit(solution)/shard_map/convert_element_type | solution.py:239
  121.3 5.7 %all-to-all-start.1 = ((bf16[64,16,1792]{2,1,0:T(8,128)(2,1)}), bf16[64,16,1792]{2,1,0:T(8,128)(2,1)}, u32[]{:S(2)}, u32[]{:S(2)}) async-start(bf16[64,16,1792]{2,1,0:T(8,128)(2,1)} %bitcast.21), calls=%async_computation.1 | async-start | bytes 7340032 | tf_op jit(solution)/shard_map/all_to_all | solution.py:240
  127.1 13.0 %convolution_convert_fusion.after = bf16[3584,1024]{1,0:T(8,128)(2,1)} fusion(bf16[1024,3584]{1,0:T(8,128)(2,1)} %get-tuple-element.11, bf16[1024,1024]{1,0:T(8,128)(2,1)S(1)} %copy-done.5), kind=kOutput, calls=%fused_computation | convolution fusion | flops 7519862784 | bytes 16777216 | tf_op jit(solution)/shard_map/dot_general | solution.py:241
  140.1 31.8 %all-to-all-done.1.parts = bf16[64,16,1792]{2,1,0:T(8,128)(2,1)} async-done(((bf16[64,16,1792]{2,1,0:T(8,128)(2,1)}), bf16[64,16,1792]{2,1,0:T(8,128)(2,1)}, u32[]{:S(2)}, u32[]{:S(2)}) %all-to-all-start.1) | async-done | bytes 3670048 | tf_op jit(solution)/shard_map/all_to_all | solution.py:240
  171.8 5.3 %chip_sum.1 = bf16[16,1792]{1,0:T(8,128)(2,1)} custom-call(bf16[64,16,1792]{2,1,0:T(8,128)(2,1)} %all-to-all-done.1.parts, bf16[3584,1024]{1,0:T(8,128)(2,1)} %convolution_convert_fusion.after), custom_call_target="tpu_custom_call" | custom-call | flops 1835008 | bytes 4194304 | tf_op jit(solution)/shard_map/chip_sum/pallas_call | solution.py:198
  177.9 4.7 %collective-permute-start.25 = (bf16[8,1792]{1,0:T(8,128)(2,1)S(1)}, bf16[8,1792]{1,0:T(8,128)(2,1)S(1)}, u32[]{:S(2)}, u32[]{:S(2)}) collective-permute-start(bf16[8,1792]{1,0:T(8,128)(2,1)S(1)} %get-tuple-element.13), channel_id=1, source_target_pairs={{0,1},{1,0},{2,3},{3,2},{4,5},{5,4},{6,7},{7,6},{8,9},{9,8},{10,11... | collective-permute-start | bytes 86024 | tf_op jit(solution)/shard_map/ppermute | solution.py:20
  (55 shorter events, 13.7 us)
Async XLA Ops:
  1.7 14.8 %collective-permute-start.3 = (bf16[128,1792]{1,0:T(8,128)(2,1)S(1)}, bf16[128,1792]{1,0:T(8,128)(2,1)S(1)}, u32[]{:S(2)}, u32[]{:S(2)}) collective-permute-start(bf16[128,1792]{1,0:T(8,128)(2,1)S(1)} %constant_dynamic-slice_fusion.2), channel_id=1, source_target_pairs={{0,64},{64,0},{1,65},{65,1},{2,66},{66,2},{3,67},{67,3},{4,68},{68... | collective-permute-start | bytes 1376264 | tf_op jit(solution)/shard_map/ppermute | solution.py:20
  6.2 12.9 %collective-permute-start = (bf16[128,1792]{1,0:T(8,128)(2,1)S(1)}, bf16[128,1792]{1,0:T(8,128)(2,1)}, u32[]{:S(2)}, u32[]{:S(2)}) collective-permute-start(bf16[128,1792]{1,0:T(8,128)(2,1)S(1)} %constant_dynamic-slice_fusion.2), channel_id=1, source_target_pairs={{0,16},{16,32},{32,48},{48,0},{1,17},{17,33},{33,49},{49,1},{2,18}... | collective-permute-start | bytes 1376264 | tf_op jit(solution)/shard_map/ppermute | solution.py:20
  7.4 13.3 %collective-permute-start.1 = (bf16[128,1792]{1,0:T(8,128)(2,1)S(1)}, bf16[128,1792]{1,0:T(8,128)(2,1)}, u32[]{:S(2)}, u32[]{:S(2)}) collective-permute-start(bf16[128,1792]{1,0:T(8,128)(2,1)S(1)} %constant_dynamic-slice_fusion.2), channel_id=1, source_target_pairs={{0,48},{16,0},{32,16},{48,32},{1,49},{17,1},{33,17},{49,33},{2,50}... | collective-permute-start | bytes 1376264 | tf_op jit(solution)/shard_map/ppermute | solution.py:20
  8.9 22.7 %collective-permute-start.2 = (bf16[128,1792]{1,0:T(8,128)(2,1)S(1)}, bf16[128,1792]{1,0:T(8,128)(2,1)}, u32[]{:S(2)}, u32[]{:S(2)}) collective-permute-start(bf16[128,1792]{1,0:T(8,128)(2,1)S(1)} %constant_dynamic-slice_fusion.2), channel_id=1, source_target_pairs={{0,32},{16,48},{32,0},{48,16},{1,33},{17,49},{33,1},{49,17},{2,34}... | collective-permute-start | bytes 1376264 | tf_op jit(solution)/shard_map/ppermute | solution.py:20
  16.4 24.8 %collective-permute-start.4 = (bf16[128,1792]{1,0:T(8,128)(2,1)S(1)}, bf16[128,1792]{1,0:T(8,128)(2,1)}, u32[]{:S(2)}, u32[]{:S(2)}) collective-permute-start(bf16[128,1792]{1,0:T(8,128)(2,1)S(1)} %collective-permute-done.3.refs_3_), channel_id=1, source_target_pairs={{0,16},{16,32},{32,48},{48,0},{1,17},{17,33},{33,49},{49,1},{2,18}... | collective-permute-start | bytes 1376264 | tf_op jit(solution)/shard_map/ppermute | solution.py:20
  17.7 23.7 %collective-permute-start.5 = (bf16[128,1792]{1,0:T(8,128)(2,1)S(1)}, bf16[128,1792]{1,0:T(8,128)(2,1)}, u32[]{:S(2)}, u32[]{:S(2)}) collective-permute-start(bf16[128,1792]{1,0:T(8,128)(2,1)S(1)} %collective-permute-done.3.refs_3_), channel_id=1, source_target_pairs={{0,48},{16,0},{32,16},{48,32},{1,49},{17,1},{33,17},{49,33},{2,50}... | collective-permute-start | bytes 1376264 | tf_op jit(solution)/shard_map/ppermute | solution.py:20
  19.1 30.0 %collective-permute-start.6 = (bf16[128,1792]{1,0:T(8,128)(2,1)S(1)}, bf16[128,1792]{1,0:T(8,128)(2,1)}, u32[]{:S(2)}, u32[]{:S(2)}) collective-permute-start(bf16[128,1792]{1,0:T(8,128)(2,1)S(1)} %collective-permute-done.3.refs_3_), channel_id=1, source_target_pairs={{0,32},{16,48},{32,0},{48,16},{1,33},{17,49},{33,1},{49,17},{2,34}... | collective-permute-start | bytes 1376264 | tf_op jit(solution)/shard_map/ppermute | solution.py:20
  20.7 30.3 %collective-permute-start.7 = (bf16[128,1792]{1,0:T(8,128)(2,1)}, bf16[128,1792]{1,0:T(8,128)(2,1)}, u32[]{:S(2)}, u32[]{:S(2)}) collective-permute-start(bf16[128,1792]{1,0:T(8,128)(2,1)} %collective-permute-done.refs_0_), channel_id=1, source_target_pairs={{0,1},{1,0},{2,3},{3,2},{4,5},{5,4},{6,7},{7,6},{8,9},{9,8},{10,11... | collective-permute-start | bytes 1376264 | tf_op jit(solution)/shard_map/ppermute | solution.py:20
  31.6 19.4 %collective-permute-start.8 = (bf16[128,1792]{1,0:T(8,128)(2,1)}, bf16[128,1792]{1,0:T(8,128)(2,1)}, u32[]{:S(2)}, u32[]{:S(2)}) collective-permute-start(bf16[128,1792]{1,0:T(8,128)(2,1)} %collective-permute-done.1.refs_1_), channel_id=1, source_target_pairs={{0,1},{1,0},{2,3},{3,2},{4,5},{5,4},{6,7},{7,6},{8,9},{9,8},{10,11... | collective-permute-start | bytes 1376264 | tf_op jit(solution)/shard_map/ppermute | solution.py:20
  36.0 18.3 %copy-start = (bf16[128,3584]{1,0:T(8,128)(2,1)S(1)}, bf16[128,3584]{1,0:T(8,128)(2,1)}, u32[]{:S(2)}) copy-start(bf16[128,3584]{1,0:T(8,128)(2,1)} %hidden.1) | copy-start | bytes 2752516
  36.0 58.6 %all-to-all-start = ((bf16[64,16,1024]{2,0,1:T(8,128)(2,1)}), bf16[64,16,1024]{2,0,1:T(8,128)(2,1)S(1)}, u32[]{:S(2)}, u32[]{:S(2)}) async-start(bf16[64,16,1024]{2,0,1:T(8,128)(2,1)} %bitcast.23), calls=%async_computation | async-start | bytes 4194304 | tf_op jit(solution)/shard_map/all_to_all | solution.py:226
  41.2 13.0 %collective-permute-start.10 = (bf16[128,1792]{1,0:T(8,128)(2,1)S(1)}, bf16[128,1792]{1,0:T(8,128)(2,1)}, u32[]{:S(2)}, u32[]{:S(2)}) collective-permute-start(bf16[128,1792]{1,0:T(8,128)(2,1)S(1)} %collective-permute-done.3.refs_3_), channel_id=1, source_target_pairs={{0,1},{1,0},{2,3},{3,2},{4,5},{5,4},{6,7},{7,6},{8,9},{9,8},{10,11... | collective-permute-start | bytes 1376264 | tf_op jit(solution)/shard_map/ppermute | solution.py:20
  41.4 12.8 %collective-permute-start.9 = (bf16[128,1792]{1,0:T(8,128)(2,1)}, bf16[128,1792]{1,0:T(8,128)(2,1)}, u32[]{:S(2)}, u32[]{:S(2)}) collective-permute-start(bf16[128,1792]{1,0:T(8,128)(2,1)} %collective-permute-done.2.refs_2_), channel_id=1, source_target_pairs={{0,1},{1,0},{2,3},{3,2},{4,5},{5,4},{6,7},{7,6},{8,9},{9,8},{10,11... | collective-permute-start | bytes 1376264 | tf_op jit(solution)/shard_map/ppermute | solution.py:20
  49.1 5.1 %collective-permute-start.11 = (bf16[128,1792]{1,0:T(8,128)(2,1)}, bf16[128,1792]{1,0:T(8,128)(2,1)}, u32[]{:S(2)}, u32[]{:S(2)}) collective-permute-start(bf16[128,1792]{1,0:T(8,128)(2,1)} %collective-permute-done.4.refs_4_), channel_id=1, source_target_pairs={{0,1},{1,0},{2,3},{3,2},{4,5},{5,4},{6,7},{7,6},{8,9},{9,8},{10,11... | collective-permute-start | bytes 1376264 | tf_op jit(solution)/shard_map/ppermute | solution.py:20
  51.0 3.3 %collective-permute-start.12 = (bf16[128,1792]{1,0:T(8,128)(2,1)}, bf16[128,1792]{1,0:T(8,128)(2,1)}, u32[]{:S(2)}, u32[]{:S(2)}) collective-permute-start(bf16[128,1792]{1,0:T(8,128)(2,1)} %collective-permute-done.5.refs_5_), channel_id=1, source_target_pairs={{0,1},{1,0},{2,3},{3,2},{4,5},{5,4},{6,7},{7,6},{8,9},{9,8},{10,11... | collective-permute-start | bytes 1376264 | tf_op jit(solution)/shard_map/ppermute | solution.py:20
  51.0 3.3 %collective-permute-start.13 = (bf16[128,1792]{1,0:T(8,128)(2,1)}, bf16[128,1792]{1,0:T(8,128)(2,1)}, u32[]{:S(2)}, u32[]{:S(2)}) collective-permute-start(bf16[128,1792]{1,0:T(8,128)(2,1)} %collective-permute-done.6.refs_6_), channel_id=1, source_target_pairs={{0,1},{1,0},{2,3},{3,2},{4,5},{5,4},{6,7},{7,6},{8,9},{9,8},{10,11... | collective-permute-start | bytes 1376264 | tf_op jit(solution)/shard_map/ppermute | solution.py:20
  72.0 1.2 collective-permute-start.14
  73.2 4.0 %collective-permute-start.17 = (f32[2,1024]{1,0:T(2,128)S(1)}, f32[2,1024]{1,0:T(2,128)S(1)}, u32[]{:S(2)}, u32[]{:S(2)}) collective-permute-start(f32[2,1024]{1,0:T(2,128)S(1)} %add.113), channel_id=1, source_target_pairs={{0,32},{16,48},{32,0},{48,16},{1,33},{17,49},{33,1},{49,17},{2,34}... | collective-permute-start | bytes 24584 | tf_op jit(solution)/shard_map/ppermute | solution.py:20
  73.7 3.6 %collective-permute-start.16 = (f32[2,1024]{1,0:T(2,128)S(1)}, f32[2,1024]{1,0:T(2,128)S(1)}, u32[]{:S(2)}, u32[]{:S(2)}) collective-permute-start(f32[2,1024]{1,0:T(2,128)S(1)} %add.113), channel_id=1, source_target_pairs={{0,48},{16,0},{32,16},{48,32},{1,49},{17,1},{33,17},{49,33},{2,50}... | collective-permute-start | bytes 24584 | tf_op jit(solution)/shard_map/ppermute | solution.py:20
  76.4 3.7 %collective-permute-start.15 = (f32[2,1024]{1,0:T(2,128)S(1)}, f32[2,1024]{1,0:T(2,128)S(1)}, u32[]{:S(2)}, u32[]{:S(2)}) collective-permute-start(f32[2,1024]{1,0:T(2,128)S(1)} %add.113), channel_id=1, source_target_pairs={{0,16},{16,32},{32,48},{48,0},{1,17},{17,33},{33,49},{49,1},{2,18}... | collective-permute-start | bytes 24584 | tf_op jit(solution)/shard_map/ppermute | solution.py:20
  80.1 4.5 %collective-permute-start.20 = (f32[2,1024]{1,0:T(2,128)S(1)}, f32[2,1024]{1,0:T(2,128)S(1)}, u32[]{:S(2)}, u32[]{:S(2)}) collective-permute-start(f32[2,1024]{1,0:T(2,128)S(1)} %add_add_fusion.2), channel_id=1, source_target_pairs={{0,8},{4,12},{8,0},{12,4},{1,9},{5,13},{9,1},{13,5},{2,10},{6,14},... | collective-permute-start | bytes 24584 | tf_op jit(solution)/shard_map/ppermute | solution.py:20
  83.1 2.8 %collective-permute-start.19 = (f32[2,1024]{1,0:T(2,128)S(1)}, f32[2,1024]{1,0:T(2,128)S(1)}, u32[]{:S(2)}, u32[]{:S(2)}) collective-permute-start(f32[2,1024]{1,0:T(2,128)S(1)} %add_add_fusion.2), channel_id=1, source_target_pairs={{0,12},{4,0},{8,4},{12,8},{1,13},{5,1},{9,5},{13,9},{2,14},{6,2},{... | collective-permute-start | bytes 24584 | tf_op jit(solution)/shard_map/ppermute | solution.py:20
  83.9 3.7 %collective-permute-start.18 = (f32[2,1024]{1,0:T(2,128)S(1)}, f32[2,1024]{1,0:T(2,128)S(1)}, u32[]{:S(2)}, u32[]{:S(2)}) collective-permute-start(f32[2,1024]{1,0:T(2,128)S(1)} %add_add_fusion.2), channel_id=1, source_target_pairs={{0,4},{4,8},{8,12},{12,0},{1,5},{5,9},{9,13},{13,1},{2,6},{6,10},{... | collective-permute-start | bytes 24584 | tf_op jit(solution)/shard_map/ppermute | solution.py:20
  87.6 4.1 %collective-permute-start.23 = (f32[2,1024]{1,0:T(2,128)S(1)}, f32[2,1024]{1,0:T(2,128)S(1)}, u32[]{:S(2)}, u32[]{:S(2)}) collective-permute-start(f32[2,1024]{1,0:T(2,128)S(1)} %add_add_fusion.1), channel_id=1, source_target_pairs={{0,64},{2,66},{64,0},{66,2},{1,65},{3,67},{65,1},{67,3},{4,68},{6,... | collective-permute-start | bytes 24584 | tf_op jit(solution)/shard_map/ppermute | solution.py:20
  87.8 3.9 %collective-permute-start.22 = (f32[2,1024]{1,0:T(2,128)S(1)}, f32[2,1024]{1,0:T(2,128)S(1)}, u32[]{:S(2)}, u32[]{:S(2)}) collective-permute-start(f32[2,1024]{1,0:T(2,128)S(1)} %add_add_fusion.1), channel_id=1, source_target_pairs={{0,66},{2,0},{64,2},{66,64},{1,67},{3,1},{65,3},{67,65},{4,70},{6,... | collective-permute-start | bytes 24584 | tf_op jit(solution)/shard_map/ppermute | solution.py:20
  90.8 3.7 %collective-permute-start.21 = (f32[2,1024]{1,0:T(2,128)S(1)}, f32[2,1024]{1,0:T(2,128)S(1)}, u32[]{:S(2)}, u32[]{:S(2)}) collective-permute-start(f32[2,1024]{1,0:T(2,128)S(1)} %add_add_fusion.1), channel_id=1, source_target_pairs={{0,2},{2,64},{64,66},{66,0},{1,3},{3,65},{65,67},{67,1},{4,6},{6,6... | collective-permute-start | bytes 24584 | tf_op jit(solution)/shard_map/ppermute | solution.py:20
  105.4 13.1 %copy-start.4 = (bf16[1024,1024]{1,0:T(8,128)(2,1)}, bf16[1024,1024]{1,0:T(8,128)(2,1)S(1)}, u32[]{:S(2)}) copy-start(bf16[1024,1024]{1,0:T(8,128)(2,1)S(1)} %get-tuple-element.9.delta) | copy-start | bytes 6291460
  105.4 13.1 %collective-permute-start.24 = (bf16[1024,1792]{1,0:T(8,128)(2,1)S(1)}, bf16[1024,1792]{1,0:T(8,128)(2,1)S(1)}, u32[]{:S(2)}, u32[]{:S(2)}) collective-permute-start(bf16[1024,1792]{1,0:T(8,128)(2,1)S(1)} %get-tuple-element.10), channel_id=1, source_target_pairs={{0,1},{1,0},{2,3},{3,2},{4,5},{5,4},{6,7},{7,6},{8,9},{9,8},{10,11... | collective-permute-start | bytes 11010056 | tf_op jit(solution)/shard_map/ppermute | solution.py:20
  110.8 3.1 %copy-start.1 = (bf16[3584,1024]{1,0:T(8,128)(2,1)S(1)}, bf16[3584,1024]{1,0:T(8,128)(2,1)}, u32[]{:S(2)}) copy-start(bf16[3584,1024]{1,0:T(8,128)(2,1)} %weight.3) | copy-start | bytes 22020100
  121.3 5.8 %copy-start.5 = (bf16[1024,1024]{1,0:T(8,128)(2,1)S(1)}, bf16[1024,1024]{1,0:T(8,128)(2,1)}, u32[]{:S(2)}) copy-start(bf16[1024,1024]{1,0:T(8,128)(2,1)} %copy-done.4) | copy-start | bytes 6291460
  121.3 50.5 %all-to-all-start.1 = ((bf16[64,16,1792]{2,1,0:T(8,128)(2,1)}), bf16[64,16,1792]{2,1,0:T(8,128)(2,1)}, u32[]{:S(2)}, u32[]{:S(2)}) async-start(bf16[64,16,1792]{2,1,0:T(8,128)(2,1)} %bitcast.21), calls=%async_computation.1 | async-start | bytes 7340032 | tf_op jit(solution)/shard_map/all_to_all | solution.py:240
  177.9 5.6 %collective-permute-start.25 = (bf16[8,1792]{1,0:T(8,128)(2,1)S(1)}, bf16[8,1792]{1,0:T(8,128)(2,1)S(1)}, u32[]{:S(2)}, u32[]{:S(2)}) collective-permute-start(bf16[8,1792]{1,0:T(8,128)(2,1)S(1)} %get-tuple-element.13), channel_id=1, source_target_pairs={{0,1},{1,0},{2,3},{3,2},{4,5},{5,4},{6,7},{7,6},{8,9},{9,8},{10,11... | collective-permute-start | bytes 86024 | tf_op jit(solution)/shard_map/ppermute | solution.py:20
  (2 other events, 4.2 us)

commit v3 on v2

--- a/solution.py
+++ b/solution.py
@@ -11,6 +11,7 @@
 F32 = jnp.float32
 CHIPS = ("zh", "x", "y", "zl")
 Z = ("zh", "zl")
+VMEM_BYTES = 60 << 20
 SMEM = pl.BlockSpec(memory_space=pltpu.SMEM)
 VMEM = pl.BlockSpec(memory_space=pltpu.VMEM)
 ANY = pl.BlockSpec(memory_space=pl.ANY)
@@ -31,39 +32,47 @@
     return v
 
 
+def left_kernel(block, *refs):
+    refs[-1][...] = block[:, : refs[-1].shape[1]]
+
+
+def left_columns(block, cols, *after):
+    return pl.pallas_call(
+        left_kernel,
+        name="left_columns",
+        in_specs=[VMEM] + [ANY] * len(after),
+        out_specs=VMEM,
+        out_shape=jax.ShapeDtypeStruct((block.shape[0], cols), BF),
+        cost_estimate=pl.CostEstimate(flops=0, bytes_accessed=1 << 20, transcendentals=0),
+    )(block, *after)
+
+
 def scores_kernel(tile, place, hidden, *refs):
-    blocks, (weight, teacher_sum, gathered, capped, sums) = refs[:14], refs[14:19]
-    rows_v, weight_v, capped_v, part, row_sem, weight_sem, out_sem, capped_sem = refs[19:]
-    rows, half = blocks[0].shape
-    own = pl.multiple_of(place[8] * half, half)
-    other = pl.multiple_of((1 - place[8]) * half, half)
-    loads = []
-    for i in range(8):
-        at = pl.ds(pl.multiple_of(place[i] * rows, rows), rows)
-        if i == 0:
-            loads.append((hidden, rows_v.at[at, :]))
-        else:
-            loads.append((blocks[i - 1], rows_v.at[at, pl.ds(own, half)]))
-            loads.append((blocks[i + 6], rows_v.at[at, pl.ds(other, half)]))
+    own, other, (weight, teacher_sum, gathered, capped, sums) = refs[:10], refs[10:20], refs[20:25]
+    rows_v, weight_v, capped_v, part, row_sem, weight_sem, out_sem, capped_sem = refs[25:]
+    rows, half = own[0].shape
+    loads = [(hidden, rows_v.at[pl.ds(pl.multiple_of(place[0] * rows, rows), rows), :])]
+    for side, blocks in ((place[8], own), (1 - place[8], other)):
+        for i, block in enumerate(blocks):
+            at = pl.multiple_of(place[i + 1 if i < 7 else i - 2] * rows, rows)
+            left = half - block.shape[1] if i > 6 else 0
+            left = pl.multiple_of(side * half + left, 128)
+            loads.append((block, rows_v.at[pl.ds(at, rows), pl.ds(left, block.shape[1])]))
     loads = [pltpu.make_async_copy(a, b, row_sem.at[i]) for i, (a, b) in enumerate(loads)]
-    count = weight.shape[1] // tile
-    cols = [slice(n * tile, (n + 1) * tile) for n in range(count)]
+    cols = [slice(n * tile, (n + 1) * tile) for n in range(weight.shape[1] // tile)]
     weights = [
         pltpu.make_async_copy(weight.at[:, c], weight_v.at[:, c], weight_sem.at[n])
         for n, c in enumerate(cols)
     ]
-    weights[0].start()
-    for c in loads:
-        c.start()
-    for c in weights[1:]:
+    for c in weights[:1] + loads:
         c.start()
     for c in loads:
         c.wait()
-    keep = pltpu.make_async_copy(rows_v, gathered, out_sem)
-    keep.start()
+    keeps = [pltpu.make_async_copy(rows_v, gathered, out_sem)]
     part[...] = jnp.zeros_like(part)
-    stores = []
     for n, c in enumerate(cols):
+        if n + 1 < len(cols):
+            weights[n + 1].start()
         weights[n].wait()
 
         @pl.loop(0, rows_v.shape[0] // 512)
@@ -78,18 +87,21 @@
                 s = s + e[:, k * 128 : (k + 1) * 128]
             part[at, :] = s
 
-        stores.append(
+        keeps.append(
             pltpu.make_async_copy(capped_v.at[:, c], capped.at[:, c], capped_sem.at[n])
         )
-        stores[-1].start()
+        keeps[-1].start()
+        if n == 0:
+            keeps[0].start()
     sums[0:1, :] = jnp.sum(part[...].T, axis=0, keepdims=True)
     sums[1:2, :] = teacher_sum[...]
-    for c in stores + [keep]:
+    for c in keeps:
         c.wait()
 
 
 def scores(place, hidden, own, other, weight, teacher_sum):
-    rows, depth, cols, tile = 8 * hidden.shape[0], *weight.shape, 256
+    (depth, cols), tile = weight.shape, 256
+    rows = 8 * hidden.shape[0]
     return pl.pallas_call(
         functools.partial(scores_kernel, tile),
         name="scores",
@@ -98,19 +110,19 @@
             jax.ShapeDtypeStruct((rows, cols), F32),
             jax.ShapeDtypeStruct((2, rows), F32),
         ),
-        in_specs=[SMEM, ANY] + [ANY] * 14 + [ANY, VMEM],
+        in_specs=[SMEM] + [ANY] * 22 + [VMEM],
         out_specs=(ANY, ANY, VMEM),
         scratch_shapes=[
             pltpu.VMEM((rows, depth), BF),
             pltpu.VMEM((depth, cols), BF),
             pltpu.VMEM((rows, cols), F32),
             pltpu.VMEM((rows, 128), F32),
-            pltpu.SemaphoreType.DMA((15,)),
+            pltpu.SemaphoreType.DMA((21,)),
             pltpu.SemaphoreType.DMA((cols // tile,)),
             pltpu.SemaphoreType.DMA,
             pltpu.SemaphoreType.DMA((cols // tile,)),
         ],
-        compiler_params=pltpu.CompilerParams(vmem_limit_bytes=40 << 20),
+        compiler_params=pltpu.CompilerParams(vmem_limit_bytes=VMEM_BYTES),
         cost_estimate=pl.CostEstimate(
             flops=2 * rows * depth * cols, bytes_accessed=20 << 20, transcendentals=2 * rows * cols
         ),
@@ -188,22 +200,39 @@
     )(core, delta, weight)
 
 
-def chip_sum_kernel(parts, after, out):
-    out[...] = jnp.sum(parts[...].astype(F32), axis=0).astype(BF)
-
-
-def chip_sum(parts, after):
-    _, rows, cols = parts.shape
-    tile = 256
+def chip_sum_kernel(core, parts, after, mine, rest, total):
+    i = pl.program_id(0)
+    now = jnp.sum(parts[...].astype(F32), axis=0)
+
+    @pl.when(i == 0)
+    def _():
+        total[...] = now
+
+    @pl.when(i > 0)
+    def _():
+        total[...] += now
+
+    @pl.when(i == pl.num_programs(0) - 1)
+    def _():
+        low, high = total[:8, :], total[8:, :]
+        mine[...] = jnp.where(core[0] == 0, low, high).astype(BF)
+        rest[...] = jnp.where(core[0] == 0, high, low).astype(BF)
+
+
+def chip_sum(core, parts, after):
+    count, rows, cols = parts.shape
+    out = pl.BlockSpec((rows // 2, cols), lambda i: (0, 0))
     return pl.pallas_call(
         chip_sum_kernel,
         name="chip_sum",
-        grid=(cols // tile,),
-        in_specs=[pl.BlockSpec((parts.shape[0], rows, tile), lambda i: (0, 0, i)), ANY],
-        out_specs=pl.BlockSpec((rows, tile), lambda i: (0, i)),
-        out_shape=jax.ShapeDtypeStruct((rows, cols), BF),
+        grid=(4,),
+        in_specs=[SMEM, pl.BlockSpec((count // 4, rows, cols), lambda i: (i, 0, 0)), ANY],
+        out_specs=(out, out),
+        out_shape=[jax.ShapeDtypeStruct((rows // 2, cols), BF)] * 2,
+        scratch_shapes=[pltpu.VMEM((rows, cols), F32)],
+        compiler_params=pltpu.CompilerParams(vmem_limit_bytes=16 << 20),
         cost_estimate=pl.CostEstimate(flops=parts.size, bytes_accessed=4 << 20, transcendentals=0),
-    )(parts, after)
+    )(core, parts, after)
 
 
 def per_device(hidden, head_weight, teacher_logits):
@@ -214,22 +243,28 @@
     rows = 8 * hidden.shape[0]
     steps = (1, 3, 2)
 
+    group = teacher_logits.shape[0]
+    mine = jnp.sum(jnp.exp(teacher_logits.astype(F32) / 2.0), axis=1)
+    teacher_sum = lax.dynamic_update_slice_in_dim(
+        jnp.zeros((rows,), F32), mine, vocab * group, 0
+    )
+    by_owner = teacher_logits.reshape(group, 16, -1).transpose(1, 0, 2)
+    teacher = lax.all_to_all(
+        by_owner, ("y", "zl", "core"), split_axis=0, concat_axis=0, tiled=True
+    ).reshape(rows, -1)
+
+    cut = 768
     near = lax.dynamic_slice_in_dim(hidden, core * half, half, 1)
     far = shift(near, "zh", 2, 1)
-    own = [shift(near, "x", 4, s) for s in steps]
-    own += [far] + [shift(far, "x", 4, s) for s in steps]
+    left = left_columns(far, cut, mine, by_owner)
+    near = [shift(near, "x", 4, s) for s in steps]
+    own = near + [far] + [shift(left, "x", 4, s) for s in steps]
+    own += [shift(b[:, cut:], "zh", 2, 1) for b in near]
     other = [swap(b) for b in own]
     place = [zh * 4 + (x - s) % 4 for s in (0,) + steps]
     place += [(1 - zh) * 4 + (x - s) % 4 for s in (0,) + steps]
     place = jnp.stack(place + [core]).astype(jnp.int32)
 
-    teacher = lax.all_to_all(
-        teacher_logits, ("y", "zl", "core"), split_axis=1, concat_axis=0, tiled=True
-    )
-    mine = jnp.sum(jnp.exp(teacher_logits.astype(F32) / 2.0), axis=1)
-    teacher_sum = lax.dynamic_update_slice_in_dim(
-        jnp.zeros((rows,), F32), mine, vocab * mine.shape[0], 0
-    )
     gathered, capped, sums = scores(place, hidden, own, other, head_weight, teacher_sum[None])
     totals = jnp.concatenate([total(sums), jnp.ones((6, rows), F32)])
 
@@ -241,9 +276,8 @@
     grad_head = lax.dot_general(
         gathered, delta, (((0,), (0,)), ((), ())), preferred_element_type=F32
     ).astype(BF)
-    summed = chip_sum(parts.reshape(64, rows // 64, half), grad_head)
-    mine = lax.dynamic_slice_in_dim(summed, core * 8, 8, 0)
-    rest = swap(lax.dynamic_slice_in_dim(summed, (1 - core) * 8, 8, 0))
+    mine, rest = chip_sum(which, parts.reshape(64, rows // 64, half), grad_head[:8, :128])
+    rest = swap(rest)
     grad_hidden = jnp.where(
         core == 0, jnp.concatenate([mine, rest], 1), jnp.concatenate([rest, mine], 1)
     )

time: 185 us -> 180 us (0.973)
  starting transfers between devices: 60.2 us -> 55.1 us
  local copies, waits for them, and re-layouts: 12.7 us -> 16.6 us
    ppermute x26 -> x32, starting transfers between devices: 49.3 us -> 43.8 us  [shift(): return lax.ppermute(v, axis, [(i, (i + step) % size) for i in range(size)])]
    all_to_all x1 -> x0, local copies, waits for them, and re-layouts: 3.24 us -> none  [per_device(): lax.all_to_all(teacher_logits, ('y', 'zl', 'core'), split_axis=1, concat_...]
    reshape x0 -> x1, local copies, waits for them, and re-layouts: none -> 3.2 us  [per_device(): by_owner = teacher_logits.reshape(group, 16, -1).transpose(1, 0, 2)]
    unnamed x12 -> x30, local copies, waits for them, and re-layouts: 7.29 us -> 9.43 us
    slice x0 -> x4, local copies, waits for them, and re-layouts: none -> 1.95 us  [the longest x3 1.95 us: per_device(): own += [shift(b[:, cut:], 'zh', 2, 1) for b in near]]
    pallas_call x1 -> x2, Pallas kernels: 5.25 us -> 4.79 us  [the longest x1 3.08 us: chip_sum(): pl.pallas_call(chip_sum_kernel, name='chip_sum', grid=(4,), in_specs=[SME...]
    ppermute x26 -> x32, waiting for transfers between devices: 25.6 us -> 25.5 us  [shift(): return lax.ppermute(v, axis, [(i, (i + step) % size) for i in range(size)])]
  transfers between devices with their start and end apart: 28 -> 34, of which waited for: 12 -> 17; matrix products, arithmetic and copies ran while one was open for 10% -> 11% of each run, Pallas kernels for 11% -> 12%
where the time goes in v3:
time: 180 us; the launch traced here: 179 us
  waiting for transfers between devices  56 us (31%)
  starting transfers between devices  55.1 us (31%)
  Pallas kernels  34.1 us (19%)
  local copies, waits for them, and re-layouts  16.6 us (9%)
  matrix products  11.2 us (6%)
  other arithmetic  5.42 us (3%)
    ppermute x32, starting transfers between devices, shift(): return lax.ppermute(v, axis, [(i, (i + step) % size) for i in range(size)])  43.8 us
    all_to_all x1, waiting for transfers between devices, per_device(): parts = lax.all_to_all(chip, CHIPS, split_axis=0, concat_axis=0, tiled=True)  30.5 us
    ppermute x32, waiting for transfers between devices, shift(): return lax.ppermute(v, axis, [(i, (i + step) % size) for i in range(size)])  25.5 us
    pallas_call x1, Pallas kernels, scores(): pl.pallas_call(functools.partial(scores_kernel, tile), name='scores', out...  16 us
    dot_general x1, matrix products, per_device(): lax.dot_general(gathered, delta, (((0,), (0,)), ((), ())), preferred_elem...  11.2 us
    unnamed x30, local copies, waits for them, and re-layouts  9.43 us
    pallas_call x1, Pallas kernels, delta_and_share(): pl.pallas_call(delta_kernel, name='delta_and_share', grid_spec=pltpu.Pref...  8.66 us
    all_to_all x1, starting transfers between devices, per_device(): parts = lax.all_to_all(chip, CHIPS, split_axis=0, concat_axis=0, tiled=True)  5.74 us
  transfers between devices with their start and end apart: 34, of which 17 were waited for; matrix products, arithmetic and copies ran while one was open for 11% of the time, Pallas kernels for 12%

profile of v3, /device:TPU:1, one launch (start us, length us, event | category | flops | bytes accessed | tf_op | source)
XLA Modules:
  0.0 179.3 jit_solution(2653361786966633802)
XLA Ops:
  1.8 4.5 %collective-permute-start.3 = (bf16[128,1792]{1,0:T(8,128)(2,1)S(1)}, bf16[128,1792]{1,0:T(8,128)(2,1)S(1)}, u32[]{:S(2)}, u32[]{:S(2)}) collective-permute-start(bf16[128,1792]{1,0:T(8,128)(2,1)S(1)} %constant_dynamic-slice_fusion), channel_id=1, source_target_pairs={{0,64},{64,0},{1,65},{65,1},{2,66},{66,2},{3,67},{67,3},{4,68},{68... | collective-permute-start | bytes 1376264 | tf_op jit(solution)/shard_map/ppermute | solution.py:21
  10.6 3.2 %copy.8 = bf16[8,16,8,1024]{3,2,0,1:T(8,128)(2,1)} copy(bf16[8,16,8,1024]{3,2,1,0:T(8,128)(2,1)} %bitcast.25) | data formatting | bytes 4194304 | tf_op jit(solution)/shard_map/reshape | solution.py:251
  15.1 1.6 collective-permute-done.3.block.refs_3_
  17.4 1.7 left_columns.1
  20.4 2.7 %collective-permute-start.7 = (bf16[128,1024]{1,0:T(8,128)(2,1)S(1)}, bf16[128,1024]{1,0:T(8,128)(2,1)S(1)}, u32[]{:S(2)}, u32[]{:S(2)}) collective-permute-start(bf16[128,1024]{1,0:T(8,128)(2,1)S(1)} %slice.16), channel_id=1, source_target_pairs={{0,64},{64,0},{1,65},{65,1},{2,66},{66,2},{3,67},{67,3},{4,68},{68... | collective-permute-start | bytes 786440 | tf_op jit(solution)/shard_map/ppermute | solution.py:21
  25.9 3.7 %collective-permute-done.2.refs_2_ = bf16[128,1792]{1,0:T(8,128)(2,1)} collective-permute-done((bf16[128,1792]{1,0:T(8,128)(2,1)S(1)}, bf16[128,1792]{1,0:T(8,128)(2,1)}, u32[]{:S(2)}, u32[]{:S(2)}) %collective-permute-start.2) | collective-permute-done | bytes 458784 | tf_op jit(solution)/shard_map/ppermute | solution.py:21
  31.1 5.0 %collective-permute-done.4.refs_4_ = bf16[128,768]{1,0:T(8,128)(2,1)} collective-permute-done((bf16[128,768]{1,0:T(8,128)(2,1)}, bf16[128,768]{1,0:T(8,128)(2,1)}, u32[]{:S(2)}, u32[]{:S(2)}) %collective-permute-start.4) | collective-permute-done | bytes 196640 | tf_op jit(solution)/shard_map/ppermute | solution.py:21
  36.1 4.3 %collective-permute-start.10 = (bf16[128,1792]{1,0:T(8,128)(2,1)S(1)}, bf16[128,1792]{1,0:T(8,128)(2,1)}, u32[]{:S(2)}, u32[]{:S(2)}) collective-permute-start(bf16[128,1792]{1,0:T(8,128)(2,1)S(1)} %collective-permute-done.refs_0_), channel_id=1, source_target_pairs={{0,1},{1,0},{2,3},{3,2},{4,5},{5,4},{6,7},{7,6},{8,9},{9,8},{10,11... | collective-permute-start | bytes 1376264 | tf_op jit(solution)/shard_map/ppermute | solution.py:21
  40.4 1.8 collective-permute-start.11
  43.0 5.6 %all-to-all-start = ((bf16[16,64,1024]{2,1,0:T(8,128)(2,1)}), bf16[16,64,1024]{2,1,0:T(8,128)(2,1)S(1)}, u32[]{:S(2)}, u32[]{:S(2)}) async-start(bf16[16,64,1024]{2,1,0:T(8,128)(2,1)} %bitcast.23), calls=%async_computation | async-start | bytes 4194304 | tf_op jit(solution)/shard_map/all_to_all | solution.py:252
  49.3 2.0 %collective-permute-done.16.refs_16_ = bf16[128,768]{1,0:T(8,128)(2,1)S(1)} collective-permute-done((bf16[128,768]{1,0:T(8,128)(2,1)}, bf16[128,768]{1,0:T(8,128)(2,1)S(1)}, u32[]{:S(2)}, u32[]{:S(2)}) %collective-permute-start.16) | collective-permute-done | bytes 196640 | tf_op jit(solution)/shard_map/ppermute | solution.py:21
  53.9 16.0 %scores.1 = (bf16[1024,3584]{1,0:T(8,128)(2,1)}, f32[1024,1024]{1,0:T(8,128)}, f32[2,1024]{1,0:T(2,128)}) custom-call(s32[9]{0:T(128)} %stack.36.place, bf16[128,3584]{1,0:T(8,128)(2,1)} %hidden.1, bf16[128,1792]{1,0:T(8,128)(2,1)} %copy-done.7, bf16[128,1792]{1,0:T(8,128)(2,1)} %collective-permute-done.1.refs_1_, ...), custom_call_target="tpu_custom_call" | custom-call | flops 7516192768 | bytes 20971520 | tf_op jit(solution)/shard_map/scores/pallas_call | solution.py:105
  72.1 1.8 %collective-permute-start.22 = (f32[2,1024]{1,0:T(2,128)S(1)}, f32[2,1024]{1,0:T(2,128)S(1)}, u32[]{:S(2)}, u32[]{:S(2)}) collective-permute-start(f32[2,1024]{1,0:T(2,128)S(1)} %add.107), channel_id=1, source_target_pairs={{0,48},{16,0},{32,16},{48,32},{1,49},{17,1},{33,17},{49,33},{2,50}... | collective-permute-start | bytes 24584 | tf_op jit(solution)/shard_map/ppermute | solution.py:21
  74.5 1.7 collective-permute-done.23
  76.1 1.5 collective-permute-done.21
  77.7 3.0 %collective-permute-start.26 = (f32[2,1024]{1,0:T(2,128)S(1)}, f32[2,1024]{1,0:T(2,128)S(1)}, u32[]{:S(2)}, u32[]{:S(2)}) collective-permute-start(f32[2,1024]{1,0:T(2,128)S(1)} %add_add_fusion.2), channel_id=1, source_target_pairs={{0,8},{4,12},{8,0},{12,4},{1,9},{5,13},{9,1},{13,5},{2,10},{6,14},... | collective-permute-start | bytes 24584 | tf_op jit(solution)/shard_map/ppermute | solution.py:21
  83.5 1.8 %collective-permute-done.24 = f32[2,1024]{1,0:T(2,128)S(1)} collective-permute-done((f32[2,1024]{1,0:T(2,128)S(1)}, f32[2,1024]{1,0:T(2,128)S(1)}, u32[]{:S(2)}, u32[]{:S(2)}) %collective-permute-start.24) | collective-permute-done | bytes 8224 | tf_op jit(solution)/shard_map/ppermute | solution.py:21
  85.3 2.0 %collective-permute-start.29 = (f32[2,1024]{1,0:T(2,128)S(1)}, f32[2,1024]{1,0:T(2,128)S(1)}, u32[]{:S(2)}, u32[]{:S(2)}) collective-permute-start(f32[2,1024]{1,0:T(2,128)S(1)} %add_add_fusion.1), channel_id=1, source_target_pairs={{0,64},{2,66},{64,0},{66,2},{1,65},{3,67},{65,1},{67,3},{4,68},{6,... | collective-permute-start | bytes 24584 | tf_op jit(solution)/shard_map/ppermute | solution.py:21
  87.3 1.6 collective-permute-start.28
  89.8 2.8 %collective-permute-done.27 = f32[2,1024]{1,0:T(2,128)S(1)} collective-permute-done((f32[2,1024]{1,0:T(2,128)S(1)}, f32[2,1024]{1,0:T(2,128)S(1)}, u32[]{:S(2)}, u32[]{:S(2)}) %collective-permute-start.27) | collective-permute-done | bytes 8224 | tf_op jit(solution)/shard_map/ppermute | solution.py:21
  92.7 2.2 %copy-done.1 = f32[1024,1024]{1,0:T(8,128)S(1)} copy-done((f32[1024,1024]{1,0:T(8,128)S(1)}, f32[1024,1024]{1,0:T(8,128)}, u32[]{:S(2)}) %copy-start.1) | copy-done | bytes 4194328
  94.9 8.7 %delta_and_share.1 = (bf16[1024,1024]{1,0:T(8,128)(2,1)S(1)}, bf16[1024,1792]{1,0:T(8,128)(2,1)S(1)}) custom-call(s32[1]{0:T(128)} %bitcast.core, f32[1024,1024]{1,0:T(8,128)S(1)} %copy-done.1, bf16[1024,1024]{1,0:T(8,128)(2,1)S(1)} %bitcast.21, f32[8,1024]{1,0:T(8,128)S(1)} %concatenate.9.totals, bf16[3584,1024]{1,0:T(8,128)(2,1)} %weight.3), custom_call_target="tpu_custom_call" | custom-call | flops 3758096384 | bytes 16777216 | tf_op jit(solution)/shard_map/delta_and_share/pallas_call | solution.py:147
  103.6 5.3 %collective-permute-start.30 = (bf16[1024,1792]{1,0:T(8,128)(2,1)S(1)}, bf16[1024,1792]{1,0:T(8,128)(2,1)S(1)}, u32[]{:S(2)}, u32[]{:S(2)}) collective-permute-start(bf16[1024,1792]{1,0:T(8,128)(2,1)S(1)} %get-tuple-element.12), channel_id=1, source_target_pairs={{0,1},{1,0},{2,3},{3,2},{4,5},{5,4},{6,7},{7,6},{8,9},{9,8},{10,11... | collective-permute-start | bytes 11010056 | tf_op jit(solution)/shard_map/ppermute | solution.py:21
  108.8 3.1 %copy-done = bf16[3584,1024]{1,0:T(8,128)(2,1)S(1)} copy-done((bf16[3584,1024]{1,0:T(8,128)(2,1)S(1)}, bf16[3584,1024]{1,0:T(8,128)(2,1)}, u32[]{:S(2)}) %copy-start) | copy-done | bytes 7340056
  111.9 4.7 %own_share.1 = bf16[1024,1792]{1,0:T(8,128)(2,1)S(1)} custom-call(s32[1]{0:T(128)} %bitcast.core, bf16[1024,1024]{1,0:T(8,128)(2,1)S(1)} %get-tuple-element.11.delta, bf16[3584,1024]{1,0:T(8,128)(2,1)S(1)} %copy-done), custom_call_target="tpu_custom_call" | custom-call | flops 3758096384 | bytes 10485760 | tf_op jit(solution)/shard_map/own_share/pallas_call | solution.py:183
  116.6 2.8 %add_convert_fusion = bf16[1024,1792]{1,0:T(8,128)(2,1)} fusion(bf16[1024,1792]{1,0:T(8,128)(2,1)S(1)} %collective-permute-done.30, bf16[1024,1792]{1,0:T(8,128)(2,1)S(1)} %own_share.1), kind=kLoop, calls=%fused_computation.1 | loop fusion | flops 7340032 | bytes 11010048 | tf_op jit(solution)/shard_map/convert_element_type | solution.py:274
  119.4 5.7 %all-to-all-start.1 = ((bf16[64,16,1792]{2,1,0:T(8,128)(2,1)}), bf16[64,16,1792]{2,1,0:T(8,128)(2,1)}, u32[]{:S(2)}, u32[]{:S(2)}) async-start(bf16[64,16,1792]{2,1,0:T(8,128)(2,1)} %bitcast.24), calls=%async_computation.1 | async-start | bytes 7340032 | tf_op jit(solution)/shard_map/all_to_all | solution.py:275
  125.1 11.2 %convolution_convert_fusion = bf16[3584,1024]{1,0:T(8,128)(2,1)S(1)} fusion(bf16[1024,3584]{1,0:T(8,128)(2,1)} %get-tuple-element.13, bf16[1024,1024]{1,0:T(8,128)(2,1)S(1)} %copy-done.3), kind=kOutput, calls=%fused_computation | convolution fusion | flops 7519862784 | bytes 16777216 | tf_op jit(solution)/shard_map/dot_general | solution.py:276
  136.3 3.0 %copy-done.10 = bf16[3584,1024]{1,0:T(8,128)(2,1)} copy-done((bf16[3584,1024]{1,0:T(8,128)(2,1)}, bf16[3584,1024]{1,0:T(8,128)(2,1)S(1)}, u32[]{:S(2)}) %copy-start.10) | copy-done | bytes 7340056
  139.3 30.5 %all-to-all-done.1.parts = bf16[64,16,1792]{2,1,0:T(8,128)(2,1)} async-done(((bf16[64,16,1792]{2,1,0:T(8,128)(2,1)}), bf16[64,16,1792]{2,1,0:T(8,128)(2,1)}, u32[]{:S(2)}, u32[]{:S(2)}) %all-to-all-start.1) | async-done | bytes 3670048 | tf_op jit(solution)/shard_map/all_to_all | solution.py:275
  169.9 3.1 %chip_sum.1 = (bf16[8,1792]{1,0:T(8,128)(2,1)S(1)}, bf16[8,1792]{1,0:T(8,128)(2,1)S(1)}) custom-call(s32[1]{0:T(128)} %bitcast.core, bf16[64,16,1792]{2,1,0:T(8,128)(2,1)} %all-to-all-done.1.parts, bf16[8,128]{1,0:T(8,128)(2,1)S(1)} %slice.19.after), custom_call_target="tpu_custom_call" | custom-call | flops 1835008 | bytes 4194304 | tf_op jit(solution)/shard_map/chip_sum/pallas_call | solution.py:225
  173.0 4.8 %collective-permute-start.31 = (bf16[8,1792]{1,0:T(8,128)(2,1)S(1)}, bf16[8,1792]{1,0:T(8,128)(2,1)S(1)}, u32[]{:S(2)}, u32[]{:S(2)}) collective-permute-start(bf16[8,1792]{1,0:T(8,128)(2,1)S(1)} %get-tuple-element.15), channel_id=1, source_target_pairs={{0,1},{1,0},{2,3},{3,2},{4,5},{5,4},{6,7},{7,6},{8,9},{9,8},{10,11... | collective-permute-start | bytes 86024 | tf_op jit(solution)/shard_map/ppermute | solution.py:21
  (89 shorter events, 25.1 us)
Async XLA Ops:
  1.8 14.8 %collective-permute-start.3 = (bf16[128,1792]{1,0:T(8,128)(2,1)S(1)}, bf16[128,1792]{1,0:T(8,128)(2,1)S(1)}, u32[]{:S(2)}, u32[]{:S(2)}) collective-permute-start(bf16[128,1792]{1,0:T(8,128)(2,1)S(1)} %constant_dynamic-slice_fusion), channel_id=1, source_target_pairs={{0,64},{64,0},{1,65},{65,1},{2,66},{66,2},{3,67},{67,3},{4,68},{68... | collective-permute-start | bytes 1376264 | tf_op jit(solution)/shard_map/ppermute | solution.py:21
  6.4 14.0 %collective-permute-start = (bf16[128,1792]{1,0:T(8,128)(2,1)S(1)}, bf16[128,1792]{1,0:T(8,128)(2,1)S(1)}, u32[]{:S(2)}, u32[]{:S(2)}) collective-permute-start(bf16[128,1792]{1,0:T(8,128)(2,1)S(1)} %constant_dynamic-slice_fusion), channel_id=1, source_target_pairs={{0,16},{16,32},{32,48},{48,0},{1,17},{17,33},{33,49},{49,1},{2,18}... | collective-permute-start | bytes 1376264 | tf_op jit(solution)/shard_map/ppermute | solution.py:21
  7.6 15.5 %collective-permute-start.1 = (bf16[128,1792]{1,0:T(8,128)(2,1)S(1)}, bf16[128,1792]{1,0:T(8,128)(2,1)}, u32[]{:S(2)}, u32[]{:S(2)}) collective-permute-start(bf16[128,1792]{1,0:T(8,128)(2,1)S(1)} %constant_dynamic-slice_fusion), channel_id=1, source_target_pairs={{0,48},{16,0},{32,16},{48,32},{1,49},{17,1},{33,17},{49,33},{2,50}... | collective-permute-start | bytes 1376264 | tf_op jit(solution)/shard_map/ppermute | solution.py:21
  9.0 20.6 %collective-permute-start.2 = (bf16[128,1792]{1,0:T(8,128)(2,1)S(1)}, bf16[128,1792]{1,0:T(8,128)(2,1)}, u32[]{:S(2)}, u32[]{:S(2)}) collective-permute-start(bf16[128,1792]{1,0:T(8,128)(2,1)S(1)} %constant_dynamic-slice_fusion), channel_id=1, source_target_pairs={{0,32},{16,48},{32,0},{48,16},{1,33},{17,49},{33,1},{49,17},{2,34}... | collective-permute-start | bytes 1376264 | tf_op jit(solution)/shard_map/ppermute | solution.py:21
  19.1 17.0 %collective-permute-start.4 = (bf16[128,768]{1,0:T(8,128)(2,1)}, bf16[128,768]{1,0:T(8,128)(2,1)}, u32[]{:S(2)}, u32[]{:S(2)}) collective-permute-start(bf16[128,768]{1,0:T(8,128)(2,1)} %left_columns.1), channel_id=1, source_target_pairs={{0,16},{16,32},{32,48},{48,0},{1,17},{17,33},{33,49},{49,1},{2,18}... | collective-permute-start | bytes 589832 | tf_op jit(solution)/shard_map/ppermute | solution.py:21
  20.4 21.8 %collective-permute-start.7 = (bf16[128,1024]{1,0:T(8,128)(2,1)S(1)}, bf16[128,1024]{1,0:T(8,128)(2,1)S(1)}, u32[]{:S(2)}, u32[]{:S(2)}) collective-permute-start(bf16[128,1024]{1,0:T(8,128)(2,1)S(1)} %slice.16), channel_id=1, source_target_pairs={{0,64},{64,0},{1,65},{65,1},{2,66},{66,2},{3,67},{67,3},{4,68},{68... | collective-permute-start | bytes 786440 | tf_op jit(solution)/shard_map/ppermute | solution.py:21
  24.1 18.2 %collective-permute-start.8 = (bf16[128,1024]{1,0:T(8,128)(2,1)S(1)}, bf16[128,1024]{1,0:T(8,128)(2,1)S(1)}, u32[]{:S(2)}, u32[]{:S(2)}) collective-permute-start(bf16[128,1024]{1,0:T(8,128)(2,1)S(1)} %slice.17), channel_id=1, source_target_pairs={{0,64},{64,0},{1,65},{65,1},{2,66},{66,2},{3,67},{67,3},{4,68},{68... | collective-permute-start | bytes 786440 | tf_op jit(solution)/shard_map/ppermute | solution.py:21
  24.5 11.6 %collective-permute-start.5 = (bf16[128,768]{1,0:T(8,128)(2,1)}, bf16[128,768]{1,0:T(8,128)(2,1)}, u32[]{:S(2)}, u32[]{:S(2)}) collective-permute-start(bf16[128,768]{1,0:T(8,128)(2,1)} %left_columns.1), channel_id=1, source_target_pairs={{0,48},{16,0},{32,16},{48,32},{1,49},{17,1},{33,17},{49,33},{2,50}... | collective-permute-start | bytes 589832 | tf_op jit(solution)/shard_map/ppermute | solution.py:21
  29.6 10.8 %collective-permute-start.6 = (bf16[128,768]{1,0:T(8,128)(2,1)}, bf16[128,768]{1,0:T(8,128)(2,1)S(1)}, u32[]{:S(2)}, u32[]{:S(2)}) collective-permute-start(bf16[128,768]{1,0:T(8,128)(2,1)} %left_columns.1), channel_id=1, source_target_pairs={{0,32},{16,48},{32,0},{48,16},{1,33},{17,49},{33,1},{49,17},{2,34}... | collective-permute-start | bytes 589832 | tf_op jit(solution)/shard_map/ppermute | solution.py:21
  36.1 12.5 %collective-permute-start.9 = (bf16[128,1024]{1,0:T(8,128)(2,1)S(1)}, bf16[128,1024]{1,0:T(8,128)(2,1)}, u32[]{:S(2)}, u32[]{:S(2)}) collective-permute-start(bf16[128,1024]{1,0:T(8,128)(2,1)S(1)} %slice.18), channel_id=1, source_target_pairs={{0,64},{64,0},{1,65},{65,1},{2,66},{66,2},{3,67},{67,3},{4,68},{68... | collective-permute-start | bytes 786440 | tf_op jit(solution)/shard_map/ppermute | solution.py:21
  36.1 15.3 %collective-permute-start.10 = (bf16[128,1792]{1,0:T(8,128)(2,1)S(1)}, bf16[128,1792]{1,0:T(8,128)(2,1)}, u32[]{:S(2)}, u32[]{:S(2)}) collective-permute-start(bf16[128,1792]{1,0:T(8,128)(2,1)S(1)} %collective-permute-done.refs_0_), channel_id=1, source_target_pairs={{0,1},{1,0},{2,3},{3,2},{4,5},{5,4},{6,7},{7,6},{8,9},{9,8},{10,11... | collective-permute-start | bytes 1376264 | tf_op jit(solution)/shard_map/ppermute | solution.py:21
  40.4 11.4 %collective-permute-start.11 = (bf16[128,1792]{1,0:T(8,128)(2,1)}, bf16[128,1792]{1,0:T(8,128)(2,1)}, u32[]{:S(2)}, u32[]{:S(2)}) collective-permute-start(bf16[128,1792]{1,0:T(8,128)(2,1)} %collective-permute-done.1.refs_1_), channel_id=1, source_target_pairs={{0,1},{1,0},{2,3},{3,2},{4,5},{5,4},{6,7},{7,6},{8,9},{9,8},{10,11... | collective-permute-start | bytes 1376264 | tf_op jit(solution)/shard_map/ppermute | solution.py:21
  42.2 6.6 %collective-permute-start.14 = (bf16[128,768]{1,0:T(8,128)(2,1)}, bf16[128,768]{1,0:T(8,128)(2,1)}, u32[]{:S(2)}, u32[]{:S(2)}) collective-permute-start(bf16[128,768]{1,0:T(8,128)(2,1)} %collective-permute-done.4.refs_4_), channel_id=1, source_target_pairs={{0,1},{1,0},{2,3},{3,2},{4,5},{5,4},{6,7},{7,6},{8,9},{9,8},{10,11... | collective-permute-start | bytes 589832 | tf_op jit(solution)/shard_map/ppermute | solution.py:21
  42.3 6.9 %collective-permute-start.15 = (bf16[128,768]{1,0:T(8,128)(2,1)}, bf16[128,768]{1,0:T(8,128)(2,1)}, u32[]{:S(2)}, u32[]{:S(2)}) collective-permute-start(bf16[128,768]{1,0:T(8,128)(2,1)} %collective-permute-done.5.refs_5_), channel_id=1, source_target_pairs={{0,1},{1,0},{2,3},{3,2},{4,5},{5,4},{6,7},{7,6},{8,9},{9,8},{10,11... | collective-permute-start | bytes 589832 | tf_op jit(solution)/shard_map/ppermute | solution.py:21
  43.0 49.7 %all-to-all-start = ((bf16[16,64,1024]{2,1,0:T(8,128)(2,1)}), bf16[16,64,1024]{2,1,0:T(8,128)(2,1)S(1)}, u32[]{:S(2)}, u32[]{:S(2)}) async-start(bf16[16,64,1024]{2,1,0:T(8,128)(2,1)} %bitcast.23), calls=%async_computation | async-start | bytes 4194304 | tf_op jit(solution)/shard_map/all_to_all | solution.py:252
  48.6 4.2 %collective-permute-start.12 = (bf16[128,1792]{1,0:T(8,128)(2,1)}, bf16[128,1792]{1,0:T(8,128)(2,1)}, u32[]{:S(2)}, u32[]{:S(2)}) collective-permute-start(bf16[128,1792]{1,0:T(8,128)(2,1)} %collective-permute-done.2.refs_2_), channel_id=1, source_target_pairs={{0,1},{1,0},{2,3},{3,2},{4,5},{5,4},{6,7},{7,6},{8,9},{9,8},{10,11... | collective-permute-start | bytes 1376264 | tf_op jit(solution)/shard_map/ppermute | solution.py:21
  48.8 2.5 %collective-permute-start.16 = (bf16[128,768]{1,0:T(8,128)(2,1)}, bf16[128,768]{1,0:T(8,128)(2,1)S(1)}, u32[]{:S(2)}, u32[]{:S(2)}) collective-permute-start(bf16[128,768]{1,0:T(8,128)(2,1)} %copy-done.13), channel_id=1, source_target_pairs={{0,1},{1,0},{2,3},{3,2},{4,5},{5,4},{6,7},{7,6},{8,9},{9,8},{10,11... | collective-permute-start | bytes 589832 | tf_op jit(solution)/shard_map/ppermute | solution.py:21
  49.2 3.6 %collective-permute-start.13 = (bf16[128,1792]{1,0:T(8,128)(2,1)S(1)}, bf16[128,1792]{1,0:T(8,128)(2,1)}, u32[]{:S(2)}, u32[]{:S(2)}) collective-permute-start(bf16[128,1792]{1,0:T(8,128)(2,1)S(1)} %copy-done.6), channel_id=1, source_target_pairs={{0,1},{1,0},{2,3},{3,2},{4,5},{5,4},{6,7},{7,6},{8,9},{9,8},{10,11... | collective-permute-start | bytes 1376264 | tf_op jit(solution)/shard_map/ppermute | solution.py:21
  51.4 2.1 %collective-permute-start.18 = (bf16[128,1024]{1,0:T(8,128)(2,1)}, bf16[128,1024]{1,0:T(8,128)(2,1)}, u32[]{:S(2)}, u32[]{:S(2)}) collective-permute-start(bf16[128,1024]{1,0:T(8,128)(2,1)} %copy-done.12), channel_id=1, source_target_pairs={{0,1},{1,0},{2,3},{3,2},{4,5},{5,4},{6,7},{7,6},{8,9},{9,8},{10,11... | collective-permute-start | bytes 786440 | tf_op jit(solution)/shard_map/ppermute | solution.py:21
  51.8 2.1 %collective-permute-start.19 = (bf16[128,1024]{1,0:T(8,128)(2,1)}, bf16[128,1024]{1,0:T(8,128)(2,1)}, u32[]{:S(2)}, u32[]{:S(2)}) collective-permute-start(bf16[128,1024]{1,0:T(8,128)(2,1)} %collective-permute-done.9.refs_9_), channel_id=1, source_target_pairs={{0,1},{1,0},{2,3},{3,2},{4,5},{5,4},{6,7},{7,6},{8,9},{9,8},{10,11... | collective-permute-start | bytes 786440 | tf_op jit(solution)/shard_map/ppermute | solution.py:21
  72.1 4.0 %collective-permute-start.23 = (f32[2,1024]{1,0:T(2,128)S(1)}, f32[2,1024]{1,0:T(2,128)S(1)}, u32[]{:S(2)}, u32[]{:S(2)}) collective-permute-start(f32[2,1024]{1,0:T(2,128)S(1)} %add.107), channel_id=1, source_target_pairs={{0,32},{16,48},{32,0},{48,16},{1,33},{17,49},{33,1},{49,17},{2,34}... | collective-permute-start | bytes 24584 | tf_op jit(solution)/shard_map/ppermute | solution.py:21
  72.1 4.0 %collective-permute-start.22 = (f32[2,1024]{1,0:T(2,128)S(1)}, f32[2,1024]{1,0:T(2,128)S(1)}, u32[]{:S(2)}, u32[]{:S(2)}) collective-permute-start(f32[2,1024]{1,0:T(2,128)S(1)} %add.107), channel_id=1, source_target_pairs={{0,48},{16,0},{32,16},{48,32},{1,49},{17,1},{33,17},{49,33},{2,50}... | collective-permute-start | bytes 24584 | tf_op jit(solution)/shard_map/ppermute | solution.py:21
  74.0 3.7 %collective-permute-start.21 = (f32[2,1024]{1,0:T(2,128)S(1)}, f32[2,1024]{1,0:T(2,128)S(1)}, u32[]{:S(2)}, u32[]{:S(2)}) collective-permute-start(f32[2,1024]{1,0:T(2,128)S(1)} %add.107), channel_id=1, source_target_pairs={{0,16},{16,32},{32,48},{48,0},{1,17},{17,33},{33,49},{49,1},{2,18}... | collective-permute-start | bytes 24584 | tf_op jit(solution)/shard_map/ppermute | solution.py:21
  77.7 4.5 %collective-permute-start.26 = (f32[2,1024]{1,0:T(2,128)S(1)}, f32[2,1024]{1,0:T(2,128)S(1)}, u32[]{:S(2)}, u32[]{:S(2)}) collective-permute-start(f32[2,1024]{1,0:T(2,128)S(1)} %add_add_fusion.2), channel_id=1, source_target_pairs={{0,8},{4,12},{8,0},{12,4},{1,9},{5,13},{9,1},{13,5},{2,10},{6,14},... | collective-permute-start | bytes 24584 | tf_op jit(solution)/shard_map/ppermute | solution.py:21
  80.7 2.8 %collective-permute-start.25 = (f32[2,1024]{1,0:T(2,128)S(1)}, f32[2,1024]{1,0:T(2,128)S(1)}, u32[]{:S(2)}, u32[]{:S(2)}) collective-permute-start(f32[2,1024]{1,0:T(2,128)S(1)} %add_add_fusion.2), channel_id=1, source_target_pairs={{0,12},{4,0},{8,4},{12,8},{1,13},{5,1},{9,5},{13,9},{2,14},{6,2},{... | collective-permute-start | bytes 24584 | tf_op jit(solution)/shard_map/ppermute | solution.py:21
  81.6 3.7 %collective-permute-start.24 = (f32[2,1024]{1,0:T(2,128)S(1)}, f32[2,1024]{1,0:T(2,128)S(1)}, u32[]{:S(2)}, u32[]{:S(2)}) collective-permute-start(f32[2,1024]{1,0:T(2,128)S(1)} %add_add_fusion.2), channel_id=1, source_target_pairs={{0,4},{4,8},{8,12},{12,0},{1,5},{5,9},{9,13},{13,1},{2,6},{6,10},{... | collective-permute-start | bytes 24584 | tf_op jit(solution)/shard_map/ppermute | solution.py:21
  85.3 4.1 %collective-permute-start.29 = (f32[2,1024]{1,0:T(2,128)S(1)}, f32[2,1024]{1,0:T(2,128)S(1)}, u32[]{:S(2)}, u32[]{:S(2)}) collective-permute-start(f32[2,1024]{1,0:T(2,128)S(1)} %add_add_fusion.1), channel_id=1, source_target_pairs={{0,64},{2,66},{64,0},{66,2},{1,65},{3,67},{65,1},{67,3},{4,68},{6,... | collective-permute-start | bytes 24584 | tf_op jit(solution)/shard_map/ppermute | solution.py:21
  87.3 2.5 %collective-permute-start.28 = (f32[2,1024]{1,0:T(2,128)S(1)}, f32[2,1024]{1,0:T(2,128)S(1)}, u32[]{:S(2)}, u32[]{:S(2)}) collective-permute-start(f32[2,1024]{1,0:T(2,128)S(1)} %add_add_fusion.1), channel_id=1, source_target_pairs={{0,66},{2,0},{64,2},{66,64},{1,67},{3,1},{65,3},{67,65},{4,70},{6,... | collective-permute-start | bytes 24584 | tf_op jit(solution)/shard_map/ppermute | solution.py:21
  88.9 3.7 %collective-permute-start.27 = (f32[2,1024]{1,0:T(2,128)S(1)}, f32[2,1024]{1,0:T(2,128)S(1)}, u32[]{:S(2)}, u32[]{:S(2)}) collective-permute-start(f32[2,1024]{1,0:T(2,128)S(1)} %add_add_fusion.1), channel_id=1, source_target_pairs={{0,2},{2,64},{64,66},{66,0},{1,3},{3,65},{65,67},{67,1},{4,6},{6,6... | collective-permute-start | bytes 24584 | tf_op jit(solution)/shard_map/ppermute | solution.py:21
  103.6 13.0 %collective-permute-start.30 = (bf16[1024,1792]{1,0:T(8,128)(2,1)S(1)}, bf16[1024,1792]{1,0:T(8,128)(2,1)S(1)}, u32[]{:S(2)}, u32[]{:S(2)}) collective-permute-start(bf16[1024,1792]{1,0:T(8,128)(2,1)S(1)} %get-tuple-element.12), channel_id=1, source_target_pairs={{0,1},{1,0},{2,3},{3,2},{4,5},{5,4},{6,7},{7,6},{8,9},{9,8},{10,11... | collective-permute-start | bytes 11010056 | tf_op jit(solution)/shard_map/ppermute | solution.py:21
  119.4 50.5 %all-to-all-start.1 = ((bf16[64,16,1792]{2,1,0:T(8,128)(2,1)}), bf16[64,16,1792]{2,1,0:T(8,128)(2,1)}, u32[]{:S(2)}, u32[]{:S(2)}) async-start(bf16[64,16,1792]{2,1,0:T(8,128)(2,1)} %bitcast.24), calls=%async_computation.1 | async-start | bytes 7340032 | tf_op jit(solution)/shard_map/all_to_all | solution.py:275
  173.0 5.7 %collective-permute-start.31 = (bf16[8,1792]{1,0:T(8,128)(2,1)S(1)}, bf16[8,1792]{1,0:T(8,128)(2,1)S(1)}, u32[]{:S(2)}, u32[]{:S(2)}) collective-permute-start(bf16[8,1792]{1,0:T(8,128)(2,1)S(1)} %get-tuple-element.15), channel_id=1, source_target_pairs={{0,1},{1,0},{2,3},{3,2},{4,5},{5,4},{6,7},{7,6},{8,9},{9,8},{10,11... | collective-permute-start | bytes 86024 | tf_op jit(solution)/shard_map/ppermute | solution.py:21
  (17 other events, 161.5 us)

commit v4 on v3

--- a/solution.py
+++ b/solution.py
@@ -9,7 +9,7 @@
 
 BF = jnp.bfloat16
 F32 = jnp.float32
-CHIPS = ("zh", "x", "y", "zl")
+EVERY = ("zh", "x", "y", "zl", "core")
 Z = ("zh", "zl")
 VMEM_BYTES = 60 << 20
 SMEM = pl.BlockSpec(memory_space=pltpu.SMEM)
@@ -172,9 +172,18 @@
     )(core, capped, teacher, totals, weight)
 
 
-def share_kernel(core, delta, weight, share):
+def share_kernel(core, delta, weight, share, weight_v, sem):
+    half = weight_v.shape[0]
+    at = pl.ds(pl.multiple_of(core[0] * half, half), half)
+    load = pltpu.make_async_copy(weight.at[at, :], weight_v, sem)
+
+    @pl.when(pl.program_id(0) == 0)
+    def _():
+        load.start()
+        load.wait()
+
     share[...] = lax.dot_general(
-        delta[...], weight[...], (((1,), (1,)), ((), ())), preferred_element_type=F32
+        delta[...], weight_v[...], (((1,), (1,)), ((), ())), preferred_element_type=F32
     ).astype(BF)
 
 
@@ -186,11 +195,9 @@
         grid_spec=pltpu.PrefetchScalarGridSpec(
             num_scalar_prefetch=1,
             grid=(rows // tile,),
-            in_specs=[
-                pl.BlockSpec((tile, cols), lambda i, core: (i, 0)),
-                pl.BlockSpec((half, cols), lambda i, core: (core[0], 0)),
-            ],
+            in_specs=[pl.BlockSpec((tile, cols), lambda i, core: (i, 0)), ANY],
             out_specs=pl.BlockSpec((tile, half), lambda i, core: (i, 0)),
+            scratch_shapes=[pltpu.VMEM((half, cols), BF), pltpu.SemaphoreType.DMA],
         ),
         out_shape=jax.ShapeDtypeStruct((rows, half), BF),
         compiler_params=pltpu.CompilerParams(vmem_limit_bytes=40 << 20),
@@ -200,7 +207,7 @@
     )(core, delta, weight)
 
 
-def chip_sum_kernel(core, parts, after, mine, rest, total):
+def chip_sum_kernel(parts, after, out, total):
     i = pl.program_id(0)
     now = jnp.sum(parts[...].astype(F32), axis=0)
 
@@ -214,25 +221,27 @@
 
     @pl.when(i == pl.num_programs(0) - 1)
     def _():
-        low, high = total[:8, :], total[8:, :]
-        mine[...] = jnp.where(core[0] == 0, low, high).astype(BF)
-        rest[...] = jnp.where(core[0] == 0, high, low).astype(BF)
-
-
-def chip_sum(core, parts, after):
-    count, rows, cols = parts.shape
-    out = pl.BlockSpec((rows // 2, cols), lambda i: (0, 0))
+        half = total.shape[2]
+        for k in range(2):
+            out[:, k * half : (k + 1) * half] = total[k].astype(BF)
+
+
+def chip_sum(parts, after):
+    count, cores, rows, cols = parts.shape
     return pl.pallas_call(
         chip_sum_kernel,
         name="chip_sum",
         grid=(4,),
-        in_specs=[SMEM, pl.BlockSpec((count // 4, rows, cols), lambda i: (i, 0, 0)), ANY],
-        out_specs=(out, out),
-        out_shape=[jax.ShapeDtypeStruct((rows // 2, cols), BF)] * 2,
-        scratch_shapes=[pltpu.VMEM((rows, cols), F32)],
+        in_specs=[
+            pl.BlockSpec((count // 4, cores, rows, cols), lambda i: (i, 0, 0, 0)),
+            ANY,
+        ],
+        out_specs=pl.BlockSpec((rows, cores * cols), lambda i: (0, 0)),
+        out_shape=jax.ShapeDtypeStruct((rows, cores * cols), BF),
+        scratch_shapes=[pltpu.VMEM((cores, rows, cols), F32)],
         compiler_params=pltpu.CompilerParams(vmem_limit_bytes=16 << 20),
         cost_estimate=pl.CostEstimate(flops=parts.size, bytes_accessed=4 << 20, transcendentals=0),
-    )(core, parts, after)
+    )(parts, after)
 
 
 def per_device(hidden, head_weight, teacher_logits):
@@ -272,15 +281,13 @@
     delta, give = delta_and_share(which, capped, teacher, totals, head_weight)
     keep = own_share(which, delta, head_weight)
     chip = (keep.astype(F32) + swap(give).astype(F32)).astype(BF)
-    parts = lax.all_to_all(chip, CHIPS, split_axis=0, concat_axis=0, tiled=True)
+    parts = lax.all_to_all(
+        chip.reshape(128, rows // 128, half), EVERY, split_axis=0, concat_axis=0, tiled=True
+    )
     grad_head = lax.dot_general(
         gathered, delta, (((0,), (0,)), ((), ())), preferred_element_type=F32
     ).astype(BF)
-    mine, rest = chip_sum(which, parts.reshape(64, rows // 64, half), grad_head[:8, :128])
-    rest = swap(rest)
-    grad_hidden = jnp.where(
-        core == 0, jnp.concatenate([mine, rest], 1), jnp.concatenate([rest, mine], 1)
-    )
+    grad_hidden = chip_sum(parts.reshape(64, 2, rows // 128, half), grad_head[:8, :128])
     return grad_hidden, grad_head
 
 

time: 180 us -> 176 us (0.978)
  starting transfers between devices: 55.1 us -> 49.8 us
    ppermute x32 -> x31, starting transfers between devices: 43.8 us -> 38.9 us  [shift(): return lax.ppermute(v, axis, [(i, (i + step) % size) for i in range(size)])]
    convert_element_type x1 -> x0, other arithmetic: 2.77 us -> none  [per_device(): chip = (keep.astype(F32) + swap(give).astype(F32)).astype(BF)]
    reshape x0 -> x1, other arithmetic: none -> 2.76 us  [per_device(): chip.reshape(128, rows // 128, half)]
    all_to_all x1, waiting for transfers between devices: 30.5 us -> 32.7 us  [per_device(): lax.all_to_all(chip.reshape(128, rows // 128, half), EVERY, split_axis=0,...]
    ppermute x32 -> x31, waiting for transfers between devices: 25.5 us -> 24.6 us  [shift(): return lax.ppermute(v, axis, [(i, (i + step) % size) for i in range(size)])]
  transfers between devices with their start and end apart: 34 -> 33, of which waited for: 17 -> 16; matrix products, arithmetic and copies ran while one was open for 11% -> 11% of each run, Pallas kernels for 12% -> 13%
where the time goes in v4:
time: 176 us
  waiting for transfers between devices  57.3 us (33%)
  starting transfers between devices  49.8 us (28%)
  Pallas kernels  35 us (20%)
  local copies, waits for them, and re-layouts  16.6 us (9%)
  matrix products  11.2 us (6%)
  other arithmetic  4.79 us (3%)
    ppermute x31, starting transfers between devices, shift(): return lax.ppermute(v, axis, [(i, (i + step) % size) for i in range(size)])  38.9 us
    all_to_all x1, waiting for transfers between devices, per_device(): lax.all_to_all(chip.reshape(128, rows // 128, half), EVERY, split_axis=0,...  32.7 us
    ppermute x31, waiting for transfers between devices, shift(): return lax.ppermute(v, axis, [(i, (i + step) % size) for i in range(size)])  24.6 us
    pallas_call x1, Pallas kernels, scores(): pl.pallas_call(functools.partial(scores_kernel, tile), name='scores', out...  16 us
    dot_general x1, matrix products, per_device(): lax.dot_general(gathered, delta, (((0,), (0,)), ((), ())), preferred_elem...  11.2 us
    unnamed x30, local copies, waits for them, and re-layouts  9.46 us
    pallas_call x1, Pallas kernels, delta_and_share(): pl.pallas_call(delta_kernel, name='delta_and_share', grid_spec=pltpu.Pref...  8.66 us
    all_to_all x1, starting transfers between devices, per_device(): lax.all_to_all(by_owner, ('y', 'zl', 'core'), split_axis=0, concat_axis=0...  5.61 us
  transfers between devices with their start and end apart: 33, of which 16 were waited for; matrix products, arithmetic and copies ran while one was open for 11% of the time, Pallas kernels for 13%

profile of v4, /device:TPU:1, one launch (start us, length us, event | category | flops | bytes accessed | tf_op | source)
XLA Modules:
  0.0 175.5 jit_solution(18179684181903593630)
XLA Ops:
  1.8 4.5 %collective-permute-start.3 = (bf16[128,1792]{1,0:T(8,128)(2,1)S(1)}, bf16[128,1792]{1,0:T(8,128)(2,1)S(1)}, u32[]{:S(2)}, u32[]{:S(2)}) collective-permute-start(bf16[128,1792]{1,0:T(8,128)(2,1)S(1)} %constant_dynamic-slice_fusion), channel_id=1, source_target_pairs={{0,64},{64,0},{1,65},{65,1},{2,66},{66,2},{3,67},{67,3},{4,68},{68... | collective-permute-start | bytes 1376264 | tf_op jit(solution)/shard_map/ppermute | solution.py:21
  9.0 1.5 collective-permute-start.2
  10.6 3.2 %copy.8 = bf16[8,16,8,1024]{3,2,0,1:T(8,128)(2,1)} copy(bf16[8,16,8,1024]{3,2,1,0:T(8,128)(2,1)} %bitcast.26) | data formatting | bytes 4194304 | tf_op jit(solution)/shard_map/reshape | solution.py:260
  15.1 1.5 collective-permute-done.3.block.refs_3_
  17.4 1.7 left_columns.1
  20.4 2.7 %collective-permute-start.7 = (bf16[128,1024]{1,0:T(8,128)(2,1)S(1)}, bf16[128,1024]{1,0:T(8,128)(2,1)S(1)}, u32[]{:S(2)}, u32[]{:S(2)}) collective-permute-start(bf16[128,1024]{1,0:T(8,128)(2,1)S(1)} %slice.16), channel_id=1, source_target_pairs={{0,64},{64,0},{1,65},{65,1},{2,66},{66,2},{3,67},{67,3},{4,68},{68... | collective-permute-start | bytes 786440 | tf_op jit(solution)/shard_map/ppermute | solution.py:21
  25.9 3.7 %collective-permute-done.2.refs_2_ = bf16[128,1792]{1,0:T(8,128)(2,1)} collective-permute-done((bf16[128,1792]{1,0:T(8,128)(2,1)S(1)}, bf16[128,1792]{1,0:T(8,128)(2,1)}, u32[]{:S(2)}, u32[]{:S(2)}) %collective-permute-start.2) | collective-permute-done | bytes 458784 | tf_op jit(solution)/shard_map/ppermute | solution.py:21
  31.1 5.0 %collective-permute-done.4.refs_4_ = bf16[128,768]{1,0:T(8,128)(2,1)} collective-permute-done((bf16[128,768]{1,0:T(8,128)(2,1)}, bf16[128,768]{1,0:T(8,128)(2,1)}, u32[]{:S(2)}, u32[]{:S(2)}) %collective-permute-start.4) | collective-permute-done | bytes 196640 | tf_op jit(solution)/shard_map/ppermute | solution.py:21
  36.1 4.3 %collective-permute-start.10 = (bf16[128,1792]{1,0:T(8,128)(2,1)S(1)}, bf16[128,1792]{1,0:T(8,128)(2,1)}, u32[]{:S(2)}, u32[]{:S(2)}) collective-permute-start(bf16[128,1792]{1,0:T(8,128)(2,1)S(1)} %collective-permute-done.refs_0_), channel_id=1, source_target_pairs={{0,1},{1,0},{2,3},{3,2},{4,5},{5,4},{6,7},{7,6},{8,9},{9,8},{10,11... | collective-permute-start | bytes 1376264 | tf_op jit(solution)/shard_map/ppermute | solution.py:21
  40.4 1.8 %collective-permute-start.11 = (bf16[128,1792]{1,0:T(8,128)(2,1)}, bf16[128,1792]{1,0:T(8,128)(2,1)}, u32[]{:S(2)}, u32[]{:S(2)}) collective-permute-start(bf16[128,1792]{1,0:T(8,128)(2,1)} %collective-permute-done.1.refs_1_), channel_id=1, source_target_pairs={{0,1},{1,0},{2,3},{3,2},{4,5},{5,4},{6,7},{7,6},{8,9},{9,8},{10,11... | collective-permute-start | bytes 1376264 | tf_op jit(solution)/shard_map/ppermute | solution.py:21
  43.0 5.6 %all-to-all-start = ((bf16[16,64,1024]{2,1,0:T(8,128)(2,1)}), bf16[16,64,1024]{2,1,0:T(8,128)(2,1)S(1)}, u32[]{:S(2)}, u32[]{:S(2)}) async-start(bf16[16,64,1024]{2,1,0:T(8,128)(2,1)} %bitcast.25), calls=%async_computation | async-start | bytes 4194304 | tf_op jit(solution)/shard_map/all_to_all | solution.py:261
  49.3 2.0 %collective-permute-done.16.refs_16_ = bf16[128,768]{1,0:T(8,128)(2,1)S(1)} collective-permute-done((bf16[128,768]{1,0:T(8,128)(2,1)}, bf16[128,768]{1,0:T(8,128)(2,1)S(1)}, u32[]{:S(2)}, u32[]{:S(2)}) %collective-permute-start.16) | collective-permute-done | bytes 196640 | tf_op jit(solution)/shard_map/ppermute | solution.py:21
  54.0 16.0 %scores.1 = (bf16[1024,3584]{1,0:T(8,128)(2,1)}, f32[1024,1024]{1,0:T(8,128)}, f32[2,1024]{1,0:T(2,128)}) custom-call(s32[9]{0:T(128)} %stack.36.place, bf16[128,3584]{1,0:T(8,128)(2,1)} %hidden.1, bf16[128,1792]{1,0:T(8,128)(2,1)} %copy-done.7, bf16[128,1792]{1,0:T(8,128)(2,1)} %collective-permute-done.1.refs_1_, ...), custom_call_target="tpu_custom_call" | custom-call | flops 7516192768 | bytes 20971520 | tf_op jit(solution)/shard_map/scores/pallas_call | solution.py:105
  72.1 1.8 %collective-permute-start.22 = (f32[2,1024]{1,0:T(2,128)S(1)}, f32[2,1024]{1,0:T(2,128)S(1)}, u32[]{:S(2)}, u32[]{:S(2)}) collective-permute-start(f32[2,1024]{1,0:T(2,128)S(1)} %add.107), channel_id=1, source_target_pairs={{0,48},{16,0},{32,16},{48,32},{1,49},{17,1},{33,17},{49,33},{2,50}... | collective-permute-start | bytes 24584 | tf_op jit(solution)/shard_map/ppermute | solution.py:21
  74.5 1.7 collective-permute-done.23
  76.2 1.5 collective-permute-done.21
  77.7 3.0 %collective-permute-start.26 = (f32[2,1024]{1,0:T(2,128)S(1)}, f32[2,1024]{1,0:T(2,128)S(1)}, u32[]{:S(2)}, u32[]{:S(2)}) collective-permute-start(f32[2,1024]{1,0:T(2,128)S(1)} %add_add_fusion.2), channel_id=1, source_target_pairs={{0,8},{4,12},{8,0},{12,4},{1,9},{5,13},{9,1},{13,5},{2,10},{6,14},... | collective-permute-start | bytes 24584 | tf_op jit(solution)/shard_map/ppermute | solution.py:21
  83.5 1.8 %collective-permute-done.24 = f32[2,1024]{1,0:T(2,128)S(1)} collective-permute-done((f32[2,1024]{1,0:T(2,128)S(1)}, f32[2,1024]{1,0:T(2,128)S(1)}, u32[]{:S(2)}, u32[]{:S(2)}) %collective-permute-start.24) | collective-permute-done | bytes 8224 | tf_op jit(solution)/shard_map/ppermute | solution.py:21
  85.3 2.0 %collective-permute-start.29 = (f32[2,1024]{1,0:T(2,128)S(1)}, f32[2,1024]{1,0:T(2,128)S(1)}, u32[]{:S(2)}, u32[]{:S(2)}) collective-permute-start(f32[2,1024]{1,0:T(2,128)S(1)} %add_add_fusion.1), channel_id=1, source_target_pairs={{0,64},{2,66},{64,0},{66,2},{1,65},{3,67},{65,1},{67,3},{4,68},{6,... | collective-permute-start | bytes 24584 | tf_op jit(solution)/shard_map/ppermute | solution.py:21
  87.3 1.6 collective-permute-start.28
  89.8 2.8 %collective-permute-done.27 = f32[2,1024]{1,0:T(2,128)S(1)} collective-permute-done((f32[2,1024]{1,0:T(2,128)S(1)}, f32[2,1024]{1,0:T(2,128)S(1)}, u32[]{:S(2)}, u32[]{:S(2)}) %collective-permute-start.27) | collective-permute-done | bytes 8224 | tf_op jit(solution)/shard_map/ppermute | solution.py:21
  92.7 2.2 %copy-done.1 = f32[1024,1024]{1,0:T(8,128)S(1)} copy-done((f32[1024,1024]{1,0:T(8,128)S(1)}, f32[1024,1024]{1,0:T(8,128)}, u32[]{:S(2)}) %copy-start.1) | copy-done | bytes 4194328
  94.9 8.7 %delta_and_share.1 = (bf16[1024,1024]{1,0:T(8,128)(2,1)S(1)}, bf16[1024,1792]{1,0:T(8,128)(2,1)S(1)}) custom-call(s32[1]{0:T(128)} %bitcast.core, f32[1024,1024]{1,0:T(8,128)S(1)} %copy-done.1, bf16[1024,1024]{1,0:T(8,128)(2,1)S(1)} %bitcast.23, f32[8,1024]{1,0:T(8,128)S(1)} %concatenate.3.totals, bf16[3584,1024]{1,0:T(8,128)(2,1)} %weight.3), custom_call_target="tpu_custom_call" | custom-call | flops 3758096384 | bytes 16777216 | tf_op jit(solution)/shard_map/delta_and_share/pallas_call | solution.py:147
  103.6 5.3 %collective-permute-start.30 = (bf16[1024,1792]{1,0:T(8,128)(2,1)S(1)}, bf16[1024,1792]{1,0:T(8,128)(2,1)S(1)}, u32[]{:S(2)}, u32[]{:S(2)}) collective-permute-start(bf16[1024,1792]{1,0:T(8,128)(2,1)S(1)} %get-tuple-element.10), channel_id=1, source_target_pairs={{0,1},{1,0},{2,3},{3,2},{4,5},{5,4},{6,7},{7,6},{8,9},{9,8},{10,11... | collective-permute-start | bytes 11010056 | tf_op jit(solution)/shard_map/ppermute | solution.py:21
  108.9 3.1 %copy-done = bf16[3584,1024]{1,0:T(8,128)(2,1)S(1)} copy-done((bf16[3584,1024]{1,0:T(8,128)(2,1)S(1)}, bf16[3584,1024]{1,0:T(8,128)(2,1)}, u32[]{:S(2)}) %copy-start) | copy-done | bytes 7340056
  111.9 4.9 %own_share.1 = bf16[1024,1792]{1,0:T(8,128)(2,1)S(1)} custom-call(s32[1]{0:T(128)} %bitcast.core, bf16[1024,1024]{1,0:T(8,128)(2,1)S(1)} %get-tuple-element.9.delta, bf16[3584,1024]{1,0:T(8,128)(2,1)S(1)} %copy-done), custom_call_target="tpu_custom_call" | custom-call | flops 3758096384 | bytes 10485760 | tf_op jit(solution)/shard_map/own_share/pallas_call | solution.py:192
  116.9 2.8 %fusion = bf16[128,8,1792]{2,1,0:T(8,128)(2,1)} fusion(bf16[1024,1792]{1,0:T(8,128)(2,1)S(1)} %collective-permute-done.30, bf16[1024,1792]{1,0:T(8,128)(2,1)S(1)} %own_share.1), kind=kLoop, calls=%fused_computation.3 | loop fusion | flops 7340032 | bytes 11010048 | tf_op jit(solution)/shard_map/reshape | solution.py:285
  119.6 5.3 %all-to-all-start.1 = ((bf16[128,8,1792]{2,1,0:T(8,128)(2,1)}), bf16[128,8,1792]{2,1,0:T(8,128)(2,1)}, u32[]{:S(2)}, u32[]{:S(2)}) async-start(bf16[128,8,1792]{2,1,0:T(8,128)(2,1)} %fusion), calls=%async_computation.1 | async-start | bytes 7340032 | tf_op jit(solution)/shard_map/all_to_all | solution.py:284
  124.9 11.2 %convolution_convert_fusion = bf16[3584,1024]{1,0:T(8,128)(2,1)S(1)} fusion(bf16[1024,3584]{1,0:T(8,128)(2,1)} %get-tuple-element.11, bf16[1024,1024]{1,0:T(8,128)(2,1)S(1)} %copy-done.3), kind=kOutput, calls=%fused_computation | convolution fusion | flops 7519862784 | bytes 16777216 | tf_op jit(solution)/shard_map/dot_general | solution.py:287
  136.1 3.0 %copy-done.10 = bf16[3584,1024]{1,0:T(8,128)(2,1)} copy-done((bf16[3584,1024]{1,0:T(8,128)(2,1)}, bf16[3584,1024]{1,0:T(8,128)(2,1)S(1)}, u32[]{:S(2)}) %copy-start.10) | copy-done | bytes 7340056
  139.2 32.7 %all-to-all-done.1 = bf16[128,8,1792]{2,1,0:T(8,128)(2,1)} async-done(((bf16[128,8,1792]{2,1,0:T(8,128)(2,1)}), bf16[128,8,1792]{2,1,0:T(8,128)(2,1)}, u32[]{:S(2)}, u32[]{:S(2)}) %all-to-all-start.1) | async-done | bytes 3670048 | tf_op jit(solution)/shard_map/all_to_all | solution.py:284
  171.8 3.7 %chip_sum.1 = bf16[8,3584]{1,0:T(8,128)(2,1)} custom-call(bf16[64,2,8,1792]{3,2,1,0:T(8,128)(2,1)} %bitcast.13.parts, bf16[8,128]{1,0:T(8,128)(2,1)S(1)} %slice.19.after), custom_call_target="tpu_custom_call" | custom-call | flops 1835008 | bytes 4194304 | tf_op jit(solution)/shard_map/chip_sum/pallas_call | solution.py:231
  (86 shorter events, 22.1 us)
Async XLA Ops:
  1.8 14.8 %collective-permute-start.3 = (bf16[128,1792]{1,0:T(8,128)(2,1)S(1)}, bf16[128,1792]{1,0:T(8,128)(2,1)S(1)}, u32[]{:S(2)}, u32[]{:S(2)}) collective-permute-start(bf16[128,1792]{1,0:T(8,128)(2,1)S(1)} %constant_dynamic-slice_fusion), channel_id=1, source_target_pairs={{0,64},{64,0},{1,65},{65,1},{2,66},{66,2},{3,67},{67,3},{4,68},{68... | collective-permute-start | bytes 1376264 | tf_op jit(solution)/shard_map/ppermute | solution.py:21
  6.4 14.0 %collective-permute-start = (bf16[128,1792]{1,0:T(8,128)(2,1)S(1)}, bf16[128,1792]{1,0:T(8,128)(2,1)S(1)}, u32[]{:S(2)}, u32[]{:S(2)}) collective-permute-start(bf16[128,1792]{1,0:T(8,128)(2,1)S(1)} %constant_dynamic-slice_fusion), channel_id=1, source_target_pairs={{0,16},{16,32},{32,48},{48,0},{1,17},{17,33},{33,49},{49,1},{2,18}... | collective-permute-start | bytes 1376264 | tf_op jit(solution)/shard_map/ppermute | solution.py:21
  7.6 15.5 %collective-permute-start.1 = (bf16[128,1792]{1,0:T(8,128)(2,1)S(1)}, bf16[128,1792]{1,0:T(8,128)(2,1)}, u32[]{:S(2)}, u32[]{:S(2)}) collective-permute-start(bf16[128,1792]{1,0:T(8,128)(2,1)S(1)} %constant_dynamic-slice_fusion), channel_id=1, source_target_pairs={{0,48},{16,0},{32,16},{48,32},{1,49},{17,1},{33,17},{49,33},{2,50}... | collective-permute-start | bytes 1376264 | tf_op jit(solution)/shard_map/ppermute | solution.py:21
  9.0 20.6 %collective-permute-start.2 = (bf16[128,1792]{1,0:T(8,128)(2,1)S(1)}, bf16[128,1792]{1,0:T(8,128)(2,1)}, u32[]{:S(2)}, u32[]{:S(2)}) collective-permute-start(bf16[128,1792]{1,0:T(8,128)(2,1)S(1)} %constant_dynamic-slice_fusion), channel_id=1, source_target_pairs={{0,32},{16,48},{32,0},{48,16},{1,33},{17,49},{33,1},{49,17},{2,34}... | collective-permute-start | bytes 1376264 | tf_op jit(solution)/shard_map/ppermute | solution.py:21
  19.1 17.0 %collective-permute-start.4 = (bf16[128,768]{1,0:T(8,128)(2,1)}, bf16[128,768]{1,0:T(8,128)(2,1)}, u32[]{:S(2)}, u32[]{:S(2)}) collective-permute-start(bf16[128,768]{1,0:T(8,128)(2,1)} %left_columns.1), channel_id=1, source_target_pairs={{0,16},{16,32},{32,48},{48,0},{1,17},{17,33},{33,49},{49,1},{2,18}... | collective-permute-start | bytes 589832 | tf_op jit(solution)/shard_map/ppermute | solution.py:21
  20.4 21.8 %collective-permute-start.7 = (bf16[128,1024]{1,0:T(8,128)(2,1)S(1)}, bf16[128,1024]{1,0:T(8,128)(2,1)S(1)}, u32[]{:S(2)}, u32[]{:S(2)}) collective-permute-start(bf16[128,1024]{1,0:T(8,128)(2,1)S(1)} %slice.16), channel_id=1, source_target_pairs={{0,64},{64,0},{1,65},{65,1},{2,66},{66,2},{3,67},{67,3},{4,68},{68... | collective-permute-start | bytes 786440 | tf_op jit(solution)/shard_map/ppermute | solution.py:21
  24.1 18.2 %collective-permute-start.8 = (bf16[128,1024]{1,0:T(8,128)(2,1)S(1)}, bf16[128,1024]{1,0:T(8,128)(2,1)S(1)}, u32[]{:S(2)}, u32[]{:S(2)}) collective-permute-start(bf16[128,1024]{1,0:T(8,128)(2,1)S(1)} %slice.17), channel_id=1, source_target_pairs={{0,64},{64,0},{1,65},{65,1},{2,66},{66,2},{3,67},{67,3},{4,68},{68... | collective-permute-start | bytes 786440 | tf_op jit(solution)/shard_map/ppermute | solution.py:21
  24.5 11.6 %collective-permute-start.5 = (bf16[128,768]{1,0:T(8,128)(2,1)}, bf16[128,768]{1,0:T(8,128)(2,1)}, u32[]{:S(2)}, u32[]{:S(2)}) collective-permute-start(bf16[128,768]{1,0:T(8,128)(2,1)} %left_columns.1), channel_id=1, source_target_pairs={{0,48},{16,0},{32,16},{48,32},{1,49},{17,1},{33,17},{49,33},{2,50}... | collective-permute-start | bytes 589832 | tf_op jit(solution)/shard_map/ppermute | solution.py:21
  29.6 10.8 %collective-permute-start.6 = (bf16[128,768]{1,0:T(8,128)(2,1)}, bf16[128,768]{1,0:T(8,128)(2,1)S(1)}, u32[]{:S(2)}, u32[]{:S(2)}) collective-permute-start(bf16[128,768]{1,0:T(8,128)(2,1)} %left_columns.1), channel_id=1, source_target_pairs={{0,32},{16,48},{32,0},{48,16},{1,33},{17,49},{33,1},{49,17},{2,34}... | collective-permute-start | bytes 589832 | tf_op jit(solution)/shard_map/ppermute | solution.py:21
  36.1 12.5 %collective-permute-start.9 = (bf16[128,1024]{1,0:T(8,128)(2,1)S(1)}, bf16[128,1024]{1,0:T(8,128)(2,1)}, u32[]{:S(2)}, u32[]{:S(2)}) collective-permute-start(bf16[128,1024]{1,0:T(8,128)(2,1)S(1)} %slice.18), channel_id=1, source_target_pairs={{0,64},{64,0},{1,65},{65,1},{2,66},{66,2},{3,67},{67,3},{4,68},{68... | collective-permute-start | bytes 786440 | tf_op jit(solution)/shard_map/ppermute | solution.py:21
  36.1 15.4 %collective-permute-start.10 = (bf16[128,1792]{1,0:T(8,128)(2,1)S(1)}, bf16[128,1792]{1,0:T(8,128)(2,1)}, u32[]{:S(2)}, u32[]{:S(2)}) collective-permute-start(bf16[128,1792]{1,0:T(8,128)(2,1)S(1)} %collective-permute-done.refs_0_), channel_id=1, source_target_pairs={{0,1},{1,0},{2,3},{3,2},{4,5},{5,4},{6,7},{7,6},{8,9},{9,8},{10,11... | collective-permute-start | bytes 1376264 | tf_op jit(solution)/shard_map/ppermute | solution.py:21
  40.4 11.4 %collective-permute-start.11 = (bf16[128,1792]{1,0:T(8,128)(2,1)}, bf16[128,1792]{1,0:T(8,128)(2,1)}, u32[]{:S(2)}, u32[]{:S(2)}) collective-permute-start(bf16[128,1792]{1,0:T(8,128)(2,1)} %collective-permute-done.1.refs_1_), channel_id=1, source_target_pairs={{0,1},{1,0},{2,3},{3,2},{4,5},{5,4},{6,7},{7,6},{8,9},{9,8},{10,11... | collective-permute-start | bytes 1376264 | tf_op jit(solution)/shard_map/ppermute | solution.py:21
  42.2 6.6 %collective-permute-start.14 = (bf16[128,768]{1,0:T(8,128)(2,1)}, bf16[128,768]{1,0:T(8,128)(2,1)}, u32[]{:S(2)}, u32[]{:S(2)}) collective-permute-start(bf16[128,768]{1,0:T(8,128)(2,1)} %collective-permute-done.4.refs_4_), channel_id=1, source_target_pairs={{0,1},{1,0},{2,3},{3,2},{4,5},{5,4},{6,7},{7,6},{8,9},{9,8},{10,11... | collective-permute-start | bytes 589832 | tf_op jit(solution)/shard_map/ppermute | solution.py:21
  42.3 6.9 %collective-permute-start.15 = (bf16[128,768]{1,0:T(8,128)(2,1)}, bf16[128,768]{1,0:T(8,128)(2,1)}, u32[]{:S(2)}, u32[]{:S(2)}) collective-permute-start(bf16[128,768]{1,0:T(8,128)(2,1)} %collective-permute-done.5.refs_5_), channel_id=1, source_target_pairs={{0,1},{1,0},{2,3},{3,2},{4,5},{5,4},{6,7},{7,6},{8,9},{9,8},{10,11... | collective-permute-start | bytes 589832 | tf_op jit(solution)/shard_map/ppermute | solution.py:21
  43.0 49.7 %all-to-all-start = ((bf16[16,64,1024]{2,1,0:T(8,128)(2,1)}), bf16[16,64,1024]{2,1,0:T(8,128)(2,1)S(1)}, u32[]{:S(2)}, u32[]{:S(2)}) async-start(bf16[16,64,1024]{2,1,0:T(8,128)(2,1)} %bitcast.25), calls=%async_computation | async-start | bytes 4194304 | tf_op jit(solution)/shard_map/all_to_all | solution.py:261
  48.6 4.2 %collective-permute-start.12 = (bf16[128,1792]{1,0:T(8,128)(2,1)}, bf16[128,1792]{1,0:T(8,128)(2,1)}, u32[]{:S(2)}, u32[]{:S(2)}) collective-permute-start(bf16[128,1792]{1,0:T(8,128)(2,1)} %collective-permute-done.2.refs_2_), channel_id=1, source_target_pairs={{0,1},{1,0},{2,3},{3,2},{4,5},{5,4},{6,7},{7,6},{8,9},{9,8},{10,11... | collective-permute-start | bytes 1376264 | tf_op jit(solution)/shard_map/ppermute | solution.py:21
  48.8 2.5 %collective-permute-start.16 = (bf16[128,768]{1,0:T(8,128)(2,1)}, bf16[128,768]{1,0:T(8,128)(2,1)S(1)}, u32[]{:S(2)}, u32[]{:S(2)}) collective-permute-start(bf16[128,768]{1,0:T(8,128)(2,1)} %copy-done.13), channel_id=1, source_target_pairs={{0,1},{1,0},{2,3},{3,2},{4,5},{5,4},{6,7},{7,6},{8,9},{9,8},{10,11... | collective-permute-start | bytes 589832 | tf_op jit(solution)/shard_map/ppermute | solution.py:21
  49.2 3.6 %collective-permute-start.13 = (bf16[128,1792]{1,0:T(8,128)(2,1)S(1)}, bf16[128,1792]{1,0:T(8,128)(2,1)}, u32[]{:S(2)}, u32[]{:S(2)}) collective-permute-start(bf16[128,1792]{1,0:T(8,128)(2,1)S(1)} %copy-done.6), channel_id=1, source_target_pairs={{0,1},{1,0},{2,3},{3,2},{4,5},{5,4},{6,7},{7,6},{8,9},{9,8},{10,11... | collective-permute-start | bytes 1376264 | tf_op jit(solution)/shard_map/ppermute | solution.py:21
  51.3 1.7 collective-permute-start.17
  51.4 2.1 %collective-permute-start.18 = (bf16[128,1024]{1,0:T(8,128)(2,1)}, bf16[128,1024]{1,0:T(8,128)(2,1)}, u32[]{:S(2)}, u32[]{:S(2)}) collective-permute-start(bf16[128,1024]{1,0:T(8,128)(2,1)} %copy-done.12), channel_id=1, source_target_pairs={{0,1},{1,0},{2,3},{3,2},{4,5},{5,4},{6,7},{7,6},{8,9},{9,8},{10,11... | collective-permute-start | bytes 786440 | tf_op jit(solution)/shard_map/ppermute | solution.py:21
  51.8 2.1 %collective-permute-start.19 = (bf16[128,1024]{1,0:T(8,128)(2,1)}, bf16[128,1024]{1,0:T(8,128)(2,1)}, u32[]{:S(2)}, u32[]{:S(2)}) collective-permute-start(bf16[128,1024]{1,0:T(8,128)(2,1)} %collective-permute-done.9.refs_9_), channel_id=1, source_target_pairs={{0,1},{1,0},{2,3},{3,2},{4,5},{5,4},{6,7},{7,6},{8,9},{9,8},{10,11... | collective-permute-start | bytes 786440 | tf_op jit(solution)/shard_map/ppermute | solution.py:21
  72.1 4.0 %collective-permute-start.23 = (f32[2,1024]{1,0:T(2,128)S(1)}, f32[2,1024]{1,0:T(2,128)S(1)}, u32[]{:S(2)}, u32[]{:S(2)}) collective-permute-start(f32[2,1024]{1,0:T(2,128)S(1)} %add.107), channel_id=1, source_target_pairs={{0,32},{16,48},{32,0},{48,16},{1,33},{17,49},{33,1},{49,17},{2,34}... | collective-permute-start | bytes 24584 | tf_op jit(solution)/shard_map/ppermute | solution.py:21
  72.1 4.0 %collective-permute-start.22 = (f32[2,1024]{1,0:T(2,128)S(1)}, f32[2,1024]{1,0:T(2,128)S(1)}, u32[]{:S(2)}, u32[]{:S(2)}) collective-permute-start(f32[2,1024]{1,0:T(2,128)S(1)} %add.107), channel_id=1, source_target_pairs={{0,48},{16,0},{32,16},{48,32},{1,49},{17,1},{33,17},{49,33},{2,50}... | collective-permute-start | bytes 24584 | tf_op jit(solution)/shard_map/ppermute | solution.py:21
  74.0 3.7 %collective-permute-start.21 = (f32[2,1024]{1,0:T(2,128)S(1)}, f32[2,1024]{1,0:T(2,128)S(1)}, u32[]{:S(2)}, u32[]{:S(2)}) collective-permute-start(f32[2,1024]{1,0:T(2,128)S(1)} %add.107), channel_id=1, source_target_pairs={{0,16},{16,32},{32,48},{48,0},{1,17},{17,33},{33,49},{49,1},{2,18}... | collective-permute-start | bytes 24584 | tf_op jit(solution)/shard_map/ppermute | solution.py:21
  77.7 4.5 %collective-permute-start.26 = (f32[2,1024]{1,0:T(2,128)S(1)}, f32[2,1024]{1,0:T(2,128)S(1)}, u32[]{:S(2)}, u32[]{:S(2)}) collective-permute-start(f32[2,1024]{1,0:T(2,128)S(1)} %add_add_fusion.2), channel_id=1, source_target_pairs={{0,8},{4,12},{8,0},{12,4},{1,9},{5,13},{9,1},{13,5},{2,10},{6,14},... | collective-permute-start | bytes 24584 | tf_op jit(solution)/shard_map/ppermute | solution.py:21
  80.7 2.8 %collective-permute-start.25 = (f32[2,1024]{1,0:T(2,128)S(1)}, f32[2,1024]{1,0:T(2,128)S(1)}, u32[]{:S(2)}, u32[]{:S(2)}) collective-permute-start(f32[2,1024]{1,0:T(2,128)S(1)} %add_add_fusion.2), channel_id=1, source_target_pairs={{0,12},{4,0},{8,4},{12,8},{1,13},{5,1},{9,5},{13,9},{2,14},{6,2},{... | collective-permute-start | bytes 24584 | tf_op jit(solution)/shard_map/ppermute | solution.py:21
  81.6 3.7 %collective-permute-start.24 = (f32[2,1024]{1,0:T(2,128)S(1)}, f32[2,1024]{1,0:T(2,128)S(1)}, u32[]{:S(2)}, u32[]{:S(2)}) collective-permute-start(f32[2,1024]{1,0:T(2,128)S(1)} %add_add_fusion.2), channel_id=1, source_target_pairs={{0,4},{4,8},{8,12},{12,0},{1,5},{5,9},{9,13},{13,1},{2,6},{6,10},{... | collective-permute-start | bytes 24584 | tf_op jit(solution)/shard_map/ppermute | solution.py:21
  85.3 4.1 %collective-permute-start.29 = (f32[2,1024]{1,0:T(2,128)S(1)}, f32[2,1024]{1,0:T(2,128)S(1)}, u32[]{:S(2)}, u32[]{:S(2)}) collective-permute-start(f32[2,1024]{1,0:T(2,128)S(1)} %add_add_fusion.1), channel_id=1, source_target_pairs={{0,64},{2,66},{64,0},{66,2},{1,65},{3,67},{65,1},{67,3},{4,68},{6,... | collective-permute-start | bytes 24584 | tf_op jit(solution)/shard_map/ppermute | solution.py:21
  87.3 2.5 %collective-permute-start.28 = (f32[2,1024]{1,0:T(2,128)S(1)}, f32[2,1024]{1,0:T(2,128)S(1)}, u32[]{:S(2)}, u32[]{:S(2)}) collective-permute-start(f32[2,1024]{1,0:T(2,128)S(1)} %add_add_fusion.1), channel_id=1, source_target_pairs={{0,66},{2,0},{64,2},{66,64},{1,67},{3,1},{65,3},{67,65},{4,70},{6,... | collective-permute-start | bytes 24584 | tf_op jit(solution)/shard_map/ppermute | solution.py:21
  89.0 3.7 %collective-permute-start.27 = (f32[2,1024]{1,0:T(2,128)S(1)}, f32[2,1024]{1,0:T(2,128)S(1)}, u32[]{:S(2)}, u32[]{:S(2)}) collective-permute-start(f32[2,1024]{1,0:T(2,128)S(1)} %add_add_fusion.1), channel_id=1, source_target_pairs={{0,2},{2,64},{64,66},{66,0},{1,3},{3,65},{65,67},{67,1},{4,6},{6,6... | collective-permute-start | bytes 24584 | tf_op jit(solution)/shard_map/ppermute | solution.py:21
  103.6 13.3 %collective-permute-start.30 = (bf16[1024,1792]{1,0:T(8,128)(2,1)S(1)}, bf16[1024,1792]{1,0:T(8,128)(2,1)S(1)}, u32[]{:S(2)}, u32[]{:S(2)}) collective-permute-start(bf16[1024,1792]{1,0:T(8,128)(2,1)S(1)} %get-tuple-element.10), channel_id=1, source_target_pairs={{0,1},{1,0},{2,3},{3,2},{4,5},{5,4},{6,7},{7,6},{8,9},{9,8},{10,11... | collective-permute-start | bytes 11010056 | tf_op jit(solution)/shard_map/ppermute | solution.py:21
  119.6 52.2 %all-to-all-start.1 = ((bf16[128,8,1792]{2,1,0:T(8,128)(2,1)}), bf16[128,8,1792]{2,1,0:T(8,128)(2,1)}, u32[]{:S(2)}, u32[]{:S(2)}) async-start(bf16[128,8,1792]{2,1,0:T(8,128)(2,1)} %fusion), calls=%async_computation.1 | async-start | bytes 7340032 | tf_op jit(solution)/shard_map/all_to_all | solution.py:284
  (16 other events, 159.7 us)

commit v5 on v4

--- a/solution.py
+++ b/solution.py
@@ -129,16 +129,37 @@
     )(place, hidden, *own, *other, weight, teacher_sum)
 
 
-def delta_kernel(core, capped, teacher, totals, weight, delta, share):
+def delta_kernel(core, capped, teacher, totals, weight, delta, share, own, weight_v, sem):
+    half = weight_v.shape[0]
+    at = pl.ds(pl.multiple_of((1 - core[0]) * half, half), half)
+    load = pltpu.make_async_copy(weight.at[at, :], weight_v, sem.at[0])
+    at = pl.ds(pl.multiple_of(core[0] * half, half), half)
+    ahead = pltpu.make_async_copy(weight.at[at, :], own, sem.at[1])
+    i = pl.program_id(0)
+
+    @pl.when(i == 0)
+    def _():
+        load.start()
+        ahead.start()
+
     scale = (8192.0 / totals[...]).T
     cap = capped[...]
     student = jnp.exp(15.0 * cap) * scale[:, 0:1]
     target = jnp.exp(teacher[...].astype(F32) * 0.5) * scale[:, 1:2]
     d = ((student - target) * (1.0 - cap * cap)).astype(BF)
     delta[...] = d
+
+    @pl.when(i == 0)
+    def _():
+        load.wait()
+
     share[...] = lax.dot_general(
-        d, weight[...], (((1,), (1,)), ((), ())), preferred_element_type=F32
+        d, weight_v[...], (((1,), (1,)), ((), ())), preferred_element_type=F32
     ).astype(BF)
+
+    @pl.when(i == pl.num_programs(0) - 1)
+    def _():
+        ahead.wait()
 
 
 def delta_and_share(core, capped, teacher, totals, weight):
@@ -154,57 +175,47 @@
                 block((tile, cols), lambda i, core: (i, 0)),
                 block((tile, cols), lambda i, core: (i, 0)),
                 block((8, tile), lambda i, core: (0, i)),
-                block((half, cols), lambda i, core: (1 - core[0], 0)),
+                ANY,
             ],
             out_specs=[
                 block((tile, cols), lambda i, core: (i, 0)),
                 block((tile, half), lambda i, core: (i, 0)),
+                ANY,
             ],
+            scratch_shapes=[pltpu.VMEM((half, cols), BF), pltpu.SemaphoreType.DMA((2,))],
         ),
         out_shape=(
             jax.ShapeDtypeStruct((rows, cols), BF),
             jax.ShapeDtypeStruct((rows, half), BF),
-        ),
-        compiler_params=pltpu.CompilerParams(vmem_limit_bytes=40 << 20),
+            pltpu.VMEM((half, cols), BF),
+        ),
+        compiler_params=pltpu.CompilerParams(vmem_limit_bytes=36 << 20),
         cost_estimate=pl.CostEstimate(
             flops=2 * rows * half * cols, bytes_accessed=16 << 20, transcendentals=2 * rows * cols
         ),
     )(core, capped, teacher, totals, weight)
 
 
-def share_kernel(core, delta, weight, share, weight_v, sem):
-    half = weight_v.shape[0]
-    at = pl.ds(pl.multiple_of(core[0] * half, half), half)
-    load = pltpu.make_async_copy(weight.at[at, :], weight_v, sem)
-
-    @pl.when(pl.program_id(0) == 0)
-    def _():
-        load.start()
-        load.wait()
-
+def share_kernel(delta, weight, share):
     share[...] = lax.dot_general(
-        delta[...], weight_v[...], (((1,), (1,)), ((), ())), preferred_element_type=F32
+        delta[...], weight[...], (((1,), (1,)), ((), ())), preferred_element_type=F32
     ).astype(BF)
 
 
-def own_share(core, delta, weight):
-    (rows, cols), half, tile = delta.shape, weight.shape[0] // 2, 256
+def own_share(delta, weight):
+    (rows, cols), half, tile = delta.shape, weight.shape[0], 256
     return pl.pallas_call(
         share_kernel,
         name="own_share",
-        grid_spec=pltpu.PrefetchScalarGridSpec(
-            num_scalar_prefetch=1,
-            grid=(rows // tile,),
-            in_specs=[pl.BlockSpec((tile, cols), lambda i, core: (i, 0)), ANY],
-            out_specs=pl.BlockSpec((tile, half), lambda i, core: (i, 0)),
-            scratch_shapes=[pltpu.VMEM((half, cols), BF), pltpu.SemaphoreType.DMA],
-        ),
+        grid=(rows // tile,),
+        in_specs=[pl.BlockSpec((tile, cols), lambda i: (i, 0)), VMEM],
+        out_specs=pl.BlockSpec((tile, half), lambda i: (i, 0)),
         out_shape=jax.ShapeDtypeStruct((rows, half), BF),
-        compiler_params=pltpu.CompilerParams(vmem_limit_bytes=40 << 20),
+        compiler_params=pltpu.CompilerParams(vmem_limit_bytes=36 << 20),
         cost_estimate=pl.CostEstimate(
             flops=2 * rows * half * cols, bytes_accessed=10 << 20, transcendentals=0
         ),
-    )(core, delta, weight)
+    )(delta, weight)
 
 
 def chip_sum_kernel(parts, after, out, total):
@@ -278,8 +289,8 @@
     totals = jnp.concatenate([total(sums), jnp.ones((6, rows), F32)])
 
     which = core[None].astype(jnp.int32)
-    delta, give = delta_and_share(which, capped, teacher, totals, head_weight)
-    keep = own_share(which, delta, head_weight)
+    delta, give, own_weight = delta_and_share(which, capped, teacher, totals, head_weight)
+    keep = own_share(delta, own_weight)
     chip = (keep.astype(F32) + swap(give).astype(F32)).astype(BF)
     parts = lax.all_to_all(
         chip.reshape(128, rows // 128, half), EVERY, split_axis=0, concat_axis=0, tiled=True

time: 176 us -> 174 us (0.989)
  local copies, waits for them, and re-layouts: 16.6 us -> 13.5 us
    unnamed x30 -> x28, local copies, waits for them, and re-layouts: 9.46 us -> 6.37 us
  transfers between devices with their start and end apart: 33 -> 33, of which waited for: 16 -> 17; matrix products, arithmetic and copies ran while one was open for 11% -> 11% of each run, Pallas kernels for 13% -> 13%
where the time goes in v5:
time: 174 us; the launch traced here: 173 us
  waiting for transfers between devices  58.7 us (34%)
  starting transfers between devices  49.5 us (28%)
  Pallas kernels  34.7 us (20%)
  local copies, waits for them, and re-layouts  13.5 us (8%)
  matrix products  11.2 us (6%)
  other arithmetic  4.8 us (3%)
    ppermute x31, starting transfers between devices, shift(): return lax.ppermute(v, axis, [(i, (i + step) % size) for i in range(size)])  39 us
    all_to_all x1, waiting for transfers between devices, per_device(): lax.all_to_all(chip.reshape(128, rows // 128, half), EVERY, split_axis=0,...  32.7 us
    ppermute x31, waiting for transfers between devices, shift(): return lax.ppermute(v, axis, [(i, (i + step) % size) for i in range(size)])  26 us
    pallas_call x1, Pallas kernels, scores(): pl.pallas_call(functools.partial(scores_kernel, tile), name='scores', out...  16 us
    dot_general x1, matrix products, per_device(): lax.dot_general(gathered, delta, (((0,), (0,)), ((), ())), preferred_elem...  11.2 us
    pallas_call x1, Pallas kernels, delta_and_share(): pl.pallas_call(delta_kernel, name='delta_and_share', grid_spec=pltpu.Pref...  8.59 us
    unnamed x28, local copies, waits for them, and re-layouts  6.37 us
    all_to_all x1, starting transfers between devices, per_device(): lax.all_to_all(by_owner, ('y', 'zl', 'core'), split_axis=0, concat_axis=0...  5.61 us
  transfers between devices with their start and end apart: 33, of which 17 were waited for; matrix products, arithmetic and copies ran while one was open for 11% of the time, Pallas kernels for 13%

profile of v5, /device:TPU:1, one launch (start us, length us, event | category | flops | bytes accessed | tf_op | source)
XLA Modules:
  0.0 173.2 jit_solution(5481974543361435996)
XLA Ops:
  1.8 4.5 %collective-permute-start.3 = (bf16[128,1792]{1,0:T(8,128)(2,1)S(1)}, bf16[128,1792]{1,0:T(8,128)(2,1)S(1)}, u32[]{:S(2)}, u32[]{:S(2)}) collective-permute-start(bf16[128,1792]{1,0:T(8,128)(2,1)S(1)} %constant_dynamic-slice_fusion), channel_id=1, source_target_pairs={{0,64},{64,0},{1,65},{65,1},{2,66},{66,2},{3,67},{67,3},{4,68},{68... | collective-permute-start | bytes 1376264 | tf_op jit(solution)/shard_map/ppermute | solution.py:21
  9.0 1.5 collective-permute-start.2
  10.6 3.2 %copy.8 = bf16[8,16,8,1024]{3,2,0,1:T(8,128)(2,1)} copy(bf16[8,16,8,1024]{3,2,1,0:T(8,128)(2,1)} %bitcast.26) | data formatting | bytes 4194304 | tf_op jit(solution)/shard_map/reshape | solution.py:271
  15.1 1.5 collective-permute-done.3.block.refs_3_
  17.4 1.7 left_columns.1
  20.4 2.7 %collective-permute-start.7 = (bf16[128,1024]{1,0:T(8,128)(2,1)S(1)}, bf16[128,1024]{1,0:T(8,128)(2,1)S(1)}, u32[]{:S(2)}, u32[]{:S(2)}) collective-permute-start(bf16[128,1024]{1,0:T(8,128)(2,1)S(1)} %slice.16), channel_id=1, source_target_pairs={{0,64},{64,0},{1,65},{65,1},{2,66},{66,2},{3,67},{67,3},{4,68},{68... | collective-permute-start | bytes 786440 | tf_op jit(solution)/shard_map/ppermute | solution.py:21
  24.5 1.5 collective-permute-start.5
  25.9 3.7 %collective-permute-done.2.refs_2_ = bf16[128,1792]{1,0:T(8,128)(2,1)} collective-permute-done((bf16[128,1792]{1,0:T(8,128)(2,1)S(1)}, bf16[128,1792]{1,0:T(8,128)(2,1)}, u32[]{:S(2)}, u32[]{:S(2)}) %collective-permute-start.2) | collective-permute-done | bytes 458784 | tf_op jit(solution)/shard_map/ppermute | solution.py:21
  31.1 5.0 %collective-permute-done.4.refs_4_ = bf16[128,768]{1,0:T(8,128)(2,1)} collective-permute-done((bf16[128,768]{1,0:T(8,128)(2,1)}, bf16[128,768]{1,0:T(8,128)(2,1)}, u32[]{:S(2)}, u32[]{:S(2)}) %collective-permute-start.4) | collective-permute-done | bytes 196640 | tf_op jit(solution)/shard_map/ppermute | solution.py:21
  36.1 4.3 %collective-permute-start.10 = (bf16[128,1792]{1,0:T(8,128)(2,1)S(1)}, bf16[128,1792]{1,0:T(8,128)(2,1)}, u32[]{:S(2)}, u32[]{:S(2)}) collective-permute-start(bf16[128,1792]{1,0:T(8,128)(2,1)S(1)} %collective-permute-done.refs_0_), channel_id=1, source_target_pairs={{0,1},{1,0},{2,3},{3,2},{4,5},{5,4},{6,7},{7,6},{8,9},{9,8},{10,11... | collective-permute-start | bytes 1376264 | tf_op jit(solution)/shard_map/ppermute | solution.py:21
  40.4 1.8 %collective-permute-start.11 = (bf16[128,1792]{1,0:T(8,128)(2,1)}, bf16[128,1792]{1,0:T(8,128)(2,1)}, u32[]{:S(2)}, u32[]{:S(2)}) collective-permute-start(bf16[128,1792]{1,0:T(8,128)(2,1)} %collective-permute-done.1.refs_1_), channel_id=1, source_target_pairs={{0,1},{1,0},{2,3},{3,2},{4,5},{5,4},{6,7},{7,6},{8,9},{9,8},{10,11... | collective-permute-start | bytes 1376264 | tf_op jit(solution)/shard_map/ppermute | solution.py:21
  43.0 5.6 %all-to-all-start = ((bf16[16,64,1024]{2,1,0:T(8,128)(2,1)}), bf16[16,64,1024]{2,1,0:T(8,128)(2,1)S(1)}, u32[]{:S(2)}, u32[]{:S(2)}) async-start(bf16[16,64,1024]{2,1,0:T(8,128)(2,1)} %bitcast.25), calls=%async_computation | async-start | bytes 4194304 | tf_op jit(solution)/shard_map/all_to_all | solution.py:272
  49.3 2.0 %collective-permute-done.16.refs_16_ = bf16[128,768]{1,0:T(8,128)(2,1)S(1)} collective-permute-done((bf16[128,768]{1,0:T(8,128)(2,1)}, bf16[128,768]{1,0:T(8,128)(2,1)S(1)}, u32[]{:S(2)}, u32[]{:S(2)}) %collective-permute-start.16) | collective-permute-done | bytes 196640 | tf_op jit(solution)/shard_map/ppermute | solution.py:21
  53.9 16.0 %scores.1 = (bf16[1024,3584]{1,0:T(8,128)(2,1)}, f32[1024,1024]{1,0:T(8,128)}, f32[2,1024]{1,0:T(2,128)}) custom-call(s32[9]{0:T(128)} %stack.36.place, bf16[128,3584]{1,0:T(8,128)(2,1)} %hidden.1, bf16[128,1792]{1,0:T(8,128)(2,1)} %copy-done.6, bf16[128,1792]{1,0:T(8,128)(2,1)} %collective-permute-done.1.refs_1_, ...), custom_call_target="tpu_custom_call" | custom-call | flops 7516192768 | bytes 20971520 | tf_op jit(solution)/shard_map/scores/pallas_call | solution.py:105
  72.2 1.8 %collective-permute-start.22 = (f32[2,1024]{1,0:T(2,128)S(1)}, f32[2,1024]{1,0:T(2,128)S(1)}, u32[]{:S(2)}, u32[]{:S(2)}) collective-permute-start(f32[2,1024]{1,0:T(2,128)S(1)} %add.107), channel_id=1, source_target_pairs={{0,48},{16,0},{32,16},{48,32},{1,49},{17,1},{33,17},{49,33},{2,50}... | collective-permute-start | bytes 24584 | tf_op jit(solution)/shard_map/ppermute | solution.py:21
  74.5 1.6 collective-permute-done.23
  76.2 1.6 collective-permute-done.21
  77.7 3.0 %collective-permute-start.26 = (f32[2,1024]{1,0:T(2,128)S(1)}, f32[2,1024]{1,0:T(2,128)S(1)}, u32[]{:S(2)}, u32[]{:S(2)}) collective-permute-start(f32[2,1024]{1,0:T(2,128)S(1)} %add_add_fusion.2), channel_id=1, source_target_pairs={{0,8},{4,12},{8,0},{12,4},{1,9},{5,13},{9,1},{13,5},{2,10},{6,14},... | collective-permute-start | bytes 24584 | tf_op jit(solution)/shard_map/ppermute | solution.py:21
  83.5 1.8 %collective-permute-done.24 = f32[2,1024]{1,0:T(2,128)S(1)} collective-permute-done((f32[2,1024]{1,0:T(2,128)S(1)}, f32[2,1024]{1,0:T(2,128)S(1)}, u32[]{:S(2)}, u32[]{:S(2)}) %collective-permute-start.24) | collective-permute-done | bytes 8224 | tf_op jit(solution)/shard_map/ppermute | solution.py:21
  85.3 2.0 %collective-permute-start.29 = (f32[2,1024]{1,0:T(2,128)S(1)}, f32[2,1024]{1,0:T(2,128)S(1)}, u32[]{:S(2)}, u32[]{:S(2)}) collective-permute-start(f32[2,1024]{1,0:T(2,128)S(1)} %add_add_fusion.1), channel_id=1, source_target_pairs={{0,64},{2,66},{64,0},{66,2},{1,65},{3,67},{65,1},{67,3},{4,68},{6,... | collective-permute-start | bytes 24584 | tf_op jit(solution)/shard_map/ppermute | solution.py:21
  87.4 1.6 collective-permute-start.28
  89.9 2.8 %collective-permute-done.27 = f32[2,1024]{1,0:T(2,128)S(1)} collective-permute-done((f32[2,1024]{1,0:T(2,128)S(1)}, f32[2,1024]{1,0:T(2,128)S(1)}, u32[]{:S(2)}, u32[]{:S(2)}) %collective-permute-start.27) | collective-permute-done | bytes 8224 | tf_op jit(solution)/shard_map/ppermute | solution.py:21
  92.8 2.2 %copy-done = f32[1024,1024]{1,0:T(8,128)S(1)} copy-done((f32[1024,1024]{1,0:T(8,128)S(1)}, f32[1024,1024]{1,0:T(8,128)}, u32[]{:S(2)}) %copy-start) | copy-done | bytes 4194328
  94.9 8.6 %delta_and_share.1 = (bf16[1024,1024]{1,0:T(8,128)(2,1)S(1)}, bf16[1024,1792]{1,0:T(8,128)(2,1)S(1)}, bf16[1792,1024]{1,0:T(8,128)(2,1)S(1)}) custom-call(s32[1]{0:T(128)} %bitcast.core, f32[1024,1024]{1,0:T(8,128)S(1)} %copy-done, bf16[1024,1024]{1,0:T(8,128)(2,1)S(1)} %bitcast.23, f32[8,1024]{1,0:T(8,128)S(1)} %concatenate.3.totals, bf16[3584,1024]{1,0:T(8,128)(2,1)} %weight.1), custom_call_target="tpu_custom_call" | custom-call | flops 3758096384 | bytes 16777216 | tf_op jit(solution)/shard_map/delta_and_share/pallas_call | solution.py:168
  103.5 5.3 %collective-permute-start.30 = (bf16[1024,1792]{1,0:T(8,128)(2,1)S(1)}, bf16[1024,1792]{1,0:T(8,128)(2,1)S(1)}, u32[]{:S(2)}, u32[]{:S(2)}) collective-permute-start(bf16[1024,1792]{1,0:T(8,128)(2,1)S(1)} %get-tuple-element.12), channel_id=1, source_target_pairs={{0,1},{1,0},{2,3},{3,2},{4,5},{5,4},{6,7},{7,6},{8,9},{9,8},{10,11... | collective-permute-start | bytes 11010056 | tf_op jit(solution)/shard_map/ppermute | solution.py:21
  108.8 4.6 %own_share.1 = bf16[1024,1792]{1,0:T(8,128)(2,1)S(1)} custom-call(bf16[1024,1024]{1,0:T(8,128)(2,1)S(1)} %get-tuple-element.10.delta, bf16[1792,1024]{1,0:T(8,128)(2,1)S(1)} %get-tuple-element.11.weight), custom_call_target="tpu_custom_call" | custom-call | flops 3758096384 | bytes 10485760 | tf_op jit(solution)/shard_map/own_share/pallas_call | solution.py:207
  114.9 2.8 %fusion = bf16[128,8,1792]{2,1,0:T(8,128)(2,1)} fusion(bf16[1024,1792]{1,0:T(8,128)(2,1)S(1)} %collective-permute-done.30, bf16[1024,1792]{1,0:T(8,128)(2,1)S(1)} %own_share.1), kind=kLoop, calls=%fused_computation.3 | loop fusion | flops 7340032 | bytes 11010048 | tf_op jit(solution)/shard_map/reshape | solution.py:296
  117.6 5.0 %all-to-all-start.1 = ((bf16[128,8,1792]{2,1,0:T(8,128)(2,1)}), bf16[128,8,1792]{2,1,0:T(8,128)(2,1)}, u32[]{:S(2)}, u32[]{:S(2)}) async-start(bf16[128,8,1792]{2,1,0:T(8,128)(2,1)} %fusion), calls=%async_computation.1 | async-start | bytes 7340032 | tf_op jit(solution)/shard_map/all_to_all | solution.py:295
  122.6 11.2 %convolution_convert_fusion = bf16[3584,1024]{1,0:T(8,128)(2,1)S(1)} fusion(bf16[1024,3584]{1,0:T(8,128)(2,1)} %get-tuple-element.13, bf16[1024,1024]{1,0:T(8,128)(2,1)S(1)} %copy-done.2), kind=kOutput, calls=%fused_computation | convolution fusion | flops 7519862784 | bytes 16777216 | tf_op jit(solution)/shard_map/dot_general | solution.py:298
  133.8 3.0 %copy-done.9 = bf16[3584,1024]{1,0:T(8,128)(2,1)} copy-done((bf16[3584,1024]{1,0:T(8,128)(2,1)}, bf16[3584,1024]{1,0:T(8,128)(2,1)S(1)}, u32[]{:S(2)}) %copy-start.9) | copy-done | bytes 7340056
  136.8 32.7 %all-to-all-done.1 = bf16[128,8,1792]{2,1,0:T(8,128)(2,1)} async-done(((bf16[128,8,1792]{2,1,0:T(8,128)(2,1)}), bf16[128,8,1792]{2,1,0:T(8,128)(2,1)}, u32[]{:S(2)}, u32[]{:S(2)}) %all-to-all-start.1) | async-done | bytes 3670048 | tf_op jit(solution)/shard_map/all_to_all | solution.py:295
  169.5 3.7 %chip_sum.1 = bf16[8,3584]{1,0:T(8,128)(2,1)} custom-call(bf16[64,2,8,1792]{3,2,1,0:T(8,128)(2,1)} %bitcast.13.parts, bf16[8,128]{1,0:T(8,128)(2,1)S(1)} %slice.19.after), custom_call_target="tpu_custom_call" | custom-call | flops 1835008 | bytes 4194304 | tf_op jit(solution)/shard_map/chip_sum/pallas_call | solution.py:242
  (84 shorter events, 22.0 us)
Async XLA Ops:
  1.8 14.8 %collective-permute-start.3 = (bf16[128,1792]{1,0:T(8,128)(2,1)S(1)}, bf16[128,1792]{1,0:T(8,128)(2,1)S(1)}, u32[]{:S(2)}, u32[]{:S(2)}) collective-permute-start(bf16[128,1792]{1,0:T(8,128)(2,1)S(1)} %constant_dynamic-slice_fusion), channel_id=1, source_target_pairs={{0,64},{64,0},{1,65},{65,1},{2,66},{66,2},{3,67},{67,3},{4,68},{68... | collective-permute-start | bytes 1376264 | tf_op jit(solution)/shard_map/ppermute | solution.py:21
  6.4 14.0 %collective-permute-start = (bf16[128,1792]{1,0:T(8,128)(2,1)S(1)}, bf16[128,1792]{1,0:T(8,128)(2,1)S(1)}, u32[]{:S(2)}, u32[]{:S(2)}) collective-permute-start(bf16[128,1792]{1,0:T(8,128)(2,1)S(1)} %constant_dynamic-slice_fusion), channel_id=1, source_target_pairs={{0,16},{16,32},{32,48},{48,0},{1,17},{17,33},{33,49},{49,1},{2,18}... | collective-permute-start | bytes 1376264 | tf_op jit(solution)/shard_map/ppermute | solution.py:21
  7.6 15.5 %collective-permute-start.1 = (bf16[128,1792]{1,0:T(8,128)(2,1)S(1)}, bf16[128,1792]{1,0:T(8,128)(2,1)}, u32[]{:S(2)}, u32[]{:S(2)}) collective-permute-start(bf16[128,1792]{1,0:T(8,128)(2,1)S(1)} %constant_dynamic-slice_fusion), channel_id=1, source_target_pairs={{0,48},{16,0},{32,16},{48,32},{1,49},{17,1},{33,17},{49,33},{2,50}... | collective-permute-start | bytes 1376264 | tf_op jit(solution)/shard_map/ppermute | solution.py:21
  9.0 20.6 %collective-permute-start.2 = (bf16[128,1792]{1,0:T(8,128)(2,1)S(1)}, bf16[128,1792]{1,0:T(8,128)(2,1)}, u32[]{:S(2)}, u32[]{:S(2)}) collective-permute-start(bf16[128,1792]{1,0:T(8,128)(2,1)S(1)} %constant_dynamic-slice_fusion), channel_id=1, source_target_pairs={{0,32},{16,48},{32,0},{48,16},{1,33},{17,49},{33,1},{49,17},{2,34}... | collective-permute-start | bytes 1376264 | tf_op jit(solution)/shard_map/ppermute | solution.py:21
  19.1 17.0 %collective-permute-start.4 = (bf16[128,768]{1,0:T(8,128)(2,1)}, bf16[128,768]{1,0:T(8,128)(2,1)}, u32[]{:S(2)}, u32[]{:S(2)}) collective-permute-start(bf16[128,768]{1,0:T(8,128)(2,1)} %left_columns.1), channel_id=1, source_target_pairs={{0,16},{16,32},{32,48},{48,0},{1,17},{17,33},{33,49},{49,1},{2,18}... | collective-permute-start | bytes 589832 | tf_op jit(solution)/shard_map/ppermute | solution.py:21
  20.4 21.8 %collective-permute-start.7 = (bf16[128,1024]{1,0:T(8,128)(2,1)S(1)}, bf16[128,1024]{1,0:T(8,128)(2,1)S(1)}, u32[]{:S(2)}, u32[]{:S(2)}) collective-permute-start(bf16[128,1024]{1,0:T(8,128)(2,1)S(1)} %slice.16), channel_id=1, source_target_pairs={{0,64},{64,0},{1,65},{65,1},{2,66},{66,2},{3,67},{67,3},{4,68},{68... | collective-permute-start | bytes 786440 | tf_op jit(solution)/shard_map/ppermute | solution.py:21
  24.1 18.2 %collective-permute-start.8 = (bf16[128,1024]{1,0:T(8,128)(2,1)S(1)}, bf16[128,1024]{1,0:T(8,128)(2,1)S(1)}, u32[]{:S(2)}, u32[]{:S(2)}) collective-permute-start(bf16[128,1024]{1,0:T(8,128)(2,1)S(1)} %slice.17), channel_id=1, source_target_pairs={{0,64},{64,0},{1,65},{65,1},{2,66},{66,2},{3,67},{67,3},{4,68},{68... | collective-permute-start | bytes 786440 | tf_op jit(solution)/shard_map/ppermute | solution.py:21
  24.5 11.6 %collective-permute-start.5 = (bf16[128,768]{1,0:T(8,128)(2,1)}, bf16[128,768]{1,0:T(8,128)(2,1)}, u32[]{:S(2)}, u32[]{:S(2)}) collective-permute-start(bf16[128,768]{1,0:T(8,128)(2,1)} %left_columns.1), channel_id=1, source_target_pairs={{0,48},{16,0},{32,16},{48,32},{1,49},{17,1},{33,17},{49,33},{2,50}... | collective-permute-start | bytes 589832 | tf_op jit(solution)/shard_map/ppermute | solution.py:21
  29.6 10.8 %collective-permute-start.6 = (bf16[128,768]{1,0:T(8,128)(2,1)}, bf16[128,768]{1,0:T(8,128)(2,1)S(1)}, u32[]{:S(2)}, u32[]{:S(2)}) collective-permute-start(bf16[128,768]{1,0:T(8,128)(2,1)} %left_columns.1), channel_id=1, source_target_pairs={{0,32},{16,48},{32,0},{48,16},{1,33},{17,49},{33,1},{49,17},{2,34}... | collective-permute-start | bytes 589832 | tf_op jit(solution)/shard_map/ppermute | solution.py:21
  36.1 12.5 %collective-permute-start.9 = (bf16[128,1024]{1,0:T(8,128)(2,1)S(1)}, bf16[128,1024]{1,0:T(8,128)(2,1)}, u32[]{:S(2)}, u32[]{:S(2)}) collective-permute-start(bf16[128,1024]{1,0:T(8,128)(2,1)S(1)} %slice.18), channel_id=1, source_target_pairs={{0,64},{64,0},{1,65},{65,1},{2,66},{66,2},{3,67},{67,3},{4,68},{68... | collective-permute-start | bytes 786440 | tf_op jit(solution)/shard_map/ppermute | solution.py:21
  36.1 15.3 %collective-permute-start.10 = (bf16[128,1792]{1,0:T(8,128)(2,1)S(1)}, bf16[128,1792]{1,0:T(8,128)(2,1)}, u32[]{:S(2)}, u32[]{:S(2)}) collective-permute-start(bf16[128,1792]{1,0:T(8,128)(2,1)S(1)} %collective-permute-done.refs_0_), channel_id=1, source_target_pairs={{0,1},{1,0},{2,3},{3,2},{4,5},{5,4},{6,7},{7,6},{8,9},{9,8},{10,11... | collective-permute-start | bytes 1376264 | tf_op jit(solution)/shard_map/ppermute | solution.py:21
  40.4 11.4 %collective-permute-start.11 = (bf16[128,1792]{1,0:T(8,128)(2,1)}, bf16[128,1792]{1,0:T(8,128)(2,1)}, u32[]{:S(2)}, u32[]{:S(2)}) collective-permute-start(bf16[128,1792]{1,0:T(8,128)(2,1)} %collective-permute-done.1.refs_1_), channel_id=1, source_target_pairs={{0,1},{1,0},{2,3},{3,2},{4,5},{5,4},{6,7},{7,6},{8,9},{9,8},{10,11... | collective-permute-start | bytes 1376264 | tf_op jit(solution)/shard_map/ppermute | solution.py:21
  42.2 6.6 %collective-permute-start.14 = (bf16[128,768]{1,0:T(8,128)(2,1)}, bf16[128,768]{1,0:T(8,128)(2,1)}, u32[]{:S(2)}, u32[]{:S(2)}) collective-permute-start(bf16[128,768]{1,0:T(8,128)(2,1)} %collective-permute-done.4.refs_4_), channel_id=1, source_target_pairs={{0,1},{1,0},{2,3},{3,2},{4,5},{5,4},{6,7},{7,6},{8,9},{9,8},{10,11... | collective-permute-start | bytes 589832 | tf_op jit(solution)/shard_map/ppermute | solution.py:21
  42.3 6.9 %collective-permute-start.15 = (bf16[128,768]{1,0:T(8,128)(2,1)}, bf16[128,768]{1,0:T(8,128)(2,1)}, u32[]{:S(2)}, u32[]{:S(2)}) collective-permute-start(bf16[128,768]{1,0:T(8,128)(2,1)} %collective-permute-done.5.refs_5_), channel_id=1, source_target_pairs={{0,1},{1,0},{2,3},{3,2},{4,5},{5,4},{6,7},{7,6},{8,9},{9,8},{10,11... | collective-permute-start | bytes 589832 | tf_op jit(solution)/shard_map/ppermute | solution.py:21
  43.0 49.7 %all-to-all-start = ((bf16[16,64,1024]{2,1,0:T(8,128)(2,1)}), bf16[16,64,1024]{2,1,0:T(8,128)(2,1)S(1)}, u32[]{:S(2)}, u32[]{:S(2)}) async-start(bf16[16,64,1024]{2,1,0:T(8,128)(2,1)} %bitcast.25), calls=%async_computation | async-start | bytes 4194304 | tf_op jit(solution)/shard_map/all_to_all | solution.py:272
  48.6 4.1 %collective-permute-start.12 = (bf16[128,1792]{1,0:T(8,128)(2,1)}, bf16[128,1792]{1,0:T(8,128)(2,1)}, u32[]{:S(2)}, u32[]{:S(2)}) collective-permute-start(bf16[128,1792]{1,0:T(8,128)(2,1)} %collective-permute-done.2.refs_2_), channel_id=1, source_target_pairs={{0,1},{1,0},{2,3},{3,2},{4,5},{5,4},{6,7},{7,6},{8,9},{9,8},{10,11... | collective-permute-start | bytes 1376264 | tf_op jit(solution)/shard_map/ppermute | solution.py:21
  48.8 2.5 %collective-permute-start.16 = (bf16[128,768]{1,0:T(8,128)(2,1)}, bf16[128,768]{1,0:T(8,128)(2,1)S(1)}, u32[]{:S(2)}, u32[]{:S(2)}) collective-permute-start(bf16[128,768]{1,0:T(8,128)(2,1)} %copy-done.12), channel_id=1, source_target_pairs={{0,1},{1,0},{2,3},{3,2},{4,5},{5,4},{6,7},{7,6},{8,9},{9,8},{10,11... | collective-permute-start | bytes 589832 | tf_op jit(solution)/shard_map/ppermute | solution.py:21
  49.2 3.5 %collective-permute-start.13 = (bf16[128,1792]{1,0:T(8,128)(2,1)S(1)}, bf16[128,1792]{1,0:T(8,128)(2,1)}, u32[]{:S(2)}, u32[]{:S(2)}) collective-permute-start(bf16[128,1792]{1,0:T(8,128)(2,1)S(1)} %copy-done.5), channel_id=1, source_target_pairs={{0,1},{1,0},{2,3},{3,2},{4,5},{5,4},{6,7},{7,6},{8,9},{9,8},{10,11... | collective-permute-start | bytes 1376264 | tf_op jit(solution)/shard_map/ppermute | solution.py:21
  51.3 1.7 collective-permute-start.17
  51.4 2.1 %collective-permute-start.18 = (bf16[128,1024]{1,0:T(8,128)(2,1)}, bf16[128,1024]{1,0:T(8,128)(2,1)}, u32[]{:S(2)}, u32[]{:S(2)}) collective-permute-start(bf16[128,1024]{1,0:T(8,128)(2,1)} %copy-done.11), channel_id=1, source_target_pairs={{0,1},{1,0},{2,3},{3,2},{4,5},{5,4},{6,7},{7,6},{8,9},{9,8},{10,11... | collective-permute-start | bytes 786440 | tf_op jit(solution)/shard_map/ppermute | solution.py:21
  51.8 2.1 %collective-permute-start.19 = (bf16[128,1024]{1,0:T(8,128)(2,1)}, bf16[128,1024]{1,0:T(8,128)(2,1)}, u32[]{:S(2)}, u32[]{:S(2)}) collective-permute-start(bf16[128,1024]{1,0:T(8,128)(2,1)} %collective-permute-done.9.refs_9_), channel_id=1, source_target_pairs={{0,1},{1,0},{2,3},{3,2},{4,5},{5,4},{6,7},{7,6},{8,9},{9,8},{10,11... | collective-permute-start | bytes 786440 | tf_op jit(solution)/shard_map/ppermute | solution.py:21
  72.2 4.0 %collective-permute-start.23 = (f32[2,1024]{1,0:T(2,128)S(1)}, f32[2,1024]{1,0:T(2,128)S(1)}, u32[]{:S(2)}, u32[]{:S(2)}) collective-permute-start(f32[2,1024]{1,0:T(2,128)S(1)} %add.107), channel_id=1, source_target_pairs={{0,32},{16,48},{32,0},{48,16},{1,33},{17,49},{33,1},{49,17},{2,34}... | collective-permute-start | bytes 24584 | tf_op jit(solution)/shard_map/ppermute | solution.py:21
  72.2 4.0 %collective-permute-start.22 = (f32[2,1024]{1,0:T(2,128)S(1)}, f32[2,1024]{1,0:T(2,128)S(1)}, u32[]{:S(2)}, u32[]{:S(2)}) collective-permute-start(f32[2,1024]{1,0:T(2,128)S(1)} %add.107), channel_id=1, source_target_pairs={{0,48},{16,0},{32,16},{48,32},{1,49},{17,1},{33,17},{49,33},{2,50}... | collective-permute-start | bytes 24584 | tf_op jit(solution)/shard_map/ppermute | solution.py:21
  74.0 3.7 %collective-permute-start.21 = (f32[2,1024]{1,0:T(2,128)S(1)}, f32[2,1024]{1,0:T(2,128)S(1)}, u32[]{:S(2)}, u32[]{:S(2)}) collective-permute-start(f32[2,1024]{1,0:T(2,128)S(1)} %add.107), channel_id=1, source_target_pairs={{0,16},{16,32},{32,48},{48,0},{1,17},{17,33},{33,49},{49,1},{2,18}... | collective-permute-start | bytes 24584 | tf_op jit(solution)/shard_map/ppermute | solution.py:21
  77.7 4.5 %collective-permute-start.26 = (f32[2,1024]{1,0:T(2,128)S(1)}, f32[2,1024]{1,0:T(2,128)S(1)}, u32[]{:S(2)}, u32[]{:S(2)}) collective-permute-start(f32[2,1024]{1,0:T(2,128)S(1)} %add_add_fusion.2), channel_id=1, source_target_pairs={{0,8},{4,12},{8,0},{12,4},{1,9},{5,13},{9,1},{13,5},{2,10},{6,14},... | collective-permute-start | bytes 24584 | tf_op jit(solution)/shard_map/ppermute | solution.py:21
  80.7 2.8 %collective-permute-start.25 = (f32[2,1024]{1,0:T(2,128)S(1)}, f32[2,1024]{1,0:T(2,128)S(1)}, u32[]{:S(2)}, u32[]{:S(2)}) collective-permute-start(f32[2,1024]{1,0:T(2,128)S(1)} %add_add_fusion.2), channel_id=1, source_target_pairs={{0,12},{4,0},{8,4},{12,8},{1,13},{5,1},{9,5},{13,9},{2,14},{6,2},{... | collective-permute-start | bytes 24584 | tf_op jit(solution)/shard_map/ppermute | solution.py:21
  81.6 3.7 %collective-permute-start.24 = (f32[2,1024]{1,0:T(2,128)S(1)}, f32[2,1024]{1,0:T(2,128)S(1)}, u32[]{:S(2)}, u32[]{:S(2)}) collective-permute-start(f32[2,1024]{1,0:T(2,128)S(1)} %add_add_fusion.2), channel_id=1, source_target_pairs={{0,4},{4,8},{8,12},{12,0},{1,5},{5,9},{9,13},{13,1},{2,6},{6,10},{... | collective-permute-start | bytes 24584 | tf_op jit(solution)/shard_map/ppermute | solution.py:21
  85.3 4.1 %collective-permute-start.29 = (f32[2,1024]{1,0:T(2,128)S(1)}, f32[2,1024]{1,0:T(2,128)S(1)}, u32[]{:S(2)}, u32[]{:S(2)}) collective-permute-start(f32[2,1024]{1,0:T(2,128)S(1)} %add_add_fusion.1), channel_id=1, source_target_pairs={{0,64},{2,66},{64,0},{66,2},{1,65},{3,67},{65,1},{67,3},{4,68},{6,... | collective-permute-start | bytes 24584 | tf_op jit(solution)/shard_map/ppermute | solution.py:21
  87.4 2.5 %collective-permute-start.28 = (f32[2,1024]{1,0:T(2,128)S(1)}, f32[2,1024]{1,0:T(2,128)S(1)}, u32[]{:S(2)}, u32[]{:S(2)}) collective-permute-start(f32[2,1024]{1,0:T(2,128)S(1)} %add_add_fusion.1), channel_id=1, source_target_pairs={{0,66},{2,0},{64,2},{66,64},{1,67},{3,1},{65,3},{67,65},{4,70},{6,... | collective-permute-start | bytes 24584 | tf_op jit(solution)/shard_map/ppermute | solution.py:21
  89.0 3.7 %collective-permute-start.27 = (f32[2,1024]{1,0:T(2,128)S(1)}, f32[2,1024]{1,0:T(2,128)S(1)}, u32[]{:S(2)}, u32[]{:S(2)}) collective-permute-start(f32[2,1024]{1,0:T(2,128)S(1)} %add_add_fusion.1), channel_id=1, source_target_pairs={{0,2},{2,64},{64,66},{66,0},{1,3},{3,65},{65,67},{67,1},{4,6},{6,6... | collective-permute-start | bytes 24584 | tf_op jit(solution)/shard_map/ppermute | solution.py:21
  103.5 11.3 %collective-permute-start.30 = (bf16[1024,1792]{1,0:T(8,128)(2,1)S(1)}, bf16[1024,1792]{1,0:T(8,128)(2,1)S(1)}, u32[]{:S(2)}, u32[]{:S(2)}) collective-permute-start(bf16[1024,1792]{1,0:T(8,128)(2,1)S(1)} %get-tuple-element.12), channel_id=1, source_target_pairs={{0,1},{1,0},{2,3},{3,2},{4,5},{5,4},{6,7},{7,6},{8,9},{9,8},{10,11... | collective-permute-start | bytes 11010056 | tf_op jit(solution)/shard_map/ppermute | solution.py:21
  117.6 51.9 %all-to-all-start.1 = ((bf16[128,8,1792]{2,1,0:T(8,128)(2,1)}), bf16[128,8,1792]{2,1,0:T(8,128)(2,1)}, u32[]{:S(2)}, u32[]{:S(2)}) async-start(bf16[128,8,1792]{2,1,0:T(8,128)(2,1)} %fusion), calls=%async_computation.1 | async-start | bytes 7340032 | tf_op jit(solution)/shard_map/all_to_all | solution.py:295
  (15 other events, 153.0 us)

commit v6 on v5

--- a/solution.py
+++ b/solution.py
@@ -1,4 +1,5 @@
 import functools
+import math
 
 import jax
 import jax.numpy as jnp
@@ -12,6 +13,7 @@
 EVERY = ("zh", "x", "y", "zl", "core")
 Z = ("zh", "zl")
 VMEM_BYTES = 60 << 20
+EXPONENT = 15.0 * math.log2(math.e)
 SMEM = pl.BlockSpec(memory_space=pltpu.SMEM)
 VMEM = pl.BlockSpec(memory_space=pltpu.VMEM)
 ANY = pl.BlockSpec(memory_space=pl.ANY)
@@ -79,9 +81,9 @@
         def _(m):
             at = pl.ds(pl.multiple_of(m * 512, 512), 512)
             raw = jnp.dot(rows_v[at, :], weight_v[:, c], preferred_element_type=F32)
-            cap = jnp.tanh(raw / 30.0)
+            cap = jnp.tanh(raw * (1.0 / 30.0))
             capped_v[at, c] = cap
-            e = jnp.exp(15.0 * cap)
+            e = jnp.exp2(EXPONENT * cap)
             s = part[at, :]
             for k in range(tile // 128):
                 s = s + e[:, k * 128 : (k + 1) * 128]
@@ -144,8 +146,8 @@
 
     scale = (8192.0 / totals[...]).T
     cap = capped[...]
-    student = jnp.exp(15.0 * cap) * scale[:, 0:1]
-    target = jnp.exp(teacher[...].astype(F32) * 0.5) * scale[:, 1:2]
+    student = jnp.exp2(EXPONENT * cap) * scale[:, 0:1]
+    target = jnp.exp2(teacher[...].astype(F32) * (EXPONENT / 30.0)) * scale[:, 1:2]
     d = ((student - target) * (1.0 - cap * cap)).astype(BF)
     delta[...] = d
 
@@ -218,38 +220,36 @@
     )(delta, weight)
 
 
-def chip_sum_kernel(parts, after, out, total):
-    i = pl.program_id(0)
-    now = jnp.sum(parts[...].astype(F32), axis=0)
-
-    @pl.when(i == 0)
-    def _():
-        total[...] = now
-
-    @pl.when(i > 0)
-    def _():
-        total[...] += now
-
-    @pl.when(i == pl.num_programs(0) - 1)
-    def _():
-        half = total.shape[2]
-        for k in range(2):
-            out[:, k * half : (k + 1) * half] = total[k].astype(BF)
+def chip_sum_kernel(parts, after, out, parts_v, total, sem):
+    count = parts.shape[0] // sem.shape[0]
+    pieces = [pl.ds(i * count, count) for i in range(sem.shape[0])]
+    loads = [
+        pltpu.make_async_copy(parts.at[p], parts_v.at[p], sem.at[i]) for i, p in enumerate(pieces)
+    ]
+    for c in loads:
+        c.start()
+    for i, p in enumerate(pieces):
+        loads[i].wait()
+        now = jnp.sum(parts_v[p].astype(F32), axis=0)
+        total[...] = now if i == 0 else total[...] + now
+    rows, half = out.shape[0], total.shape[1]
+    for k in range(2):
+        out[:, k * half : (k + 1) * half] = total[k * rows : (k + 1) * rows, :].astype(BF)
 
 
 def chip_sum(parts, after):
-    count, cores, rows, cols = parts.shape
+    count, rows, cols = parts.shape
     return pl.pallas_call(
         chip_sum_kernel,
         name="chip_sum",
-        grid=(4,),
-        in_specs=[
-            pl.BlockSpec((count // 4, cores, rows, cols), lambda i: (i, 0, 0, 0)),
-            ANY,
+        in_specs=[ANY, ANY],
+        out_specs=VMEM,
+        out_shape=jax.ShapeDtypeStruct((rows // 2, 2 * cols), BF),
+        scratch_shapes=[
+            pltpu.VMEM((count, rows, cols), BF),
+            pltpu.VMEM((rows, cols), F32),
+            pltpu.SemaphoreType.DMA((8,)),
         ],
-        out_specs=pl.BlockSpec((rows, cores * cols), lambda i: (0, 0)),
-        out_shape=jax.ShapeDtypeStruct((rows, cores * cols), BF),
-        scratch_shapes=[pltpu.VMEM((cores, rows, cols), F32)],
         compiler_params=pltpu.CompilerParams(vmem_limit_bytes=16 << 20),
         cost_estimate=pl.CostEstimate(flops=parts.size, bytes_accessed=4 << 20, transcendentals=0),
     )(parts, after)
@@ -298,7 +298,7 @@
     grad_head = lax.dot_general(
         gathered, delta, (((0,), (0,)), ((), ())), preferred_element_type=F32
     ).astype(BF)
-    grad_hidden = chip_sum(parts.reshape(64, 2, rows // 128, half), grad_head[:8, :128])
+    grad_hidden = chip_sum(parts.reshape(64, rows // 64, half), grad_head[:8, :128])
     return grad_hidden, grad_head
 
 

time: 174 us -> 173 us (level)
  no operation moved by 1% of the time
where the time goes in v6:
time: 173 us; the launch traced here: 172 us
  waiting for transfers between devices  58.7 us (34%)
  starting transfers between devices  49.5 us (29%)
  Pallas kernels  33.6 us (19%)
  local copies, waits for them, and re-layouts  13.5 us (8%)
  matrix products  11.2 us (6%)
  other arithmetic  4.8 us (3%)
    ppermute x31, starting transfers between devices, shift(): return lax.ppermute(v, axis, [(i, (i + step) % size) for i in range(size)])  39 us
    all_to_all x1, waiting for transfers between devices, per_device(): lax.all_to_all(chip.reshape(128, rows // 128, half), EVERY, split_axis=0,...  32.7 us
    ppermute x31, waiting for transfers between devices, shift(): return lax.ppermute(v, axis, [(i, (i + step) % size) for i in range(size)])  26 us
    pallas_call x1, Pallas kernels, scores(): pl.pallas_call(functools.partial(scores_kernel, tile), name='scores', out...  16 us
    dot_general x1, matrix products, per_device(): lax.dot_general(gathered, delta, (((0,), (0,)), ((), ())), preferred_elem...  11.2 us
    pallas_call x1, Pallas kernels, delta_and_share(): pl.pallas_call(delta_kernel, name='delta_and_share', grid_spec=pltpu.Pref...  8.52 us
    unnamed x28, local copies, waits for them, and re-layouts  6.37 us
    all_to_all x1, starting transfers between devices, per_device(): lax.all_to_all(by_owner, ('y', 'zl', 'core'), split_axis=0, concat_axis=0...  5.61 us
  transfers between devices with their start and end apart: 33, of which 17 were waited for; matrix products, arithmetic and copies ran while one was open for 11% of the time, Pallas kernels for 13%

profile of v6, /device:TPU:1, one launch (start us, length us, event | category | flops | bytes accessed | tf_op | source)
XLA Modules:
  0.0 172.3 jit_solution(1892854982960220535)
XLA Ops:
  1.8 4.5 %collective-permute-start.3 = (bf16[128,1792]{1,0:T(8,128)(2,1)S(1)}, bf16[128,1792]{1,0:T(8,128)(2,1)S(1)}, u32[]{:S(2)}, u32[]{:S(2)}) collective-permute-start(bf16[128,1792]{1,0:T(8,128)(2,1)S(1)} %constant_dynamic-slice_fusion), channel_id=1, source_target_pairs={{0,64},{64,0},{1,65},{65,1},{2,66},{66,2},{3,67},{67,3},{4,68},{68... | collective-permute-start | bytes 1376264 | tf_op jit(solution)/shard_map/ppermute | solution.py:23
  7.6 1.5 collective-permute-start.1
  9.0 1.5 collective-permute-start.2
  10.6 3.2 %copy.8 = bf16[8,16,8,1024]{3,2,0,1:T(8,128)(2,1)} copy(bf16[8,16,8,1024]{3,2,1,0:T(8,128)(2,1)} %bitcast.26) | data formatting | bytes 4194304 | tf_op jit(solution)/shard_map/reshape | solution.py:271
  15.1 1.5 collective-permute-done.3.block.refs_3_
  17.4 1.7 left_columns.1
  20.4 2.7 %collective-permute-start.7 = (bf16[128,1024]{1,0:T(8,128)(2,1)S(1)}, bf16[128,1024]{1,0:T(8,128)(2,1)S(1)}, u32[]{:S(2)}, u32[]{:S(2)}) collective-permute-start(bf16[128,1024]{1,0:T(8,128)(2,1)S(1)} %slice.16), channel_id=1, source_target_pairs={{0,64},{64,0},{1,65},{65,1},{2,66},{66,2},{3,67},{67,3},{4,68},{68... | collective-permute-start | bytes 786440 | tf_op jit(solution)/shard_map/ppermute | solution.py:23
  25.9 3.7 %collective-permute-done.2.refs_2_ = bf16[128,1792]{1,0:T(8,128)(2,1)} collective-permute-done((bf16[128,1792]{1,0:T(8,128)(2,1)S(1)}, bf16[128,1792]{1,0:T(8,128)(2,1)}, u32[]{:S(2)}, u32[]{:S(2)}) %collective-permute-start.2) | collective-permute-done | bytes 458784 | tf_op jit(solution)/shard_map/ppermute | solution.py:23
  31.1 5.0 %collective-permute-done.4.refs_4_ = bf16[128,768]{1,0:T(8,128)(2,1)} collective-permute-done((bf16[128,768]{1,0:T(8,128)(2,1)}, bf16[128,768]{1,0:T(8,128)(2,1)}, u32[]{:S(2)}, u32[]{:S(2)}) %collective-permute-start.4) | collective-permute-done | bytes 196640 | tf_op jit(solution)/shard_map/ppermute | solution.py:23
  36.1 4.3 %collective-permute-start.10 = (bf16[128,1792]{1,0:T(8,128)(2,1)S(1)}, bf16[128,1792]{1,0:T(8,128)(2,1)}, u32[]{:S(2)}, u32[]{:S(2)}) collective-permute-start(bf16[128,1792]{1,0:T(8,128)(2,1)S(1)} %collective-permute-done.refs_0_), channel_id=1, source_target_pairs={{0,1},{1,0},{2,3},{3,2},{4,5},{5,4},{6,7},{7,6},{8,9},{9,8},{10,11... | collective-permute-start | bytes 1376264 | tf_op jit(solution)/shard_map/ppermute | solution.py:23
  40.4 1.8 %collective-permute-start.11 = (bf16[128,1792]{1,0:T(8,128)(2,1)}, bf16[128,1792]{1,0:T(8,128)(2,1)}, u32[]{:S(2)}, u32[]{:S(2)}) collective-permute-start(bf16[128,1792]{1,0:T(8,128)(2,1)} %collective-permute-done.1.refs_1_), channel_id=1, source_target_pairs={{0,1},{1,0},{2,3},{3,2},{4,5},{5,4},{6,7},{7,6},{8,9},{9,8},{10,11... | collective-permute-start | bytes 1376264 | tf_op jit(solution)/shard_map/ppermute | solution.py:23
  43.0 5.6 %all-to-all-start = ((bf16[16,64,1024]{2,1,0:T(8,128)(2,1)}), bf16[16,64,1024]{2,1,0:T(8,128)(2,1)S(1)}, u32[]{:S(2)}, u32[]{:S(2)}) async-start(bf16[16,64,1024]{2,1,0:T(8,128)(2,1)} %bitcast.25), calls=%async_computation | async-start | bytes 4194304 | tf_op jit(solution)/shard_map/all_to_all | solution.py:272
  49.3 2.0 %collective-permute-done.16.refs_16_ = bf16[128,768]{1,0:T(8,128)(2,1)S(1)} collective-permute-done((bf16[128,768]{1,0:T(8,128)(2,1)}, bf16[128,768]{1,0:T(8,128)(2,1)S(1)}, u32[]{:S(2)}, u32[]{:S(2)}) %collective-permute-start.16) | collective-permute-done | bytes 196640 | tf_op jit(solution)/shard_map/ppermute | solution.py:23
  53.9 16.0 %scores.1 = (bf16[1024,3584]{1,0:T(8,128)(2,1)}, f32[1024,1024]{1,0:T(8,128)}, f32[2,1024]{1,0:T(2,128)}) custom-call(s32[9]{0:T(128)} %stack.36.place, bf16[128,3584]{1,0:T(8,128)(2,1)} %hidden.1, bf16[128,1792]{1,0:T(8,128)(2,1)} %copy-done.6, bf16[128,1792]{1,0:T(8,128)(2,1)} %collective-permute-done.1.refs_1_, ...), custom_call_target="tpu_custom_call" | custom-call | flops 7516192768 | bytes 20971520 | tf_op jit(solution)/shard_map/scores/pallas_call | solution.py:107
  72.1 1.8 %collective-permute-start.22 = (f32[2,1024]{1,0:T(2,128)S(1)}, f32[2,1024]{1,0:T(2,128)S(1)}, u32[]{:S(2)}, u32[]{:S(2)}) collective-permute-start(f32[2,1024]{1,0:T(2,128)S(1)} %add.107), channel_id=1, source_target_pairs={{0,48},{16,0},{32,16},{48,32},{1,49},{17,1},{33,17},{49,33},{2,50}... | collective-permute-start | bytes 24584 | tf_op jit(solution)/shard_map/ppermute | solution.py:23
  74.5 1.7 collective-permute-done.23
  76.2 1.6 collective-permute-done.21
  77.7 3.0 %collective-permute-start.26 = (f32[2,1024]{1,0:T(2,128)S(1)}, f32[2,1024]{1,0:T(2,128)S(1)}, u32[]{:S(2)}, u32[]{:S(2)}) collective-permute-start(f32[2,1024]{1,0:T(2,128)S(1)} %add_add_fusion.2), channel_id=1, source_target_pairs={{0,8},{4,12},{8,0},{12,4},{1,9},{5,13},{9,1},{13,5},{2,10},{6,14},... | collective-permute-start | bytes 24584 | tf_op jit(solution)/shard_map/ppermute | solution.py:23
  83.5 1.8 %collective-permute-done.24 = f32[2,1024]{1,0:T(2,128)S(1)} collective-permute-done((f32[2,1024]{1,0:T(2,128)S(1)}, f32[2,1024]{1,0:T(2,128)S(1)}, u32[]{:S(2)}, u32[]{:S(2)}) %collective-permute-start.24) | collective-permute-done | bytes 8224 | tf_op jit(solution)/shard_map/ppermute | solution.py:23
  85.3 2.0 %collective-permute-start.29 = (f32[2,1024]{1,0:T(2,128)S(1)}, f32[2,1024]{1,0:T(2,128)S(1)}, u32[]{:S(2)}, u32[]{:S(2)}) collective-permute-start(f32[2,1024]{1,0:T(2,128)S(1)} %add_add_fusion.1), channel_id=1, source_target_pairs={{0,64},{2,66},{64,0},{66,2},{1,65},{3,67},{65,1},{67,3},{4,68},{6,... | collective-permute-start | bytes 24584 | tf_op jit(solution)/shard_map/ppermute | solution.py:23
  87.3 1.6 collective-permute-start.28
  89.8 2.8 %collective-permute-done.27 = f32[2,1024]{1,0:T(2,128)S(1)} collective-permute-done((f32[2,1024]{1,0:T(2,128)S(1)}, f32[2,1024]{1,0:T(2,128)S(1)}, u32[]{:S(2)}, u32[]{:S(2)}) %collective-permute-start.27) | collective-permute-done | bytes 8224 | tf_op jit(solution)/shard_map/ppermute | solution.py:23
  92.7 2.2 %copy-done = f32[1024,1024]{1,0:T(8,128)S(1)} copy-done((f32[1024,1024]{1,0:T(8,128)S(1)}, f32[1024,1024]{1,0:T(8,128)}, u32[]{:S(2)}) %copy-start) | copy-done | bytes 4194328
  94.9 8.5 %delta_and_share.1 = (bf16[1024,1024]{1,0:T(8,128)(2,1)S(1)}, bf16[1024,1792]{1,0:T(8,128)(2,1)S(1)}, bf16[1792,1024]{1,0:T(8,128)(2,1)S(1)}) custom-call(s32[1]{0:T(128)} %bitcast.core, f32[1024,1024]{1,0:T(8,128)S(1)} %copy-done, bf16[1024,1024]{1,0:T(8,128)(2,1)S(1)} %bitcast.23, f32[8,1024]{1,0:T(8,128)S(1)} %concatenate.3.totals, bf16[3584,1024]{1,0:T(8,128)(2,1)} %weight.1), custom_call_target="tpu_custom_call" | custom-call | flops 3758096384 | bytes 16777216 | tf_op jit(solution)/shard_map/delta_and_share/pallas_call | solution.py:170
  103.5 5.3 %collective-permute-start.30 = (bf16[1024,1792]{1,0:T(8,128)(2,1)S(1)}, bf16[1024,1792]{1,0:T(8,128)(2,1)S(1)}, u32[]{:S(2)}, u32[]{:S(2)}) collective-permute-start(bf16[1024,1792]{1,0:T(8,128)(2,1)S(1)} %get-tuple-element.12), channel_id=1, source_target_pairs={{0,1},{1,0},{2,3},{3,2},{4,5},{5,4},{6,7},{7,6},{8,9},{9,8},{10,11... | collective-permute-start | bytes 11010056 | tf_op jit(solution)/shard_map/ppermute | solution.py:23
  108.7 4.6 %own_share.1 = bf16[1024,1792]{1,0:T(8,128)(2,1)S(1)} custom-call(bf16[1024,1024]{1,0:T(8,128)(2,1)S(1)} %get-tuple-element.10.delta, bf16[1792,1024]{1,0:T(8,128)(2,1)S(1)} %get-tuple-element.11.weight), custom_call_target="tpu_custom_call" | custom-call | flops 3758096384 | bytes 10485760 | tf_op jit(solution)/shard_map/own_share/pallas_call | solution.py:209
  114.8 2.8 %fusion = bf16[128,8,1792]{2,1,0:T(8,128)(2,1)} fusion(bf16[1024,1792]{1,0:T(8,128)(2,1)S(1)} %collective-permute-done.30, bf16[1024,1792]{1,0:T(8,128)(2,1)S(1)} %own_share.1), kind=kLoop, calls=%fused_computation.3 | loop fusion | flops 7340032 | bytes 11010048 | tf_op jit(solution)/shard_map/reshape | solution.py:296
  117.5 5.0 %all-to-all-start.1 = ((bf16[128,8,1792]{2,1,0:T(8,128)(2,1)}), bf16[128,8,1792]{2,1,0:T(8,128)(2,1)}, u32[]{:S(2)}, u32[]{:S(2)}) async-start(bf16[128,8,1792]{2,1,0:T(8,128)(2,1)} %fusion), calls=%async_computation.1 | async-start | bytes 7340032 | tf_op jit(solution)/shard_map/all_to_all | solution.py:295
  122.5 11.2 %convolution_convert_fusion = bf16[3584,1024]{1,0:T(8,128)(2,1)S(1)} fusion(bf16[1024,3584]{1,0:T(8,128)(2,1)} %get-tuple-element.13, bf16[1024,1024]{1,0:T(8,128)(2,1)S(1)} %copy-done.2), kind=kOutput, calls=%fused_computation | convolution fusion | flops 7519862784 | bytes 16777216 | tf_op jit(solution)/shard_map/dot_general | solution.py:298
  133.7 3.0 %copy-done.9 = bf16[3584,1024]{1,0:T(8,128)(2,1)} copy-done((bf16[3584,1024]{1,0:T(8,128)(2,1)}, bf16[3584,1024]{1,0:T(8,128)(2,1)S(1)}, u32[]{:S(2)}) %copy-start.9) | copy-done | bytes 7340056
  136.7 32.7 %all-to-all-done.1 = bf16[128,8,1792]{2,1,0:T(8,128)(2,1)} async-done(((bf16[128,8,1792]{2,1,0:T(8,128)(2,1)}), bf16[128,8,1792]{2,1,0:T(8,128)(2,1)}, u32[]{:S(2)}, u32[]{:S(2)}) %all-to-all-start.1) | async-done | bytes 3670048 | tf_op jit(solution)/shard_map/all_to_all | solution.py:295
  169.4 2.7 %chip_sum.1 = bf16[8,3584]{1,0:T(8,128)(2,1)} custom-call(bf16[64,16,1792]{2,1,0:T(8,128)(2,1)} %bitcast.13.parts, bf16[8,128]{1,0:T(8,128)(2,1)S(1)} %slice.19.after), custom_call_target="tpu_custom_call" | custom-call | flops 1835008 | bytes 4194304 | tf_op jit(solution)/shard_map/chip_sum/pallas_call | solution.py:242
  (84 shorter events, 22.0 us)
Async XLA Ops:
  1.8 14.8 %collective-permute-start.3 = (bf16[128,1792]{1,0:T(8,128)(2,1)S(1)}, bf16[128,1792]{1,0:T(8,128)(2,1)S(1)}, u32[]{:S(2)}, u32[]{:S(2)}) collective-permute-start(bf16[128,1792]{1,0:T(8,128)(2,1)S(1)} %constant_dynamic-slice_fusion), channel_id=1, source_target_pairs={{0,64},{64,0},{1,65},{65,1},{2,66},{66,2},{3,67},{67,3},{4,68},{68... | collective-permute-start | bytes 1376264 | tf_op jit(solution)/shard_map/ppermute | solution.py:23
  6.4 14.0 %collective-permute-start = (bf16[128,1792]{1,0:T(8,128)(2,1)S(1)}, bf16[128,1792]{1,0:T(8,128)(2,1)S(1)}, u32[]{:S(2)}, u32[]{:S(2)}) collective-permute-start(bf16[128,1792]{1,0:T(8,128)(2,1)S(1)} %constant_dynamic-slice_fusion), channel_id=1, source_target_pairs={{0,16},{16,32},{32,48},{48,0},{1,17},{17,33},{33,49},{49,1},{2,18}... | collective-permute-start | bytes 1376264 | tf_op jit(solution)/shard_map/ppermute | solution.py:23
  7.6 15.5 %collective-permute-start.1 = (bf16[128,1792]{1,0:T(8,128)(2,1)S(1)}, bf16[128,1792]{1,0:T(8,128)(2,1)}, u32[]{:S(2)}, u32[]{:S(2)}) collective-permute-start(bf16[128,1792]{1,0:T(8,128)(2,1)S(1)} %constant_dynamic-slice_fusion), channel_id=1, source_target_pairs={{0,48},{16,0},{32,16},{48,32},{1,49},{17,1},{33,17},{49,33},{2,50}... | collective-permute-start | bytes 1376264 | tf_op jit(solution)/shard_map/ppermute | solution.py:23
  9.0 20.6 %collective-permute-start.2 = (bf16[128,1792]{1,0:T(8,128)(2,1)S(1)}, bf16[128,1792]{1,0:T(8,128)(2,1)}, u32[]{:S(2)}, u32[]{:S(2)}) collective-permute-start(bf16[128,1792]{1,0:T(8,128)(2,1)S(1)} %constant_dynamic-slice_fusion), channel_id=1, source_target_pairs={{0,32},{16,48},{32,0},{48,16},{1,33},{17,49},{33,1},{49,17},{2,34}... | collective-permute-start | bytes 1376264 | tf_op jit(solution)/shard_map/ppermute | solution.py:23
  19.1 17.0 %collective-permute-start.4 = (bf16[128,768]{1,0:T(8,128)(2,1)}, bf16[128,768]{1,0:T(8,128)(2,1)}, u32[]{:S(2)}, u32[]{:S(2)}) collective-permute-start(bf16[128,768]{1,0:T(8,128)(2,1)} %left_columns.1), channel_id=1, source_target_pairs={{0,16},{16,32},{32,48},{48,0},{1,17},{17,33},{33,49},{49,1},{2,18}... | collective-permute-start | bytes 589832 | tf_op jit(solution)/shard_map/ppermute | solution.py:23
  20.4 21.8 %collective-permute-start.7 = (bf16[128,1024]{1,0:T(8,128)(2,1)S(1)}, bf16[128,1024]{1,0:T(8,128)(2,1)S(1)}, u32[]{:S(2)}, u32[]{:S(2)}) collective-permute-start(bf16[128,1024]{1,0:T(8,128)(2,1)S(1)} %slice.16), channel_id=1, source_target_pairs={{0,64},{64,0},{1,65},{65,1},{2,66},{66,2},{3,67},{67,3},{4,68},{68... | collective-permute-start | bytes 786440 | tf_op jit(solution)/shard_map/ppermute | solution.py:23
  24.1 18.2 %collective-permute-start.8 = (bf16[128,1024]{1,0:T(8,128)(2,1)S(1)}, bf16[128,1024]{1,0:T(8,128)(2,1)S(1)}, u32[]{:S(2)}, u32[]{:S(2)}) collective-permute-start(bf16[128,1024]{1,0:T(8,128)(2,1)S(1)} %slice.17), channel_id=1, source_target_pairs={{0,64},{64,0},{1,65},{65,1},{2,66},{66,2},{3,67},{67,3},{4,68},{68... | collective-permute-start | bytes 786440 | tf_op jit(solution)/shard_map/ppermute | solution.py:23
  24.5 11.6 %collective-permute-start.5 = (bf16[128,768]{1,0:T(8,128)(2,1)}, bf16[128,768]{1,0:T(8,128)(2,1)}, u32[]{:S(2)}, u32[]{:S(2)}) collective-permute-start(bf16[128,768]{1,0:T(8,128)(2,1)} %left_columns.1), channel_id=1, source_target_pairs={{0,48},{16,0},{32,16},{48,32},{1,49},{17,1},{33,17},{49,33},{2,50}... | collective-permute-start | bytes 589832 | tf_op jit(solution)/shard_map/ppermute | solution.py:23
  29.6 10.8 %collective-permute-start.6 = (bf16[128,768]{1,0:T(8,128)(2,1)}, bf16[128,768]{1,0:T(8,128)(2,1)S(1)}, u32[]{:S(2)}, u32[]{:S(2)}) collective-permute-start(bf16[128,768]{1,0:T(8,128)(2,1)} %left_columns.1), channel_id=1, source_target_pairs={{0,32},{16,48},{32,0},{48,16},{1,33},{17,49},{33,1},{49,17},{2,34}... | collective-permute-start | bytes 589832 | tf_op jit(solution)/shard_map/ppermute | solution.py:23
  36.1 12.5 %collective-permute-start.9 = (bf16[128,1024]{1,0:T(8,128)(2,1)S(1)}, bf16[128,1024]{1,0:T(8,128)(2,1)}, u32[]{:S(2)}, u32[]{:S(2)}) collective-permute-start(bf16[128,1024]{1,0:T(8,128)(2,1)S(1)} %slice.18), channel_id=1, source_target_pairs={{0,64},{64,0},{1,65},{65,1},{2,66},{66,2},{3,67},{67,3},{4,68},{68... | collective-permute-start | bytes 786440 | tf_op jit(solution)/shard_map/ppermute | solution.py:23
  36.1 15.3 %collective-permute-start.10 = (bf16[128,1792]{1,0:T(8,128)(2,1)S(1)}, bf16[128,1792]{1,0:T(8,128)(2,1)}, u32[]{:S(2)}, u32[]{:S(2)}) collective-permute-start(bf16[128,1792]{1,0:T(8,128)(2,1)S(1)} %collective-permute-done.refs_0_), channel_id=1, source_target_pairs={{0,1},{1,0},{2,3},{3,2},{4,5},{5,4},{6,7},{7,6},{8,9},{9,8},{10,11... | collective-permute-start | bytes 1376264 | tf_op jit(solution)/shard_map/ppermute | solution.py:23
  40.4 11.4 %collective-permute-start.11 = (bf16[128,1792]{1,0:T(8,128)(2,1)}, bf16[128,1792]{1,0:T(8,128)(2,1)}, u32[]{:S(2)}, u32[]{:S(2)}) collective-permute-start(bf16[128,1792]{1,0:T(8,128)(2,1)} %collective-permute-done.1.refs_1_), channel_id=1, source_target_pairs={{0,1},{1,0},{2,3},{3,2},{4,5},{5,4},{6,7},{7,6},{8,9},{9,8},{10,11... | collective-permute-start | bytes 1376264 | tf_op jit(solution)/shard_map/ppermute | solution.py:23
  42.2 6.6 %collective-permute-start.14 = (bf16[128,768]{1,0:T(8,128)(2,1)}, bf16[128,768]{1,0:T(8,128)(2,1)}, u32[]{:S(2)}, u32[]{:S(2)}) collective-permute-start(bf16[128,768]{1,0:T(8,128)(2,1)} %collective-permute-done.4.refs_4_), channel_id=1, source_target_pairs={{0,1},{1,0},{2,3},{3,2},{4,5},{5,4},{6,7},{7,6},{8,9},{9,8},{10,11... | collective-permute-start | bytes 589832 | tf_op jit(solution)/shard_map/ppermute | solution.py:23
  42.3 6.9 %collective-permute-start.15 = (bf16[128,768]{1,0:T(8,128)(2,1)}, bf16[128,768]{1,0:T(8,128)(2,1)}, u32[]{:S(2)}, u32[]{:S(2)}) collective-permute-start(bf16[128,768]{1,0:T(8,128)(2,1)} %collective-permute-done.5.refs_5_), channel_id=1, source_target_pairs={{0,1},{1,0},{2,3},{3,2},{4,5},{5,4},{6,7},{7,6},{8,9},{9,8},{10,11... | collective-permute-start | bytes 589832 | tf_op jit(solution)/shard_map/ppermute | solution.py:23
  43.0 49.7 %all-to-all-start = ((bf16[16,64,1024]{2,1,0:T(8,128)(2,1)}), bf16[16,64,1024]{2,1,0:T(8,128)(2,1)S(1)}, u32[]{:S(2)}, u32[]{:S(2)}) async-start(bf16[16,64,1024]{2,1,0:T(8,128)(2,1)} %bitcast.25), calls=%async_computation | async-start | bytes 4194304 | tf_op jit(solution)/shard_map/all_to_all | solution.py:272
  48.6 4.1 %collective-permute-start.12 = (bf16[128,1792]{1,0:T(8,128)(2,1)}, bf16[128,1792]{1,0:T(8,128)(2,1)}, u32[]{:S(2)}, u32[]{:S(2)}) collective-permute-start(bf16[128,1792]{1,0:T(8,128)(2,1)} %collective-permute-done.2.refs_2_), channel_id=1, source_target_pairs={{0,1},{1,0},{2,3},{3,2},{4,5},{5,4},{6,7},{7,6},{8,9},{9,8},{10,11... | collective-permute-start | bytes 1376264 | tf_op jit(solution)/shard_map/ppermute | solution.py:23
  48.8 2.5 %collective-permute-start.16 = (bf16[128,768]{1,0:T(8,128)(2,1)}, bf16[128,768]{1,0:T(8,128)(2,1)S(1)}, u32[]{:S(2)}, u32[]{:S(2)}) collective-permute-start(bf16[128,768]{1,0:T(8,128)(2,1)} %copy-done.12), channel_id=1, source_target_pairs={{0,1},{1,0},{2,3},{3,2},{4,5},{5,4},{6,7},{7,6},{8,9},{9,8},{10,11... | collective-permute-start | bytes 589832 | tf_op jit(solution)/shard_map/ppermute | solution.py:23
  49.2 3.5 %collective-permute-start.13 = (bf16[128,1792]{1,0:T(8,128)(2,1)S(1)}, bf16[128,1792]{1,0:T(8,128)(2,1)}, u32[]{:S(2)}, u32[]{:S(2)}) collective-permute-start(bf16[128,1792]{1,0:T(8,128)(2,1)S(1)} %copy-done.5), channel_id=1, source_target_pairs={{0,1},{1,0},{2,3},{3,2},{4,5},{5,4},{6,7},{7,6},{8,9},{9,8},{10,11... | collective-permute-start | bytes 1376264 | tf_op jit(solution)/shard_map/ppermute | solution.py:23
  51.3 1.7 collective-permute-start.17
  51.4 2.1 %collective-permute-start.18 = (bf16[128,1024]{1,0:T(8,128)(2,1)}, bf16[128,1024]{1,0:T(8,128)(2,1)}, u32[]{:S(2)}, u32[]{:S(2)}) collective-permute-start(bf16[128,1024]{1,0:T(8,128)(2,1)} %copy-done.11), channel_id=1, source_target_pairs={{0,1},{1,0},{2,3},{3,2},{4,5},{5,4},{6,7},{7,6},{8,9},{9,8},{10,11... | collective-permute-start | bytes 786440 | tf_op jit(solution)/shard_map/ppermute | solution.py:23
  51.8 2.1 %collective-permute-start.19 = (bf16[128,1024]{1,0:T(8,128)(2,1)}, bf16[128,1024]{1,0:T(8,128)(2,1)}, u32[]{:S(2)}, u32[]{:S(2)}) collective-permute-start(bf16[128,1024]{1,0:T(8,128)(2,1)} %collective-permute-done.9.refs_9_), channel_id=1, source_target_pairs={{0,1},{1,0},{2,3},{3,2},{4,5},{5,4},{6,7},{7,6},{8,9},{9,8},{10,11... | collective-permute-start | bytes 786440 | tf_op jit(solution)/shard_map/ppermute | solution.py:23
  72.1 4.0 %collective-permute-start.23 = (f32[2,1024]{1,0:T(2,128)S(1)}, f32[2,1024]{1,0:T(2,128)S(1)}, u32[]{:S(2)}, u32[]{:S(2)}) collective-permute-start(f32[2,1024]{1,0:T(2,128)S(1)} %add.107), channel_id=1, source_target_pairs={{0,32},{16,48},{32,0},{48,16},{1,33},{17,49},{33,1},{49,17},{2,34}... | collective-permute-start | bytes 24584 | tf_op jit(solution)/shard_map/ppermute | solution.py:23
  72.1 4.0 %collective-permute-start.22 = (f32[2,1024]{1,0:T(2,128)S(1)}, f32[2,1024]{1,0:T(2,128)S(1)}, u32[]{:S(2)}, u32[]{:S(2)}) collective-permute-start(f32[2,1024]{1,0:T(2,128)S(1)} %add.107), channel_id=1, source_target_pairs={{0,48},{16,0},{32,16},{48,32},{1,49},{17,1},{33,17},{49,33},{2,50}... | collective-permute-start | bytes 24584 | tf_op jit(solution)/shard_map/ppermute | solution.py:23
  74.0 3.7 %collective-permute-start.21 = (f32[2,1024]{1,0:T(2,128)S(1)}, f32[2,1024]{1,0:T(2,128)S(1)}, u32[]{:S(2)}, u32[]{:S(2)}) collective-permute-start(f32[2,1024]{1,0:T(2,128)S(1)} %add.107), channel_id=1, source_target_pairs={{0,16},{16,32},{32,48},{48,0},{1,17},{17,33},{33,49},{49,1},{2,18}... | collective-permute-start | bytes 24584 | tf_op jit(solution)/shard_map/ppermute | solution.py:23
  77.7 4.5 %collective-permute-start.26 = (f32[2,1024]{1,0:T(2,128)S(1)}, f32[2,1024]{1,0:T(2,128)S(1)}, u32[]{:S(2)}, u32[]{:S(2)}) collective-permute-start(f32[2,1024]{1,0:T(2,128)S(1)} %add_add_fusion.2), channel_id=1, source_target_pairs={{0,8},{4,12},{8,0},{12,4},{1,9},{5,13},{9,1},{13,5},{2,10},{6,14},... | collective-permute-start | bytes 24584 | tf_op jit(solution)/shard_map/ppermute | solution.py:23
  80.7 2.8 %collective-permute-start.25 = (f32[2,1024]{1,0:T(2,128)S(1)}, f32[2,1024]{1,0:T(2,128)S(1)}, u32[]{:S(2)}, u32[]{:S(2)}) collective-permute-start(f32[2,1024]{1,0:T(2,128)S(1)} %add_add_fusion.2), channel_id=1, source_target_pairs={{0,12},{4,0},{8,4},{12,8},{1,13},{5,1},{9,5},{13,9},{2,14},{6,2},{... | collective-permute-start | bytes 24584 | tf_op jit(solution)/shard_map/ppermute | solution.py:23
  81.6 3.7 %collective-permute-start.24 = (f32[2,1024]{1,0:T(2,128)S(1)}, f32[2,1024]{1,0:T(2,128)S(1)}, u32[]{:S(2)}, u32[]{:S(2)}) collective-permute-start(f32[2,1024]{1,0:T(2,128)S(1)} %add_add_fusion.2), channel_id=1, source_target_pairs={{0,4},{4,8},{8,12},{12,0},{1,5},{5,9},{9,13},{13,1},{2,6},{6,10},{... | collective-permute-start | bytes 24584 | tf_op jit(solution)/shard_map/ppermute | solution.py:23
  85.3 4.1 %collective-permute-start.29 = (f32[2,1024]{1,0:T(2,128)S(1)}, f32[2,1024]{1,0:T(2,128)S(1)}, u32[]{:S(2)}, u32[]{:S(2)}) collective-permute-start(f32[2,1024]{1,0:T(2,128)S(1)} %add_add_fusion.1), channel_id=1, source_target_pairs={{0,64},{2,66},{64,0},{66,2},{1,65},{3,67},{65,1},{67,3},{4,68},{6,... | collective-permute-start | bytes 24584 | tf_op jit(solution)/shard_map/ppermute | solution.py:23
  87.3 2.5 %collective-permute-start.28 = (f32[2,1024]{1,0:T(2,128)S(1)}, f32[2,1024]{1,0:T(2,128)S(1)}, u32[]{:S(2)}, u32[]{:S(2)}) collective-permute-start(f32[2,1024]{1,0:T(2,128)S(1)} %add_add_fusion.1), channel_id=1, source_target_pairs={{0,66},{2,0},{64,2},{66,64},{1,67},{3,1},{65,3},{67,65},{4,70},{6,... | collective-permute-start | bytes 24584 | tf_op jit(solution)/shard_map/ppermute | solution.py:23
  89.0 3.7 %collective-permute-start.27 = (f32[2,1024]{1,0:T(2,128)S(1)}, f32[2,1024]{1,0:T(2,128)S(1)}, u32[]{:S(2)}, u32[]{:S(2)}) collective-permute-start(f32[2,1024]{1,0:T(2,128)S(1)} %add_add_fusion.1), channel_id=1, source_target_pairs={{0,2},{2,64},{64,66},{66,0},{1,3},{3,65},{65,67},{67,1},{4,6},{6,6... | collective-permute-start | bytes 24584 | tf_op jit(solution)/shard_map/ppermute | solution.py:23
  103.5 11.3 %collective-permute-start.30 = (bf16[1024,1792]{1,0:T(8,128)(2,1)S(1)}, bf16[1024,1792]{1,0:T(8,128)(2,1)S(1)}, u32[]{:S(2)}, u32[]{:S(2)}) collective-permute-start(bf16[1024,1792]{1,0:T(8,128)(2,1)S(1)} %get-tuple-element.12), channel_id=1, source_target_pairs={{0,1},{1,0},{2,3},{3,2},{4,5},{5,4},{6,7},{7,6},{8,9},{9,8},{10,11... | collective-permute-start | bytes 11010056 | tf_op jit(solution)/shard_map/ppermute | solution.py:23
  117.5 51.9 %all-to-all-start.1 = ((bf16[128,8,1792]{2,1,0:T(8,128)(2,1)}), bf16[128,8,1792]{2,1,0:T(8,128)(2,1)}, u32[]{:S(2)}, u32[]{:S(2)}) async-start(bf16[128,8,1792]{2,1,0:T(8,128)(2,1)} %fusion), calls=%async_computation.1 | async-start | bytes 7340032 | tf_op jit(solution)/shard_map/all_to_all | solution.py:295
  (15 other events, 153.0 us)

commit v7 on v6

--- a/solution.py
+++ b/solution.py
@@ -142,7 +142,6 @@
     @pl.when(i == 0)
     def _():
         load.start()
-        ahead.start()
 
     scale = (8192.0 / totals[...]).T
     cap = capped[...]
@@ -154,6 +153,7 @@
     @pl.when(i == 0)
     def _():
         load.wait()
+        ahead.start()
 
     share[...] = lax.dot_general(
         d, weight_v[...], (((1,), (1,)), ((), ())), preferred_element_type=F32

time: 173 us -> 173 us (level)
  no operation moved by 1% of the time
where the time goes in v7:
time: 173 us; the launch traced here: 172 us
  waiting for transfers between devices  58.7 us (34%)
  starting transfers between devices  49.5 us (29%)
  Pallas kernels  33.6 us (19%)
  local copies, waits for them, and re-layouts  13.5 us (8%)
  matrix products  11.2 us (6%)
  other arithmetic  4.8 us (3%)
    ppermute x31, starting transfers between devices, shift(): return lax.ppermute(v, axis, [(i, (i + step) % size) for i in range(size)])  39 us
    all_to_all x1, waiting for transfers between devices, per_device(): lax.all_to_all(chip.reshape(128, rows // 128, half), EVERY, split_axis=0,...  32.7 us
    ppermute x31, waiting for transfers between devices, shift(): return lax.ppermute(v, axis, [(i, (i + step) % size) for i in range(size)])  26 us
    pallas_call x1, Pallas kernels, scores(): pl.pallas_call(functools.partial(scores_kernel, tile), name='scores', out...  16 us
    dot_general x1, matrix products, per_device(): lax.dot_general(gathered, delta, (((0,), (0,)), ((), ())), preferred_elem...  11.2 us
    pallas_call x1, Pallas kernels, delta_and_share(): pl.pallas_call(delta_kernel, name='delta_and_share', grid_spec=pltpu.Pref...  8.52 us
    unnamed x28, local copies, waits for them, and re-layouts  6.37 us
    all_to_all x1, starting transfers between devices, per_device(): lax.all_to_all(by_owner, ('y', 'zl', 'core'), split_axis=0, concat_axis=0...  5.61 us
  transfers between devices with their start and end apart: 33, of which 17 were waited for; matrix products, arithmetic and copies ran while one was open for 11% of the time, Pallas kernels for 13%

profile of v7, /device:TPU:1, one launch (start us, length us, event | category | flops | bytes accessed | tf_op | source)
XLA Modules:
  0.0 172.3 jit_solution(7193014280600494520)
XLA Ops:
  1.8 4.5 %collective-permute-start.3 = (bf16[128,1792]{1,0:T(8,128)(2,1)S(1)}, bf16[128,1792]{1,0:T(8,128)(2,1)S(1)}, u32[]{:S(2)}, u32[]{:S(2)}) collective-permute-start(bf16[128,1792]{1,0:T(8,128)(2,1)S(1)} %constant_dynamic-slice_fusion), channel_id=1, source_target_pairs={{0,64},{64,0},{1,65},{65,1},{2,66},{66,2},{3,67},{67,3},{4,68},{68... | collective-permute-start | bytes 1376264 | tf_op jit(solution)/shard_map/ppermute | solution.py:23
  7.6 1.5 collective-permute-start.1
  9.0 1.5 collective-permute-start.2
  10.6 3.2 %copy.8 = bf16[8,16,8,1024]{3,2,0,1:T(8,128)(2,1)} copy(bf16[8,16,8,1024]{3,2,1,0:T(8,128)(2,1)} %bitcast.26) | data formatting | bytes 4194304 | tf_op jit(solution)/shard_map/reshape | solution.py:271
  15.1 1.5 collective-permute-done.3.block.refs_3_
  17.4 1.7 left_columns.1
  20.4 2.7 %collective-permute-start.7 = (bf16[128,1024]{1,0:T(8,128)(2,1)S(1)}, bf16[128,1024]{1,0:T(8,128)(2,1)S(1)}, u32[]{:S(2)}, u32[]{:S(2)}) collective-permute-start(bf16[128,1024]{1,0:T(8,128)(2,1)S(1)} %slice.16), channel_id=1, source_target_pairs={{0,64},{64,0},{1,65},{65,1},{2,66},{66,2},{3,67},{67,3},{4,68},{68... | collective-permute-start | bytes 786440 | tf_op jit(solution)/shard_map/ppermute | solution.py:23
  25.9 3.7 %collective-permute-done.2.refs_2_ = bf16[128,1792]{1,0:T(8,128)(2,1)} collective-permute-done((bf16[128,1792]{1,0:T(8,128)(2,1)S(1)}, bf16[128,1792]{1,0:T(8,128)(2,1)}, u32[]{:S(2)}, u32[]{:S(2)}) %collective-permute-start.2) | collective-permute-done | bytes 458784 | tf_op jit(solution)/shard_map/ppermute | solution.py:23
  31.1 5.0 %collective-permute-done.4.refs_4_ = bf16[128,768]{1,0:T(8,128)(2,1)} collective-permute-done((bf16[128,768]{1,0:T(8,128)(2,1)}, bf16[128,768]{1,0:T(8,128)(2,1)}, u32[]{:S(2)}, u32[]{:S(2)}) %collective-permute-start.4) | collective-permute-done | bytes 196640 | tf_op jit(solution)/shard_map/ppermute | solution.py:23
  36.1 4.3 %collective-permute-start.10 = (bf16[128,1792]{1,0:T(8,128)(2,1)S(1)}, bf16[128,1792]{1,0:T(8,128)(2,1)}, u32[]{:S(2)}, u32[]{:S(2)}) collective-permute-start(bf16[128,1792]{1,0:T(8,128)(2,1)S(1)} %collective-permute-done.refs_0_), channel_id=1, source_target_pairs={{0,1},{1,0},{2,3},{3,2},{4,5},{5,4},{6,7},{7,6},{8,9},{9,8},{10,11... | collective-permute-start | bytes 1376264 | tf_op jit(solution)/shard_map/ppermute | solution.py:23
  40.4 1.8 %collective-permute-start.11 = (bf16[128,1792]{1,0:T(8,128)(2,1)}, bf16[128,1792]{1,0:T(8,128)(2,1)}, u32[]{:S(2)}, u32[]{:S(2)}) collective-permute-start(bf16[128,1792]{1,0:T(8,128)(2,1)} %collective-permute-done.1.refs_1_), channel_id=1, source_target_pairs={{0,1},{1,0},{2,3},{3,2},{4,5},{5,4},{6,7},{7,6},{8,9},{9,8},{10,11... | collective-permute-start | bytes 1376264 | tf_op jit(solution)/shard_map/ppermute | solution.py:23
  43.0 5.6 %all-to-all-start = ((bf16[16,64,1024]{2,1,0:T(8,128)(2,1)}), bf16[16,64,1024]{2,1,0:T(8,128)(2,1)S(1)}, u32[]{:S(2)}, u32[]{:S(2)}) async-start(bf16[16,64,1024]{2,1,0:T(8,128)(2,1)} %bitcast.25), calls=%async_computation | async-start | bytes 4194304 | tf_op jit(solution)/shard_map/all_to_all | solution.py:272
  49.3 2.0 %collective-permute-done.16.refs_16_ = bf16[128,768]{1,0:T(8,128)(2,1)S(1)} collective-permute-done((bf16[128,768]{1,0:T(8,128)(2,1)}, bf16[128,768]{1,0:T(8,128)(2,1)S(1)}, u32[]{:S(2)}, u32[]{:S(2)}) %collective-permute-start.16) | collective-permute-done | bytes 196640 | tf_op jit(solution)/shard_map/ppermute | solution.py:23
  53.9 16.0 %scores.1 = (bf16[1024,3584]{1,0:T(8,128)(2,1)}, f32[1024,1024]{1,0:T(8,128)}, f32[2,1024]{1,0:T(2,128)}) custom-call(s32[9]{0:T(128)} %stack.36.place, bf16[128,3584]{1,0:T(8,128)(2,1)} %hidden.1, bf16[128,1792]{1,0:T(8,128)(2,1)} %copy-done.6, bf16[128,1792]{1,0:T(8,128)(2,1)} %collective-permute-done.1.refs_1_, ...), custom_call_target="tpu_custom_call" | custom-call | flops 7516192768 | bytes 20971520 | tf_op jit(solution)/shard_map/scores/pallas_call | solution.py:107
  72.1 1.8 %collective-permute-start.22 = (f32[2,1024]{1,0:T(2,128)S(1)}, f32[2,1024]{1,0:T(2,128)S(1)}, u32[]{:S(2)}, u32[]{:S(2)}) collective-permute-start(f32[2,1024]{1,0:T(2,128)S(1)} %add.107), channel_id=1, source_target_pairs={{0,48},{16,0},{32,16},{48,32},{1,49},{17,1},{33,17},{49,33},{2,50}... | collective-permute-start | bytes 24584 | tf_op jit(solution)/shard_map/ppermute | solution.py:23
  74.5 1.7 collective-permute-done.23
  76.2 1.6 collective-permute-done.21
  77.7 3.0 %collective-permute-start.26 = (f32[2,1024]{1,0:T(2,128)S(1)}, f32[2,1024]{1,0:T(2,128)S(1)}, u32[]{:S(2)}, u32[]{:S(2)}) collective-permute-start(f32[2,1024]{1,0:T(2,128)S(1)} %add_add_fusion.2), channel_id=1, source_target_pairs={{0,8},{4,12},{8,0},{12,4},{1,9},{5,13},{9,1},{13,5},{2,10},{6,14},... | collective-permute-start | bytes 24584 | tf_op jit(solution)/shard_map/ppermute | solution.py:23
  83.5 1.8 %collective-permute-done.24 = f32[2,1024]{1,0:T(2,128)S(1)} collective-permute-done((f32[2,1024]{1,0:T(2,128)S(1)}, f32[2,1024]{1,0:T(2,128)S(1)}, u32[]{:S(2)}, u32[]{:S(2)}) %collective-permute-start.24) | collective-permute-done | bytes 8224 | tf_op jit(solution)/shard_map/ppermute | solution.py:23
  85.3 2.0 %collective-permute-start.29 = (f32[2,1024]{1,0:T(2,128)S(1)}, f32[2,1024]{1,0:T(2,128)S(1)}, u32[]{:S(2)}, u32[]{:S(2)}) collective-permute-start(f32[2,1024]{1,0:T(2,128)S(1)} %add_add_fusion.1), channel_id=1, source_target_pairs={{0,64},{2,66},{64,0},{66,2},{1,65},{3,67},{65,1},{67,3},{4,68},{6,... | collective-permute-start | bytes 24584 | tf_op jit(solution)/shard_map/ppermute | solution.py:23
  87.3 1.6 collective-permute-start.28
  89.8 2.8 %collective-permute-done.27 = f32[2,1024]{1,0:T(2,128)S(1)} collective-permute-done((f32[2,1024]{1,0:T(2,128)S(1)}, f32[2,1024]{1,0:T(2,128)S(1)}, u32[]{:S(2)}, u32[]{:S(2)}) %collective-permute-start.27) | collective-permute-done | bytes 8224 | tf_op jit(solution)/shard_map/ppermute | solution.py:23
  92.7 2.2 %copy-done = f32[1024,1024]{1,0:T(8,128)S(1)} copy-done((f32[1024,1024]{1,0:T(8,128)S(1)}, f32[1024,1024]{1,0:T(8,128)}, u32[]{:S(2)}) %copy-start) | copy-done | bytes 4194328
  94.9 8.5 %delta_and_share.1 = (bf16[1024,1024]{1,0:T(8,128)(2,1)S(1)}, bf16[1024,1792]{1,0:T(8,128)(2,1)S(1)}, bf16[1792,1024]{1,0:T(8,128)(2,1)S(1)}) custom-call(s32[1]{0:T(128)} %bitcast.core, f32[1024,1024]{1,0:T(8,128)S(1)} %copy-done, bf16[1024,1024]{1,0:T(8,128)(2,1)S(1)} %bitcast.23, f32[8,1024]{1,0:T(8,128)S(1)} %concatenate.3.totals, bf16[3584,1024]{1,0:T(8,128)(2,1)} %weight.1), custom_call_target="tpu_custom_call" | custom-call | flops 3758096384 | bytes 16777216 | tf_op jit(solution)/shard_map/delta_and_share/pallas_call | solution.py:170
  103.5 5.3 %collective-permute-start.30 = (bf16[1024,1792]{1,0:T(8,128)(2,1)S(1)}, bf16[1024,1792]{1,0:T(8,128)(2,1)S(1)}, u32[]{:S(2)}, u32[]{:S(2)}) collective-permute-start(bf16[1024,1792]{1,0:T(8,128)(2,1)S(1)} %get-tuple-element.12), channel_id=1, source_target_pairs={{0,1},{1,0},{2,3},{3,2},{4,5},{5,4},{6,7},{7,6},{8,9},{9,8},{10,11... | collective-permute-start | bytes 11010056 | tf_op jit(solution)/shard_map/ppermute | solution.py:23
  108.7 4.6 %own_share.1 = bf16[1024,1792]{1,0:T(8,128)(2,1)S(1)} custom-call(bf16[1024,1024]{1,0:T(8,128)(2,1)S(1)} %get-tuple-element.10.delta, bf16[1792,1024]{1,0:T(8,128)(2,1)S(1)} %get-tuple-element.11.weight), custom_call_target="tpu_custom_call" | custom-call | flops 3758096384 | bytes 10485760 | tf_op jit(solution)/shard_map/own_share/pallas_call | solution.py:209
  114.8 2.8 %fusion = bf16[128,8,1792]{2,1,0:T(8,128)(2,1)} fusion(bf16[1024,1792]{1,0:T(8,128)(2,1)S(1)} %collective-permute-done.30, bf16[1024,1792]{1,0:T(8,128)(2,1)S(1)} %own_share.1), kind=kLoop, calls=%fused_computation.3 | loop fusion | flops 7340032 | bytes 11010048 | tf_op jit(solution)/shard_map/reshape | solution.py:296
  117.5 5.0 %all-to-all-start.1 = ((bf16[128,8,1792]{2,1,0:T(8,128)(2,1)}), bf16[128,8,1792]{2,1,0:T(8,128)(2,1)}, u32[]{:S(2)}, u32[]{:S(2)}) async-start(bf16[128,8,1792]{2,1,0:T(8,128)(2,1)} %fusion), calls=%async_computation.1 | async-start | bytes 7340032 | tf_op jit(solution)/shard_map/all_to_all | solution.py:295
  122.5 11.2 %convolution_convert_fusion = bf16[3584,1024]{1,0:T(8,128)(2,1)S(1)} fusion(bf16[1024,3584]{1,0:T(8,128)(2,1)} %get-tuple-element.13, bf16[1024,1024]{1,0:T(8,128)(2,1)S(1)} %copy-done.2), kind=kOutput, calls=%fused_computation | convolution fusion | flops 7519862784 | bytes 16777216 | tf_op jit(solution)/shard_map/dot_general | solution.py:298
  133.7 3.0 %copy-done.9 = bf16[3584,1024]{1,0:T(8,128)(2,1)} copy-done((bf16[3584,1024]{1,0:T(8,128)(2,1)}, bf16[3584,1024]{1,0:T(8,128)(2,1)S(1)}, u32[]{:S(2)}) %copy-start.9) | copy-done | bytes 7340056
  136.7 32.7 %all-to-all-done.1 = bf16[128,8,1792]{2,1,0:T(8,128)(2,1)} async-done(((bf16[128,8,1792]{2,1,0:T(8,128)(2,1)}), bf16[128,8,1792]{2,1,0:T(8,128)(2,1)}, u32[]{:S(2)}, u32[]{:S(2)}) %all-to-all-start.1) | async-done | bytes 3670048 | tf_op jit(solution)/shard_map/all_to_all | solution.py:295
  169.4 2.7 %chip_sum.1 = bf16[8,3584]{1,0:T(8,128)(2,1)} custom-call(bf16[64,16,1792]{2,1,0:T(8,128)(2,1)} %bitcast.13.parts, bf16[8,128]{1,0:T(8,128)(2,1)S(1)} %slice.19.after), custom_call_target="tpu_custom_call" | custom-call | flops 1835008 | bytes 4194304 | tf_op jit(solution)/shard_map/chip_sum/pallas_call | solution.py:242
  (84 shorter events, 22.0 us)
Async XLA Ops:
  1.8 14.8 %collective-permute-start.3 = (bf16[128,1792]{1,0:T(8,128)(2,1)S(1)}, bf16[128,1792]{1,0:T(8,128)(2,1)S(1)}, u32[]{:S(2)}, u32[]{:S(2)}) collective-permute-start(bf16[128,1792]{1,0:T(8,128)(2,1)S(1)} %constant_dynamic-slice_fusion), channel_id=1, source_target_pairs={{0,64},{64,0},{1,65},{65,1},{2,66},{66,2},{3,67},{67,3},{4,68},{68... | collective-permute-start | bytes 1376264 | tf_op jit(solution)/shard_map/ppermute | solution.py:23
  6.4 14.0 %collective-permute-start = (bf16[128,1792]{1,0:T(8,128)(2,1)S(1)}, bf16[128,1792]{1,0:T(8,128)(2,1)S(1)}, u32[]{:S(2)}, u32[]{:S(2)}) collective-permute-start(bf16[128,1792]{1,0:T(8,128)(2,1)S(1)} %constant_dynamic-slice_fusion), channel_id=1, source_target_pairs={{0,16},{16,32},{32,48},{48,0},{1,17},{17,33},{33,49},{49,1},{2,18}... | collective-permute-start | bytes 1376264 | tf_op jit(solution)/shard_map/ppermute | solution.py:23
  7.6 15.5 %collective-permute-start.1 = (bf16[128,1792]{1,0:T(8,128)(2,1)S(1)}, bf16[128,1792]{1,0:T(8,128)(2,1)}, u32[]{:S(2)}, u32[]{:S(2)}) collective-permute-start(bf16[128,1792]{1,0:T(8,128)(2,1)S(1)} %constant_dynamic-slice_fusion), channel_id=1, source_target_pairs={{0,48},{16,0},{32,16},{48,32},{1,49},{17,1},{33,17},{49,33},{2,50}... | collective-permute-start | bytes 1376264 | tf_op jit(solution)/shard_map/ppermute | solution.py:23
  9.0 20.6 %collective-permute-start.2 = (bf16[128,1792]{1,0:T(8,128)(2,1)S(1)}, bf16[128,1792]{1,0:T(8,128)(2,1)}, u32[]{:S(2)}, u32[]{:S(2)}) collective-permute-start(bf16[128,1792]{1,0:T(8,128)(2,1)S(1)} %constant_dynamic-slice_fusion), channel_id=1, source_target_pairs={{0,32},{16,48},{32,0},{48,16},{1,33},{17,49},{33,1},{49,17},{2,34}... | collective-permute-start | bytes 1376264 | tf_op jit(solution)/shard_map/ppermute | solution.py:23
  19.1 17.0 %collective-permute-start.4 = (bf16[128,768]{1,0:T(8,128)(2,1)}, bf16[128,768]{1,0:T(8,128)(2,1)}, u32[]{:S(2)}, u32[]{:S(2)}) collective-permute-start(bf16[128,768]{1,0:T(8,128)(2,1)} %left_columns.1), channel_id=1, source_target_pairs={{0,16},{16,32},{32,48},{48,0},{1,17},{17,33},{33,49},{49,1},{2,18}... | collective-permute-start | bytes 589832 | tf_op jit(solution)/shard_map/ppermute | solution.py:23
  20.4 21.8 %collective-permute-start.7 = (bf16[128,1024]{1,0:T(8,128)(2,1)S(1)}, bf16[128,1024]{1,0:T(8,128)(2,1)S(1)}, u32[]{:S(2)}, u32[]{:S(2)}) collective-permute-start(bf16[128,1024]{1,0:T(8,128)(2,1)S(1)} %slice.16), channel_id=1, source_target_pairs={{0,64},{64,0},{1,65},{65,1},{2,66},{66,2},{3,67},{67,3},{4,68},{68... | collective-permute-start | bytes 786440 | tf_op jit(solution)/shard_map/ppermute | solution.py:23
  24.1 18.2 %collective-permute-start.8 = (bf16[128,1024]{1,0:T(8,128)(2,1)S(1)}, bf16[128,1024]{1,0:T(8,128)(2,1)S(1)}, u32[]{:S(2)}, u32[]{:S(2)}) collective-permute-start(bf16[128,1024]{1,0:T(8,128)(2,1)S(1)} %slice.17), channel_id=1, source_target_pairs={{0,64},{64,0},{1,65},{65,1},{2,66},{66,2},{3,67},{67,3},{4,68},{68... | collective-permute-start | bytes 786440 | tf_op jit(solution)/shard_map/ppermute | solution.py:23
  24.5 11.6 %collective-permute-start.5 = (bf16[128,768]{1,0:T(8,128)(2,1)}, bf16[128,768]{1,0:T(8,128)(2,1)}, u32[]{:S(2)}, u32[]{:S(2)}) collective-permute-start(bf16[128,768]{1,0:T(8,128)(2,1)} %left_columns.1), channel_id=1, source_target_pairs={{0,48},{16,0},{32,16},{48,32},{1,49},{17,1},{33,17},{49,33},{2,50}... | collective-permute-start | bytes 589832 | tf_op jit(solution)/shard_map/ppermute | solution.py:23
  29.6 10.8 %collective-permute-start.6 = (bf16[128,768]{1,0:T(8,128)(2,1)}, bf16[128,768]{1,0:T(8,128)(2,1)S(1)}, u32[]{:S(2)}, u32[]{:S(2)}) collective-permute-start(bf16[128,768]{1,0:T(8,128)(2,1)} %left_columns.1), channel_id=1, source_target_pairs={{0,32},{16,48},{32,0},{48,16},{1,33},{17,49},{33,1},{49,17},{2,34}... | collective-permute-start | bytes 589832 | tf_op jit(solution)/shard_map/ppermute | solution.py:23
  36.1 12.5 %collective-permute-start.9 = (bf16[128,1024]{1,0:T(8,128)(2,1)S(1)}, bf16[128,1024]{1,0:T(8,128)(2,1)}, u32[]{:S(2)}, u32[]{:S(2)}) collective-permute-start(bf16[128,1024]{1,0:T(8,128)(2,1)S(1)} %slice.18), channel_id=1, source_target_pairs={{0,64},{64,0},{1,65},{65,1},{2,66},{66,2},{3,67},{67,3},{4,68},{68... | collective-permute-start | bytes 786440 | tf_op jit(solution)/shard_map/ppermute | solution.py:23
  36.1 15.3 %collective-permute-start.10 = (bf16[128,1792]{1,0:T(8,128)(2,1)S(1)}, bf16[128,1792]{1,0:T(8,128)(2,1)}, u32[]{:S(2)}, u32[]{:S(2)}) collective-permute-start(bf16[128,1792]{1,0:T(8,128)(2,1)S(1)} %collective-permute-done.refs_0_), channel_id=1, source_target_pairs={{0,1},{1,0},{2,3},{3,2},{4,5},{5,4},{6,7},{7,6},{8,9},{9,8},{10,11... | collective-permute-start | bytes 1376264 | tf_op jit(solution)/shard_map/ppermute | solution.py:23
  40.4 11.4 %collective-permute-start.11 = (bf16[128,1792]{1,0:T(8,128)(2,1)}, bf16[128,1792]{1,0:T(8,128)(2,1)}, u32[]{:S(2)}, u32[]{:S(2)}) collective-permute-start(bf16[128,1792]{1,0:T(8,128)(2,1)} %collective-permute-done.1.refs_1_), channel_id=1, source_target_pairs={{0,1},{1,0},{2,3},{3,2},{4,5},{5,4},{6,7},{7,6},{8,9},{9,8},{10,11... | collective-permute-start | bytes 1376264 | tf_op jit(solution)/shard_map/ppermute | solution.py:23
  42.2 6.6 %collective-permute-start.14 = (bf16[128,768]{1,0:T(8,128)(2,1)}, bf16[128,768]{1,0:T(8,128)(2,1)}, u32[]{:S(2)}, u32[]{:S(2)}) collective-permute-start(bf16[128,768]{1,0:T(8,128)(2,1)} %collective-permute-done.4.refs_4_), channel_id=1, source_target_pairs={{0,1},{1,0},{2,3},{3,2},{4,5},{5,4},{6,7},{7,6},{8,9},{9,8},{10,11... | collective-permute-start | bytes 589832 | tf_op jit(solution)/shard_map/ppermute | solution.py:23
  42.3 6.9 %collective-permute-start.15 = (bf16[128,768]{1,0:T(8,128)(2,1)}, bf16[128,768]{1,0:T(8,128)(2,1)}, u32[]{:S(2)}, u32[]{:S(2)}) collective-permute-start(bf16[128,768]{1,0:T(8,128)(2,1)} %collective-permute-done.5.refs_5_), channel_id=1, source_target_pairs={{0,1},{1,0},{2,3},{3,2},{4,5},{5,4},{6,7},{7,6},{8,9},{9,8},{10,11... | collective-permute-start | bytes 589832 | tf_op jit(solution)/shard_map/ppermute | solution.py:23
  43.0 49.7 %all-to-all-start = ((bf16[16,64,1024]{2,1,0:T(8,128)(2,1)}), bf16[16,64,1024]{2,1,0:T(8,128)(2,1)S(1)}, u32[]{:S(2)}, u32[]{:S(2)}) async-start(bf16[16,64,1024]{2,1,0:T(8,128)(2,1)} %bitcast.25), calls=%async_computation | async-start | bytes 4194304 | tf_op jit(solution)/shard_map/all_to_all | solution.py:272
  48.6 4.1 %collective-permute-start.12 = (bf16[128,1792]{1,0:T(8,128)(2,1)}, bf16[128,1792]{1,0:T(8,128)(2,1)}, u32[]{:S(2)}, u32[]{:S(2)}) collective-permute-start(bf16[128,1792]{1,0:T(8,128)(2,1)} %collective-permute-done.2.refs_2_), channel_id=1, source_target_pairs={{0,1},{1,0},{2,3},{3,2},{4,5},{5,4},{6,7},{7,6},{8,9},{9,8},{10,11... | collective-permute-start | bytes 1376264 | tf_op jit(solution)/shard_map/ppermute | solution.py:23
  48.8 2.5 %collective-permute-start.16 = (bf16[128,768]{1,0:T(8,128)(2,1)}, bf16[128,768]{1,0:T(8,128)(2,1)S(1)}, u32[]{:S(2)}, u32[]{:S(2)}) collective-permute-start(bf16[128,768]{1,0:T(8,128)(2,1)} %copy-done.12), channel_id=1, source_target_pairs={{0,1},{1,0},{2,3},{3,2},{4,5},{5,4},{6,7},{7,6},{8,9},{9,8},{10,11... | collective-permute-start | bytes 589832 | tf_op jit(solution)/shard_map/ppermute | solution.py:23
  49.2 3.5 %collective-permute-start.13 = (bf16[128,1792]{1,0:T(8,128)(2,1)S(1)}, bf16[128,1792]{1,0:T(8,128)(2,1)}, u32[]{:S(2)}, u32[]{:S(2)}) collective-permute-start(bf16[128,1792]{1,0:T(8,128)(2,1)S(1)} %copy-done.5), channel_id=1, source_target_pairs={{0,1},{1,0},{2,3},{3,2},{4,5},{5,4},{6,7},{7,6},{8,9},{9,8},{10,11... | collective-permute-start | bytes 1376264 | tf_op jit(solution)/shard_map/ppermute | solution.py:23
  51.3 1.7 collective-permute-start.17
  51.4 2.1 %collective-permute-start.18 = (bf16[128,1024]{1,0:T(8,128)(2,1)}, bf16[128,1024]{1,0:T(8,128)(2,1)}, u32[]{:S(2)}, u32[]{:S(2)}) collective-permute-start(bf16[128,1024]{1,0:T(8,128)(2,1)} %copy-done.11), channel_id=1, source_target_pairs={{0,1},{1,0},{2,3},{3,2},{4,5},{5,4},{6,7},{7,6},{8,9},{9,8},{10,11... | collective-permute-start | bytes 786440 | tf_op jit(solution)/shard_map/ppermute | solution.py:23
  51.8 2.1 %collective-permute-start.19 = (bf16[128,1024]{1,0:T(8,128)(2,1)}, bf16[128,1024]{1,0:T(8,128)(2,1)}, u32[]{:S(2)}, u32[]{:S(2)}) collective-permute-start(bf16[128,1024]{1,0:T(8,128)(2,1)} %collective-permute-done.9.refs_9_), channel_id=1, source_target_pairs={{0,1},{1,0},{2,3},{3,2},{4,5},{5,4},{6,7},{7,6},{8,9},{9,8},{10,11... | collective-permute-start | bytes 786440 | tf_op jit(solution)/shard_map/ppermute | solution.py:23
  72.1 4.0 %collective-permute-start.23 = (f32[2,1024]{1,0:T(2,128)S(1)}, f32[2,1024]{1,0:T(2,128)S(1)}, u32[]{:S(2)}, u32[]{:S(2)}) collective-permute-start(f32[2,1024]{1,0:T(2,128)S(1)} %add.107), channel_id=1, source_target_pairs={{0,32},{16,48},{32,0},{48,16},{1,33},{17,49},{33,1},{49,17},{2,34}... | collective-permute-start | bytes 24584 | tf_op jit(solution)/shard_map/ppermute | solution.py:23
  72.1 4.0 %collective-permute-start.22 = (f32[2,1024]{1,0:T(2,128)S(1)}, f32[2,1024]{1,0:T(2,128)S(1)}, u32[]{:S(2)}, u32[]{:S(2)}) collective-permute-start(f32[2,1024]{1,0:T(2,128)S(1)} %add.107), channel_id=1, source_target_pairs={{0,48},{16,0},{32,16},{48,32},{1,49},{17,1},{33,17},{49,33},{2,50}... | collective-permute-start | bytes 24584 | tf_op jit(solution)/shard_map/ppermute | solution.py:23
  74.0 3.7 %collective-permute-start.21 = (f32[2,1024]{1,0:T(2,128)S(1)}, f32[2,1024]{1,0:T(2,128)S(1)}, u32[]{:S(2)}, u32[]{:S(2)}) collective-permute-start(f32[2,1024]{1,0:T(2,128)S(1)} %add.107), channel_id=1, source_target_pairs={{0,16},{16,32},{32,48},{48,0},{1,17},{17,33},{33,49},{49,1},{2,18}... | collective-permute-start | bytes 24584 | tf_op jit(solution)/shard_map/ppermute | solution.py:23
  77.7 4.5 %collective-permute-start.26 = (f32[2,1024]{1,0:T(2,128)S(1)}, f32[2,1024]{1,0:T(2,128)S(1)}, u32[]{:S(2)}, u32[]{:S(2)}) collective-permute-start(f32[2,1024]{1,0:T(2,128)S(1)} %add_add_fusion.2), channel_id=1, source_target_pairs={{0,8},{4,12},{8,0},{12,4},{1,9},{5,13},{9,1},{13,5},{2,10},{6,14},... | collective-permute-start | bytes 24584 | tf_op jit(solution)/shard_map/ppermute | solution.py:23
  80.7 2.8 %collective-permute-start.25 = (f32[2,1024]{1,0:T(2,128)S(1)}, f32[2,1024]{1,0:T(2,128)S(1)}, u32[]{:S(2)}, u32[]{:S(2)}) collective-permute-start(f32[2,1024]{1,0:T(2,128)S(1)} %add_add_fusion.2), channel_id=1, source_target_pairs={{0,12},{4,0},{8,4},{12,8},{1,13},{5,1},{9,5},{13,9},{2,14},{6,2},{... | collective-permute-start | bytes 24584 | tf_op jit(solution)/shard_map/ppermute | solution.py:23
  81.6 3.7 %collective-permute-start.24 = (f32[2,1024]{1,0:T(2,128)S(1)}, f32[2,1024]{1,0:T(2,128)S(1)}, u32[]{:S(2)}, u32[]{:S(2)}) collective-permute-start(f32[2,1024]{1,0:T(2,128)S(1)} %add_add_fusion.2), channel_id=1, source_target_pairs={{0,4},{4,8},{8,12},{12,0},{1,5},{5,9},{9,13},{13,1},{2,6},{6,10},{... | collective-permute-start | bytes 24584 | tf_op jit(solution)/shard_map/ppermute | solution.py:23
  85.3 4.1 %collective-permute-start.29 = (f32[2,1024]{1,0:T(2,128)S(1)}, f32[2,1024]{1,0:T(2,128)S(1)}, u32[]{:S(2)}, u32[]{:S(2)}) collective-permute-start(f32[2,1024]{1,0:T(2,128)S(1)} %add_add_fusion.1), channel_id=1, source_target_pairs={{0,64},{2,66},{64,0},{66,2},{1,65},{3,67},{65,1},{67,3},{4,68},{6,... | collective-permute-start | bytes 24584 | tf_op jit(solution)/shard_map/ppermute | solution.py:23
  87.3 2.5 %collective-permute-start.28 = (f32[2,1024]{1,0:T(2,128)S(1)}, f32[2,1024]{1,0:T(2,128)S(1)}, u32[]{:S(2)}, u32[]{:S(2)}) collective-permute-start(f32[2,1024]{1,0:T(2,128)S(1)} %add_add_fusion.1), channel_id=1, source_target_pairs={{0,66},{2,0},{64,2},{66,64},{1,67},{3,1},{65,3},{67,65},{4,70},{6,... | collective-permute-start | bytes 24584 | tf_op jit(solution)/shard_map/ppermute | solution.py:23
  89.0 3.7 %collective-permute-start.27 = (f32[2,1024]{1,0:T(2,128)S(1)}, f32[2,1024]{1,0:T(2,128)S(1)}, u32[]{:S(2)}, u32[]{:S(2)}) collective-permute-start(f32[2,1024]{1,0:T(2,128)S(1)} %add_add_fusion.1), channel_id=1, source_target_pairs={{0,2},{2,64},{64,66},{66,0},{1,3},{3,65},{65,67},{67,1},{4,6},{6,6... | collective-permute-start | bytes 24584 | tf_op jit(solution)/shard_map/ppermute | solution.py:23
  103.5 11.3 %collective-permute-start.30 = (bf16[1024,1792]{1,0:T(8,128)(2,1)S(1)}, bf16[1024,1792]{1,0:T(8,128)(2,1)S(1)}, u32[]{:S(2)}, u32[]{:S(2)}) collective-permute-start(bf16[1024,1792]{1,0:T(8,128)(2,1)S(1)} %get-tuple-element.12), channel_id=1, source_target_pairs={{0,1},{1,0},{2,3},{3,2},{4,5},{5,4},{6,7},{7,6},{8,9},{9,8},{10,11... | collective-permute-start | bytes 11010056 | tf_op jit(solution)/shard_map/ppermute | solution.py:23
  117.5 51.9 %all-to-all-start.1 = ((bf16[128,8,1792]{2,1,0:T(8,128)(2,1)}), bf16[128,8,1792]{2,1,0:T(8,128)(2,1)}, u32[]{:S(2)}, u32[]{:S(2)}) async-start(bf16[128,8,1792]{2,1,0:T(8,128)(2,1)} %fusion), calls=%async_computation.1 | async-start | bytes 7340032 | tf_op jit(solution)/shard_map/all_to_all | solution.py:295
  (15 other events, 153.0 us)
